TPU v7x, 32 devices: a whole 2x2x4 slice. The times are simulated.
32 devices in a mesh: groups: 2 (over y), seq: 4 (over z), mp: 2 (over x), batch: 2 (over core).
Axes of the slice: x: 2, y: 2, z: 4, core: 2. Of those that a mesh axis runs over, the one named last changes fastest.
Arguments:
- image_token_states: bfloat16 [8, 576, 2432], P(('groups', 'batch'), 'seq'), parts along dimension 0, may hold values from -6 to 6
- timestep: int32 [8], P(('groups', 'batch')), parts along dimension 0, may hold values from 0 to 9
- prompt_token_length: int32 [8], P(('groups', 'batch')), parts along dimension 0, may hold values from 1 to 84, as said below
- modulation: float32 [10, 3, 2432], replicated, may hold values from -3 to 11
- text_key_value: bfloat16 [8, 2, 84, 1536], P(('groups', 'batch'), None, 'seq', 'mp'), parts along dimension 0, may hold values from -9 to 9
- frozen_query_key_value: bfloat16 [2432, 3, 1536], P(None, None, ('mp', 'batch')), may hold values from -0.125 to 0.125
- frozen_output_weight: bfloat16 [1536, 2432], P(('mp', 'batch')), may hold values from -0.15625 to 0.15625
- adapter_down_factors: bfloat16 [4, 32, 2432], P('seq'), may hold values from -0.125 to 0.125
- adapter_up_factors: bfloat16 [4, 32, 3, 1536], P('seq', None, None, 'mp'), may hold values from -1 to 1
- owner: int32 [3], replicated, may hold values from 0 to 3, as said below
Outputs:
- hidden_out: bfloat16 [8, 576, 2432], P(('groups', 'batch'), 'seq'), parts along dimension 0
There are 2 independent parts, one for each index of `groups`. A program takes and returns all parts, laid end to end along the dimension named above; an argument that names none is the same for every part. Nothing has to cross between parts.
Inputs may be any that keep to these rules, and one draw needn't show every extreme that they name: `prompt_token_length`: in every draw some sample's prompt fills all 84 text slots. `owner`: the three entries are distinct.
All inputs are finite; a program needn't handle non-finite values.
Results may differ from a plain program's by a relative error of at most 0.012.
The roundings to bfloat16 on the way count: a program that leaves them out, or rounds other values in their place, can miss the bound.
Values may be sent and summed in bfloat16 or wider, within the bound.
A program may use at most 128 MiB of HBM per device.

v0:
```python
import jax
import jax.numpy as jnp
from jax import lax
from jax.sharding import PartitionSpec as P

HEAD_SIZE = 64


def broadcast(block, axis, source):
    block = jnp.where(lax.axis_index(axis) == source, block, jnp.zeros_like(block))
    return lax.psum(block, axis)


def body(
    image_token_states,
    timestep,
    prompt_token_length,
    modulation,
    text_key_value,
    frozen_query_key_value,
    frozen_output_weight,
    adapter_down_factors,
    adapter_up_factors,
    owner,
):
    samples, img_rows, width = image_token_states.shape
    txt_rows = text_key_value.shape[2]
    resident_columns = adapter_up_factors.shape[3]
    heads_here = resident_columns // HEAD_SIZE
    steps_all = modulation.shape[0]
    onehot = (timestep[:, None] == jnp.arange(steps_all, dtype=jnp.int32)[None, :]).astype(
        jnp.float32
    )
    mods = jnp.einsum("st,tcd->scd", onehot, modulation, precision=lax.Precision.HIGHEST)
    shift = mods[:, 0][:, None, :]
    scale = mods[:, 1][:, None, :]
    gate = mods[:, 2][:, None, :]
    wide = image_token_states.astype(jnp.float32)
    mean = jnp.mean(wide, axis=-1, keepdims=True)
    centred = wide - mean
    var = jnp.mean(centred * centred, axis=-1, keepdims=True)
    normed = (centred * lax.rsqrt(var + 1e-06) * (1.0 + scale) + shift).astype(jnp.bfloat16)
    down_list = []
    up_list = []
    for which in range(3):
        packed_tensor = jnp.concatenate(
            [adapter_down_factors[0], adapter_up_factors[0][:, which]], axis=1
        )
        packed_tensor = broadcast(packed_tensor, "seq", owner[which])
        down_list.append(packed_tensor[:, :width])
        up_list.append(packed_tensor[:, width:])
    down_factor = jnp.stack(down_list, axis=0)
    up_factor = jnp.stack(up_list, axis=1)
    delta = jnp.einsum("crd,rcn->dcn", down_factor, up_factor, preferred_element_type=jnp.float32)
    merged = (
        lax.all_gather(frozen_query_key_value, "batch", axis=2, tiled=True).astype(jnp.float32)
        + delta
    ).astype(jnp.bfloat16)
    qkv = jnp.einsum("sid,dcn->sicn", normed, merged, preferred_element_type=jnp.float32).astype(
        jnp.bfloat16
    )
    queries = qkv[:, :, 0]
    keys = jnp.concatenate([qkv[:, :, 1], text_key_value[:, 0]], axis=1)
    values = jnp.concatenate([qkv[:, :, 2], text_key_value[:, 1]], axis=1)
    query_heads = queries.reshape(samples, img_rows, heads_here, HEAD_SIZE)
    block = img_rows + txt_rows
    start_top = jnp.full((samples, heads_here, img_rows), -1e30, jnp.float32)
    top = start_top
    key_piece = lax.all_gather(keys, "seq", axis=1, tiled=True)
    value_piece = lax.all_gather(values, "seq", axis=1, tiled=True)
    count = key_piece.shape[1]
    position = jnp.arange(count, dtype=jnp.int32)
    shard = position // block
    inside = position % block
    text_index = shard * txt_rows + inside - img_rows
    live = (inside < img_rows)[None, :] | (text_index[None, :] < prompt_token_length[:, None])
    key_heads = key_piece.reshape(samples, count, heads_here, HEAD_SIZE)
    value_heads = value_piece.reshape(samples, count, heads_here, HEAD_SIZE)
    attention_scores = jnp.einsum(
        "sihe,snhe->shin", query_heads, key_heads, preferred_element_type=jnp.float32
    ) * HEAD_SIZE ** (-0.5)
    attention_scores = jnp.where(live[:, None, None, :], attention_scores, -1e30)
    new_top = jnp.maximum(top, jnp.max(attention_scores, axis=-1))
    expo = jnp.exp(attention_scores - new_top[..., None])
    total = jnp.sum(expo, axis=-1)
    attention_weights = expo.astype(jnp.bfloat16)
    reduced_sum = jnp.einsum(
        "shin,snhe->sihe", attention_weights, value_heads, preferred_element_type=jnp.float32
    )
    top, total, reduced_sum = (new_top, total, reduced_sum)
    attn = (
        (reduced_sum / total.transpose(0, 2, 1)[..., None])
        .reshape(samples, img_rows, resident_columns)
        .astype(jnp.bfloat16)
    )
    proj = jnp.einsum(
        "sin,nd->sid",
        attn,
        lax.all_gather(frozen_output_weight, "batch", axis=0, tiled=True),
        preferred_element_type=jnp.float32,
    )
    summed_heads = lax.psum(proj.astype(jnp.bfloat16), "mp").astype(jnp.float32)
    return (wide + gate * summed_heads).astype(jnp.bfloat16)


def solution(mesh):
    placed = (
        P(("groups", "batch"), "seq", None),
        P(("groups", "batch")),
        P(("groups", "batch")),
        P(),
        P(("groups", "batch"), None, "seq", "mp"),
        P(None, None, ("mp", "batch")),
        P(("mp", "batch"), None),
        P("seq", None, None),
        P("seq", None, None, "mp"),
        P(),
    )
    return jax.shard_map(
        body,
        mesh=mesh,
        in_specs=placed,
        out_specs=P(("groups", "batch"), "seq", None),
        check_vma=False,
    )
```

profile of v0, /device:TPU:0, one launch (start us, length us, event | category | flops | bytes accessed | tf_op | source)
XLA Modules:
  0.0 242.0 jit_solution(6120827369843836584)
XLA Ops:
  7.4 0.9 slice_bitcast_fusion.10
  8.3 1.4 fusion.79
  11.7 1.8 fusion.47
  13.6 8.7 %copy.26 = bf16[2432,3,384]{0,2,1:T(8,128)(2,1)} copy(bf16[2432,3,384]{2,0,1:T(8,128)(2,1)} %param.15) | data formatting | bytes 11206656 | tf_op args[5]
  22.4 1.2 copy-done.1
  25.0 31.5 %all-reduce.6.cloned.1.call-done = (bf16[32,3200]{1,0:T(8,128)(2,1)}, bf16[32,3200]{1,0:T(8,128)(2,1)}, bf16[32,3200]{1,0:T(8,128)(2,1)}) async-done(((bf16[32,3200]{1,0:T(8,128)(2,1)}, bf16[32,3200]{1,0:T(8,128)(2,1)}, bf16[32,3200]{1,0:T(8,128)(2,1)}), (bf16[32,3200]{1,0:T(8,128)(2,1)}, bf16[32,3200]{1,0:T(8,128)(2,1)}, bf16[32,3200]{1,0:T(8,128)(2,1)})) %all-reduce.6.cloned.1.call-update) | async-done | bytes 614416 | tf_op jit(solution)/shard_map/psum | solution.py:11
  56.5 0.8 slice_bitcast_fusion.9
  57.3 0.8 slice_bitcast_fusion.5
  58.1 0.9 slice_bitcast_fusion.4
  59.1 1.0 slice_bitcast_fusion.2
  60.1 11.9 %fusion.23 = bf16[2,144,3,768]{3,1,2,0:T(8,128)(2,1)} fusion(bf16[2432,3,768]{0,2,1:T(8,128)(2,1)} %all-gather.5.cloned.1.call-done, bf16[2,144,2432]{2,1,0:T(8,128)(2,1)S(1)} %copy-done.1, f32[2,2432]{1,0:T(2,128)S(1)} %get-tuple-element.20, f32[2,2432]{1,0:T(2,128)S(1)} %get-tuple-element.21, f32[2,144]{1,0:T(2,128)S(1)} %add_rsqrt_fusion, ...), kind=kOutput, calls=%fused_computation.27 | convolution fusion | flops 3608420352 | bytes 14590208 | tf_op jit(solution)/shard_map/sid,dcn->sicn/dot_general | solution.py:59
  72.0 1.4 slice_bitcast_fusion
  73.4 1.2 copy.29
  74.7 1.2 copy.33
  77.1 41.7 %all-gather.7.cloned.1.call-done = bf16[2,660,768]{2,0,1:T(2,128)(2,1)} async-done(((bf16[2,165,768]{2,0,1:T(2,128)(2,1)}), bf16[2,660,768]{2,0,1:T(2,128)(2,1)}) %all-gather.7.cloned.1.call-update) | async-done | bytes 2027536 | tf_op jit(solution)/shard_map/all_gather | solution.py:70
  118.8 6.7 %copy.30 = bf16[2,660,768]{1,2,0:T(8,128)(2,1)} copy(bf16[2,660,768]{2,0,1:T(2,128)(2,1)} %all-gather.7.cloned.1.call-done) | data formatting | bytes 4055040 | tf_op jit(solution)/shard_map/all_gather | solution.py:70
  125.6 38.3 %all-gather.9.cloned.1.call-done = bf16[2,660,768]{2,0,1:T(2,128)(2,1)} async-done(((bf16[2,165,768]{2,0,1:T(2,128)(2,1)}), bf16[2,660,768]{2,0,1:T(2,128)(2,1)}) %all-gather.9.cloned.1.call-update) | async-done | bytes 2027536 | tf_op jit(solution)/shard_map/all_gather | solution.py:69
  163.9 6.7 %copy.34 = bf16[2,660,768]{1,2,0:T(8,128)(2,1)} copy(bf16[2,660,768]{2,0,1:T(2,128)(2,1)} %all-gather.9.cloned.1.call-done) | data formatting | bytes 4055040 | tf_op jit(solution)/shard_map/all_gather | solution.py:69
  170.6 4.0 %fusion.4 = (f32[2,12,144]{2,1,0:T(8,128)S(1)}, f32[2,12,144,660]{3,2,1,0:T(8,128)S(1)}) fusion(pred[2,660]{1,0:T(4,128)(4,1)S(1)} %compare_or_fusion, bf16[2,144,12,64]{1,3,2,0:T(8,128)(2,1)S(1)} %bitcast.76, bf16[2,660,12,64]{1,3,2,0:T(8,128)(2,1)} %bitcast.75), kind=kOutput, calls=%fused_computation.6 | convolution fusion | flops 298802304 | bytes 11608872 | tf_op jit(solution)/shard_map/sihe,snhe->shin/dot_general | solution.py:79
  174.6 2.9 %fusion.5 = f32[2,12,144]{2,1,0:T(8,128)S(1)} fusion(f32[2,12,144,660]{3,2,1,0:T(8,128)S(1)} %get-tuple-element.26, f32[2,12,144]{2,1,0:T(8,128)S(1)} %broadcast_maximum_fusion, pred[2,660]{1,0:T(4,128)(4,1)S(1)} %compare_or_fusion), kind=kLoop, calls=%fused_computation.7 | loop fusion | flops 9120384 | bytes 9152808 | tf_op jit(solution)/shard_map/reduce_sum | solution.py:85
  177.6 3.2 %fusion.26 = bf16[2,144,12,64]{1,3,2,0:T(8,128)(2,1)S(1)} fusion(bf16[2,660,12,64]{1,3,2,0:T(8,128)(2,1)S(1)} %bitcast.77, f32[2,12,144,660]{3,2,1,0:T(8,128)S(1)} %get-tuple-element.26, f32[2,12,144]{2,1,0:T(8,128)S(1)} %broadcast_maximum_fusion, pred[2,660]{1,0:T(4,128)(4,1)S(1)} %compare_or_fusion, f32[2,144,12]{1,2,0:T(8,128)S(1)} %bitcast.81), kind=kOutput, calls=%fused_computation.29 | convolution fusion | flops 301529088 | bytes 11622696 | tf_op jit(solution)/shard_map/shin,snhe->sihe/dot_general | solution.py:87
  180.8 4.5 %convolution_convert_fusion = bf16[2,144,2432]{2,1,0:T(8,128)(2,1)} fusion(bf16[2,144,768]{1,2,0:T(8,128)(2,1)S(1)} %bitcast.78, bf16[768,2432]{1,0:T(8,128)(2,1)} %all-gather.11.cloned.1.call-done), kind=kOutput, calls=%fused_computation.18 | convolution fusion | flops 1076539392 | bytes 5578752 | tf_op jit(solution)/shard_map/sin,nd->sid/dot_general | solution.py:96
  185.3 46.7 %all-reduce.4.cloned.1.call-done = bf16[2,144,2432]{2,1,0:T(8,128)(2,1)} async-done(((bf16[2,144,2432]{2,1,0:T(8,128)(2,1)}), bf16[2,144,2432]{2,1,0:T(8,128)(2,1)}) %all-reduce.4.cloned.1.call-update) | async-done | bytes 1400848 | tf_op jit(solution)/shard_map/psum | solution.py:102
  232.0 2.9 %fusion.22 = bf16[2,144,2432]{2,1,0:T(8,128)(2,1)} fusion(bf16[2,144,2432]{2,1,0:T(8,128)(2,1)S(1)} %copy-done.1, bf16[2,144,2432]{2,1,0:T(8,128)(2,1)} %all-reduce.4.cloned.1.call-done, f32[2,2432]{1,0:T(2,128)S(1)} %get-tuple-element.19), kind=kLoop, calls=%fused_computation.26 | loop fusion | flops 3502080 | bytes 4221952 | tf_op jit(solution)/shard_map/convert_element_type | solution.py:103
  (40 shorter events, 2.8 us)
Async XLA Ops:
  7.4 17.3 %copy-start = (f32[10,3,2432]{2,1,0:T(4,128)S(1)}, f32[10,3,2432]{2,1,0:T(4,128)}, u32[]{:S(2)}) copy-start(f32[10,3,2432]{2,1,0:T(4,128)} %param.13) | copy-start | bytes 875524
  7.4 49.1 %all-reduce.6.cloned.1.call-start = ((), (), s32[]{:S(2)}) async-start(), calls=%async_computation.5 | async-start | bytes 1228800 | tf_op jit(solution)/shard_map/psum | solution.py:11
  13.5 46.6 %all-gather.5.cloned.1.call-start = ((), (), s32[]{:S(2)}) async-start(), calls=%async_computation | async-start | bytes 16809984 | tf_op jit(solution)/shard_map/all_gather | solution.py:56
  22.3 1.3 copy-start.1
  22.3 2.1 copy-start.3
  22.3 2.4 copy-start.4
  22.4 96.5 %all-gather.7.cloned.1.call-start = ((), (), s32[]{:S(2)}) async-start(), calls=%async_computation.1 | async-start | bytes 2534400 | tf_op jit(solution)/shard_map/all_gather | solution.py:70
  73.4 3.4 %copy-start.5 = (s32[2]{0:T(128)S(1)}, s32[2]{0:T(128)}, u32[]{:S(2)}) copy-start(s32[2]{0:T(128)} %param.12) | copy-start | bytes 28
  74.6 89.2 %all-gather.9.cloned.1.call-start = ((), (), s32[]{:S(2)}) async-start(), calls=%async_computation.2 | async-start | bytes 2534400 | tf_op jit(solution)/shard_map/all_gather | solution.py:69
  75.9 104.8 %all-gather.11.cloned.1.call-start = ((), (), s32[]{:S(2)}) async-start(), calls=%async_computation.3 | async-start | bytes 5603328 | tf_op jit(solution)/shard_map/all_gather | solution.py:99
  76.5 155.4 %all-reduce.4.cloned.1.call-start = ((), (), s32[]{:S(2)}) async-start(), calls=%async_computation.4 | async-start | bytes 2801664 | tf_op jit(solution)/shard_map/psum | solution.py:102
  174.6 2.9 %copy-start.2 = (bf16[2,660,768]{1,2,0:T(8,128)(2,1)S(1)}, bf16[2,660,768]{1,2,0:T(8,128)(2,1)}, u32[]{:S(2)}) copy-start(bf16[2,660,768]{1,2,0:T(8,128)(2,1)} %copy.30) | copy-start | bytes 6082564
Sparse Core Ops, SparseCore 0:
  13.7 42.7 all-reduce.5
  74.8 44.0 all-gather.6
  120.4 43.3 all-gather.8
  165.3 11.8 all-gather.10
  185.4 46.4 all-reduce.3
Sparse Core Ops, SparseCore 1:
  22.4 25.6 all-gather.4
where the time goes:
time: 243 us; the launch traced here: 242 us
  waiting for transfers between devices  159 us (65%)
  local copies, waits for them, and re-layouts  33.5 us (14%)
  matrix products  23.9 us (10%)
  between operations  16.8 us (7%)
  other arithmetic  8.55 us (4%)
    psum x1, waiting for transfers between devices, body(): summed_heads = lax.psum(proj.astype(jnp.bfloat16), 'mp').astype(jnp.float32)  46.7 us
    all_gather x1, waiting for transfers between devices, body(): value_piece = lax.all_gather(values, 'seq', axis=1, tiled=True)  41.7 us
    all_gather x1, waiting for transfers between devices, body(): key_piece = lax.all_gather(keys, 'seq', axis=1, tiled=True)  38.3 us
    psum x1, waiting for transfers between devices, broadcast(): return lax.psum(block, axis)  31.5 us
    dot_general x1, matrix products, body(): jnp.einsum('sid,dcn->sicn', normed, merged, preferred_element_type=jnp.fl...  11.9 us
    unnamed x13, local copies, waits for them, and re-layouts  9.99 us
    all_gather x1, local copies, waits for them, and re-layouts, body(): key_piece = lax.all_gather(keys, 'seq', axis=1, tiled=True)  6.73 us
    all_gather x1, local copies, waits for them, and re-layouts, body(): value_piece = lax.all_gather(values, 'seq', axis=1, tiled=True)  6.71 us
  transfers between devices with their start and end apart: 6, of which 4 were waited for; matrix products, arithmetic and copies ran while one was open for 16% of the time, Pallas kernels for 0%

commit v1 on v0

--- a/solution.py
+++ b/solution.py
@@ -103,6 +103,153 @@
     return (wide + gate * summed_heads).astype(jnp.bfloat16)
 
 
+def flip(block, axis):
+    return lax.ppermute(block, axis, [(0, 1), (1, 0)])
+
+
+def swap_pair(block, split_axis, concat_axis):
+    me = lax.axis_index("batch")
+    half = block.shape[split_axis] // 2
+    mine = lax.dynamic_slice_in_dim(block, me * half, half, split_axis)
+    away = lax.dynamic_slice_in_dim(block, (1 - me) * half, half, split_axis)
+    came = flip(away, "batch")
+    first = jnp.where(me == 0, mine, came)
+    second = jnp.where(me == 0, came, mine)
+    return jnp.concatenate([first, second], axis=concat_axis)
+
+
+def body_by_sample(
+    image_token_states,
+    timestep,
+    prompt_token_length,
+    modulation,
+    text_key_value,
+    frozen_query_key_value,
+    frozen_output_weight,
+    adapter_down_factors,
+    adapter_up_factors,
+    owner,
+):
+    samples, img_rows, width = image_token_states.shape
+    txt_rows = text_key_value.shape[2]
+    columns = frozen_query_key_value.shape[2]
+    heads_here = columns // HEAD_SIZE
+    steps_all = modulation.shape[0]
+    at_seq = lax.axis_index("seq")
+    at_mp = lax.axis_index("mp")
+    at_core = lax.axis_index("batch")
+    n_seq = 2 * samples
+
+    up_mine = jnp.zeros(adapter_up_factors.shape[1:2] + adapter_up_factors.shape[3:], jnp.bfloat16)
+    for which in range(3):
+        up_mine = jnp.where(owner[which] == at_seq, adapter_up_factors[0][:, which], up_mine)
+    up_mine = lax.dynamic_slice_in_dim(up_mine, at_core * columns, columns, 1)
+    packed = jnp.concatenate([adapter_down_factors[0], up_mine], axis=1)
+    packed = lax.all_gather(packed, "seq", axis=0)
+
+    length_row = jnp.broadcast_to(
+        prompt_token_length.astype(jnp.bfloat16)[:, None, None, None],
+        (samples, 2, 1, text_key_value.shape[3]),
+    )
+    text = swap_pair(jnp.concatenate([text_key_value, length_row], axis=2), 3, 0)
+
+    away_weight = flip(frozen_output_weight, "mp")
+    weight_here = lax.all_gather(frozen_output_weight, "batch", axis=0, tiled=True)
+    weight_away = lax.all_gather(away_weight, "batch", axis=0, tiled=True)
+
+    onehot = (timestep[:, None] == jnp.arange(steps_all, dtype=jnp.int32)[None, :]).astype(
+        jnp.float32
+    )
+    mods = jnp.einsum("st,tcd->scd", onehot, modulation, precision=lax.Precision.HIGHEST)
+    shift = mods[:, 0][:, None, :]
+    scale = mods[:, 1][:, None, :]
+    gate = mods[:, 2][:, None, :]
+    wide = image_token_states.astype(jnp.float32)
+
+    rows_mp = img_rows // 2
+    part = lax.dynamic_slice_in_dim(image_token_states, at_mp * rows_mp, rows_mp, 1).astype(
+        jnp.float32
+    )
+    mean = jnp.mean(part, axis=-1, keepdims=True)
+    centred = part - mean
+    var = jnp.mean(centred * centred, axis=-1, keepdims=True)
+    normed = (centred * lax.rsqrt(var + 1e-06) * (1.0 + scale) + shift).astype(jnp.bfloat16)
+
+    piece = swap_pair(normed, 1, 0)
+    piece = lax.all_to_all(piece, "seq", 0, 0, tiled=True)
+    text = lax.all_to_all(text, "seq", 0, 0, tiled=True)
+    piece_rows = piece.shape[1]
+    whole = lax.all_gather(
+        piece.reshape(n_seq * piece_rows, width), ("mp", "batch"), axis=0, tiled=True
+    )
+
+    triple = []
+    for which in range(3):
+        chosen = lax.dynamic_index_in_dim(packed, owner[which], 0, keepdims=False)
+        delta = jnp.einsum(
+            "rd,rn->dn", chosen[:, :width], chosen[:, width:], preferred_element_type=jnp.float32
+        )
+        merged = (frozen_query_key_value[:, which].astype(jnp.float32) + delta).astype(jnp.bfloat16)
+        triple.append(
+            jnp.dot(whole, merged, preferred_element_type=jnp.float32).astype(jnp.bfloat16)
+        )
+    queries, keys, values = triple
+    tokens = queries.shape[0]
+    text_keys = text[:, 0, :txt_rows].reshape(n_seq * txt_rows, columns)
+    text_values = text[:, 1, :txt_rows].reshape(n_seq * txt_rows, columns)
+    length = text[0, 0, txt_rows, 0].astype(jnp.int32)
+    keys = jnp.concatenate([keys, text_keys], axis=0)
+    values = jnp.concatenate([values, text_values], axis=0)
+    position = jnp.arange(keys.shape[0], dtype=jnp.int32)
+    live = position < tokens + length
+    scores = (
+        jnp.einsum(
+            "ihe,nhe->hin",
+            queries.reshape(-1, heads_here, HEAD_SIZE),
+            keys.reshape(-1, heads_here, HEAD_SIZE),
+            preferred_element_type=jnp.float32,
+        )
+        * HEAD_SIZE ** (-0.5)
+    )
+    scores = jnp.where(live[None, None, :], scores, -1e30)
+    top = jnp.max(scores, axis=-1, keepdims=True)
+    expo = jnp.exp(scores - top)
+    total = jnp.sum(expo, axis=-1)
+    summed = jnp.einsum(
+        "hin,nhe->ihe",
+        expo.astype(jnp.bfloat16),
+        values.reshape(-1, heads_here, HEAD_SIZE),
+        preferred_element_type=jnp.float32,
+    )
+    attn = (summed / total.T[:, :, None]).reshape(tokens, columns).astype(jnp.bfloat16)
+
+    attn = attn.reshape(-1, n_seq, piece_rows, columns).transpose(1, 0, 2, 3)
+    attn = lax.all_to_all(attn.reshape(n_seq, img_rows, columns), "seq", 0, 0, tiled=True)
+    attn = swap_pair(attn, 0, 2)
+    attn_away = flip(attn, "mp")
+    proj = jnp.einsum("sin,nd->sid", attn, weight_here, preferred_element_type=jnp.float32)
+    proj = proj + jnp.einsum(
+        "sin,nd->sid", attn_away, weight_away, preferred_element_type=jnp.float32
+    )
+    return (wide + gate * proj).astype(jnp.bfloat16)
+
+
+def pick(mesh):
+    def run(*arrays):
+        image, text = arrays[0], arrays[4]
+        sizes = mesh.shape
+        by_sample = (
+            sizes["batch"] == 2
+            and sizes["mp"] == 2
+            and sizes["seq"] == 2 * image.shape[0]
+            and image.shape[1] % 4 == 0
+            and sizes["seq"] * text.shape[2] <= 256
+        )
+        return (body_by_sample if by_sample else body)(*arrays)
+
+    return run
+
+
 def solution(mesh):
     placed = (
         P(("groups", "batch"), "seq", None),
@@ -117,7 +264,7 @@
         P(),
     )
     return jax.shard_map(
-        body,
+        pick(mesh),
         mesh=mesh,
         in_specs=placed,
         out_specs=P(("groups", "batch"), "seq", None),

time: 243 us -> 206 us (0.85)
  waiting for transfers between devices: 159 us -> 84.4 us
  blocking collectives: 0 us -> 44 us
  local copies, waits for them, and re-layouts: 33.5 us -> 8.19 us
  starting transfers between devices: 0.39 us -> 10.8 us
  matrix products: 23.9 us -> 28.9 us
  between operations: 16.8 us -> 20.9 us
    all_gather x4 -> x3, waiting for transfers between devices: 80 us -> 0.04 us  [the longest x1 0.02 us: body_by_sample(): lax.all_gather(frozen_output_weight, 'batch', axis=0, tiled=True)]
    psum x2 -> x0, waiting for transfers between devices: 78.1 us -> none  [the longest x1 46.7 us: body(): summed_heads = lax.psum(proj.astype(jnp.bfloat16), 'mp').astype(jnp.float32)]
    ppermute x0 -> x5, waiting for transfers between devices: none -> 68.7 us  [flip(): return lax.ppermute(block, axis, [(0, 1), (1, 0)])]
    all_to_all x0 -> x1, blocking collectives: none -> 26.4 us  [body_by_sample(): piece = lax.all_to_all(piece, 'seq', 0, 0, tiled=True)]
    all_gather x0 -> x1, blocking collectives: none -> 17.6 us  [body_by_sample(): packed = lax.all_gather(packed, 'seq', axis=0)]
    all_to_all x0 -> x2, waiting for transfers between devices: none -> 15.2 us  [the longest x1 9.48 us: body_by_sample(): lax.all_to_all(attn.reshape(n_seq, img_rows, columns), 'seq', 0, 0, tiled...]
    all_gather x2 -> x0, local copies, waits for them, and re-layouts: 13.4 us -> none  [the longest x1 6.73 us: body(): key_piece = lax.all_gather(keys, 'seq', axis=1, tiled=True)]
    unnamed x13 -> x16, local copies, waits for them, and re-layouts: 9.99 us -> 0.74 us
  transfers between devices with their start and end apart: 6 -> 10, of which waited for: 4 -> 6; matrix products, arithmetic and copies ran while one was open for 16% -> 16% of each run, Pallas kernels for 0% -> 0%
where the time goes in v1:
time: 206 us
  waiting for transfers between devices  84.4 us (41%)
  blocking collectives  44 us (21%)
  matrix products  28.9 us (14%)
  between operations  20.9 us (10%)
  starting transfers between devices  10.8 us (5%)
  other arithmetic  8.58 us (4%)
  local copies, waits for them, and re-layouts  8.19 us (4%)
    ppermute x5, waiting for transfers between devices, flip(): return lax.ppermute(block, axis, [(0, 1), (1, 0)])  68.7 us
    all_to_all x1, blocking collectives, body_by_sample(): piece = lax.all_to_all(piece, 'seq', 0, 0, tiled=True)  26.4 us
    all_gather x1, blocking collectives, body_by_sample(): packed = lax.all_gather(packed, 'seq', axis=0)  17.6 us
    dot_general x3, matrix products, body_by_sample(): jnp.dot(whole, merged, preferred_element_type=jnp.float32)  13.6 us
    all_to_all x1, waiting for transfers between devices, body_by_sample(): lax.all_to_all(attn.reshape(n_seq, img_rows, columns), 'seq', 0, 0, tiled...  9.48 us
    all_to_all x1, waiting for transfers between devices, body_by_sample(): text = lax.all_to_all(text, 'seq', 0, 0, tiled=True)  5.68 us
    dot_general x1, matrix products, body_by_sample(): jnp.einsum('sin,nd->sid', attn, weight_here, preferred_element_type=jnp.f...  5.09 us
  transfers between devices with their start and end apart: 10, of which 6 were waited for; matrix products, arithmetic and copies ran while one was open for 16% of the time, Pallas kernels for 0%

profile of v1, /device:TPU:0, one launch (start us, length us, event | category | flops | bytes accessed | tf_op | source)
XLA Modules:
  0.0 205.8 jit_solution(6005909734539775984)
XLA Ops:
  6.5 1.3 convert_reduce_fusion
  7.9 1.5 fusion.17
  10.4 1.7 fusion.20
  12.7 1.3 collective-permute-done
  14.4 26.4 %all_to_all.15 = bf16[4,36,2432]{2,1,0:T(8,128)(2,1)S(1)} all-to-all(bf16[4,36,2432]{2,1,0:T(8,128)(2,1)S(1)} %pad_maximum_fusion), channel_id=1, replica_groups=mesh['groups'=2,'seq'=4,'mp'=2,'batch'=2] {'seq'}, dimensions={0} | all-to-all | bytes 1400832 | tf_op jit(solution)/shard_map/all_to_all | solution.py:179
  41.9 1.6 collective-permute-start.4
  43.5 55.1 %collective-permute-done.4 = bf16[384,2432]{1,0:T(8,128)(2,1)} collective-permute-done((bf16[384,2432]{1,0:T(8,128)(2,1)S(1)}, bf16[384,2432]{1,0:T(8,128)(2,1)}, u32[]{:S(2)}, u32[]{:S(2)}) %collective-permute-start.4) | collective-permute-done | bytes 1867808 | tf_op jit(solution)/shard_map/ppermute | solution.py:107
  101.7 17.6 %all-gather = bf16[128,2816]{1,0:T(8,128)(2,1)S(1)} all-gather(bf16[32,2816]{1,0:T(8,128)(2,1)S(1)} %pad_maximum_fusion.2), channel_id=2, replica_groups=mesh['groups'=2,'seq'=4,'mp'=2,'batch'=2] {'seq'}, dimensions={0}, use_global_device_ids=true | all-gather | bytes 901120 | tf_op jit(solution)/shard_map/all_gather | solution.py:148
  125.5 3.5 %all-to-all-start.1 = ((bf16[4,2,22,384]{3,1,2,0:T(2,128)(2,1)}), bf16[4,2,22,384]{3,1,2,0:T(2,128)(2,1)S(1)}, u32[]{:S(2)}, u32[]{:S(2)}) async-start(bf16[4,2,22,384]{3,1,2,0:T(2,128)(2,1)} %pad_maximum_fusion.3), calls=%async_computation.1 | async-start | bytes 270336 | tf_op jit(solution)/shard_map/all_to_all | solution.py:180
  129.1 5.7 %all-to-all-done.1 = bf16[4,2,22,384]{3,1,2,0:T(2,128)(2,1)S(1)} async-done(((bf16[4,2,22,384]{3,1,2,0:T(2,128)(2,1)}), bf16[4,2,22,384]{3,1,2,0:T(2,128)(2,1)S(1)}, u32[]{:S(2)}, u32[]{:S(2)}) %all-to-all-start.1) | async-done | bytes 135200 | tf_op jit(solution)/shard_map/all_to_all | solution.py:180
  137.2 4.5 %fusion.29 = bf16[576,384]{1,0:T(8,128)(2,1)S(1)} fusion(bf16[576,2432]{1,0:T(8,128)(2,1)} %all-gather.5.cloned.1.call-done, bf16[2432,3,384]{2,0,1:T(8,128)(2,1)} %param.15, bf16[32,2816]{1,0:T(8,128)(2,1)S(1)} %get-tuple-element.12), kind=kOutput, calls=%fused_computation.34 | convolution fusion | flops 1138630656 | bytes 5292032 | tf_op jit(solution)/shard_map/dot_general | solution.py:194
  142.0 4.5 %fusion.28 = bf16[576,384]{1,0:T(8,128)(2,1)S(1)} fusion(bf16[576,2432]{1,0:T(8,128)(2,1)} %all-gather.5.cloned.1.call-done, bf16[2432,3,384]{2,0,1:T(8,128)(2,1)} %param.15, bf16[32,2816]{1,0:T(8,128)(2,1)S(1)} %get-tuple-element.13), kind=kOutput, calls=%fused_computation.33 | convolution fusion | flops 1138630656 | bytes 5292032 | tf_op jit(solution)/shard_map/dot_general | solution.py:194
  146.8 4.5 %fusion.27 = bf16[576,384]{1,0:T(8,128)(2,1)S(1)} fusion(bf16[576,2432]{1,0:T(8,128)(2,1)} %all-gather.5.cloned.1.call-done, bf16[2432,3,384]{2,0,1:T(8,128)(2,1)} %param.15, bf16[32,2816]{1,0:T(8,128)(2,1)S(1)} %get-tuple-element.11), kind=kOutput, calls=%fused_computation.32 | convolution fusion | flops 1138630656 | bytes 5292032 | tf_op jit(solution)/shard_map/dot_general | solution.py:194
  151.6 3.2 %fusion = (f32[6,576]{1,0:T(8,128)S(1)}, f32[6,576,660]{1,2,0:T(8,128)S(1)}) fusion(pred[660]{0:T(1024)(128)(4,1)S(1)} %iota_compare_fusion, bf16[576,6,64]{0,2,1:T(8,128)(2,1)S(1)} %bitcast.68, bf16[84,6,64]{0,2,1:T(8,128)(2,1)S(1)} %copy.23, bf16[576,6,64]{0,2,1:T(8,128)(2,1)S(1)} %bitcast.67), kind=kOutput, calls=%fused_computation.2 | convolution fusion | flops 299816064 | bytes 10087572 | tf_op jit(solution)/shard_map/ihe,nhe->hin/dot_general | solution.py:206
  154.7 2.5 %fusion.1 = f32[6,576]{1,0:T(8,128)S(1)} fusion(f32[6,576,660]{1,2,0:T(8,128)S(1)} %get-tuple-element.26, f32[6,576]{1,0:T(8,128)S(1)} %get-tuple-element.25, pred[660]{0:T(1024)(128)(4,1)S(1)} %iota_compare_fusion), kind=kLoop, calls=%fused_computation.3 | loop fusion | flops 9120384 | bytes 9152148 | tf_op jit(solution)/shard_map/reduce_sum | solution.py:217
  157.2 2.6 %divide_convert_fusion = bf16[576,6,64]{0,2,1:T(8,128)(2,1)S(1)} fusion(f32[6,576,660]{1,2,0:T(8,128)S(1)} %get-tuple-element.26, f32[6,576]{1,0:T(8,128)S(1)} %get-tuple-element.25, pred[660]{0:T(1024)(128)(4,1)S(1)} %iota_compare_fusion, bf16[84,6,64]{0,2,1:T(8,128)(2,1)S(1)} %copy.20, bf16[576,6,64]{0,2,1:T(8,128)(2,1)S(1)} %bitcast.71, ...), kind=kOutput, calls=%fused_computation.35 | convolution fusion | flops 302542848 | bytes 10101396 | tf_op jit(solution)/shard_map/hin,nhe->ihe/dot_general | solution.py:218
  159.8 1.3 copy.24
  162.9 3.5 %all-to-all-start.2 = ((bf16[4,144,384]{2,1,0:T(8,128)(2,1)}), bf16[4,144,384]{2,1,0:T(8,128)(2,1)S(1)}, u32[]{:S(2)}, u32[]{:S(2)}) async-start(bf16[4,144,384]{2,1,0:T(8,128)(2,1)} %copy.26), calls=%async_computation.2 | async-start | bytes 884736 | tf_op jit(solution)/shard_map/all_to_all | solution.py:227
  166.4 9.5 %all-to-all-done.2 = bf16[4,144,384]{2,1,0:T(8,128)(2,1)S(1)} async-done(((bf16[4,144,384]{2,1,0:T(8,128)(2,1)}), bf16[4,144,384]{2,1,0:T(8,128)(2,1)S(1)}, u32[]{:S(2)}, u32[]{:S(2)}) %all-to-all-start.2) | async-done | bytes 442400 | tf_op jit(solution)/shard_map/all_to_all | solution.py:227
  176.0 1.5 collective-permute-done.2
  178.2 1.6 collective-permute-start.3
  179.8 10.8 %collective-permute-done.3 = bf16[2,144,768]{2,1,0:T(8,128)(2,1)} collective-permute-done((bf16[2,144,768]{2,1,0:T(8,128)(2,1)S(1)}, bf16[2,144,768]{2,1,0:T(8,128)(2,1)}, u32[]{:S(2)}, u32[]{:S(2)}) %collective-permute-start.3) | collective-permute-done | bytes 442400 | tf_op jit(solution)/shard_map/ppermute | solution.py:107
  190.6 3.5 %fusion.12 = f32[2,144,2432]{2,1,0:T(8,128)S(1)} fusion(bf16[2,144,768]{2,1,0:T(8,128)(2,1)} %collective-permute-done.3, bf16[768,2432]{1,0:T(8,128)(2,1)} %all-gather.9.cloned.1.call-done), kind=kOutput, calls=%fused_computation.17 | convolution fusion | flops 1075838976 | bytes 6979584 | tf_op jit(solution)/shard_map/sin,nd->sid/dot_general | solution.py:231
  194.1 5.1 %fusion.11 = bf16[2,144,2432]{2,1,0:T(8,128)(2,1)} fusion(f32[2,144,2432]{2,1,0:T(8,128)S(1)} %fusion.12, bf16[768,2432]{1,0:T(8,128)(2,1)} %all-gather.7.cloned.1.call-done, bf16[2,144,2432]{2,1,0:T(8,128)(2,1)} %param.10, f32[2,2432]{1,0:T(2,128)S(1)} %get-tuple-element.19, bf16[2,144,384]{2,1,0:T(8,128)(2,1)} %copy-done.1, ...), kind=kOutput, calls=%fused_computation.16 | convolution fusion | flops 1080225792 | bytes 9800704 | tf_op jit(solution)/shard_map/sin,nd->sid/dot_general | solution.py:230
  (64 shorter events, 10.7 us)
Async XLA Ops:
  6.5 2.8 %copy-start = (f32[10,3,2432]{2,1,0:T(4,128)S(1)}, f32[10,3,2432]{2,1,0:T(4,128)}, u32[]{:S(2)}) copy-start(f32[10,3,2432]{2,1,0:T(4,128)} %param.13) | copy-start | bytes 875524
  6.5 130.6 %all-gather.5.cloned.1.call-start = ((), (), s32[]{:S(2)}) async-start(), calls=%async_computation.3 | async-start | bytes 3502080 | tf_op jit(solution)/shard_map/all_gather | solution.py:182
  12.2 1.9 collective-permute-start
  14.3 27.6 %copy-start.2 = (bf16[384,2432]{1,0:T(8,128)(2,1)S(1)}, bf16[384,2432]{1,0:T(8,128)(2,1)}, u32[]{:S(2)}) copy-start(bf16[384,2432]{1,0:T(8,128)(2,1)} %param.16) | copy-start | bytes 5603332
  14.4 84.2 %copy-start.7 = (s32[2]{0:T(128)S(1)}, s32[2]{0:T(128)}, u32[]{:S(2)}) copy-start(s32[2]{0:T(128)} %param.12) | copy-start | bytes 28
  14.4 84.3 %copy-start.3 = (bf16[2,2,21,768]{3,1,2,0:T(2,128)(2,1)S(1)}, bf16[2,2,21,768]{3,1,2,0:T(2,128)(2,1)}, u32[]{:S(2)}) copy-start(bf16[2,2,21,768]{3,1,2,0:T(2,128)(2,1)} %param.14) | copy-start | bytes 387076
  40.8 58.5 %copy-start.6 = (s32[3]{0:T(128)S(1)}, s32[3]{0:T(128)}, u32[]{:S(2)}) copy-start(s32[3]{0:T(128)} %param.19) | copy-start | bytes 40
  41.8 59.8 %copy-start.5 = (bf16[1,32,3,768]{3,1,2,0:T(8,128)(2,1)S(1)}, bf16[1,32,3,768]{3,1,2,0:T(8,128)(2,1)}, u32[]{:S(2)}) copy-start(bf16[1,32,3,768]{3,1,2,0:T(8,128)(2,1)} %param.18) | copy-start | bytes 442372
  41.8 59.9 %copy-start.4 = (bf16[1,32,2432]{2,1,0:T(8,128)(2,1)S(1)}, bf16[1,32,2432]{2,1,0:T(8,128)(2,1)}, u32[]{:S(2)}) copy-start(bf16[1,32,2432]{2,1,0:T(8,128)(2,1)} %param.17) | copy-start | bytes 466948
  41.8 137.9 %all-gather.9.cloned.1.call-start = ((), (), s32[]{:S(2)}) async-start(), calls=%async_computation.5 | async-start | bytes 5603328 | tf_op jit(solution)/shard_map/all_gather | solution.py:158
  41.9 56.6 %collective-permute-start.4 = (bf16[384,2432]{1,0:T(8,128)(2,1)S(1)}, bf16[384,2432]{1,0:T(8,128)(2,1)}, u32[]{:S(2)}, u32[]{:S(2)}) collective-permute-start(bf16[384,2432]{1,0:T(8,128)(2,1)S(1)} %copy-done.2), channel_id=1, source_target_pairs={{0,2},{2,0},{1,3},{3,1},{4,6},{6,4},{5,7},{7,5},{8,10},{10,8},{9,1... | collective-permute-start | bytes 5603336 | tf_op jit(solution)/shard_map/ppermute | solution.py:107
  98.5 95.6 %all-gather.7.cloned.1.call-start = ((), (), s32[]{:S(2)}) async-start(), calls=%async_computation.4 | async-start | bytes 5603328 | tf_op jit(solution)/shard_map/all_gather | solution.py:157
  98.8 25.7 %collective-permute-start.1 = (bf16[2,2,22,384]{3,1,2,0:T(2,128)(2,1)S(1)}, bf16[2,2,22,384]{3,1,2,0:T(2,128)(2,1)S(1)}, u32[]{:S(2)}, u32[]{:S(2)}) collective-permute-start(bf16[2,2,22,384]{3,1,2,0:T(2,128)(2,1)S(1)} %fusion.47), channel_id=1, source_target_pairs={{0,1},{1,0},{2,3},{3,2},{4,5},{5,4},{6,7},{7,6},{8,9},{9,8},{10,11... | collective-permute-start | bytes 202760 | tf_op jit(solution)/shard_map/ppermute | solution.py:107
  125.5 9.3 %all-to-all-start.1 = ((bf16[4,2,22,384]{3,1,2,0:T(2,128)(2,1)}), bf16[4,2,22,384]{3,1,2,0:T(2,128)(2,1)S(1)}, u32[]{:S(2)}, u32[]{:S(2)}) async-start(bf16[4,2,22,384]{3,1,2,0:T(2,128)(2,1)} %pad_maximum_fusion.3), calls=%async_computation.1 | async-start | bytes 270336 | tf_op jit(solution)/shard_map/all_to_all | solution.py:180
  162.9 13.0 %all-to-all-start.2 = ((bf16[4,144,384]{2,1,0:T(8,128)(2,1)}), bf16[4,144,384]{2,1,0:T(8,128)(2,1)S(1)}, u32[]{:S(2)}, u32[]{:S(2)}) async-start(bf16[4,144,384]{2,1,0:T(8,128)(2,1)} %copy.26), calls=%async_computation.2 | async-start | bytes 884736 | tf_op jit(solution)/shard_map/all_to_all | solution.py:227
  175.9 1.5 collective-permute-start.2
  177.5 0.7 copy-start.1
  178.2 12.4 %collective-permute-start.3 = (bf16[2,144,768]{2,1,0:T(8,128)(2,1)S(1)}, bf16[2,144,768]{2,1,0:T(8,128)(2,1)}, u32[]{:S(2)}, u32[]{:S(2)}) collective-permute-start(bf16[2,144,768]{2,1,0:T(8,128)(2,1)S(1)} %pad_maximum_fusion.1), channel_id=1, source_target_pairs={{0,2},{2,0},{1,3},{3,1},{4,6},{6,4},{5,7},{7,5},{8,10},{10,8},{9,1... | collective-permute-start | bytes 1327112 | tf_op jit(solution)/shard_map/ppermute | solution.py:107
Sparse Core Ops, SparseCore 0:
  42.0 40.8 all-gather.4
  98.7 12.6 all-gather.8
  112.9 14.1 all-gather.6

commit v2 on v1

--- a/solution.py
+++ b/solution.py
@@ -152,10 +152,10 @@
         (samples, 2, 1, text_key_value.shape[3]),
     )
     text = swap_pair(jnp.concatenate([text_key_value, length_row], axis=2), 3, 0)
+    text = lax.all_gather(text, "seq", axis=0)
+    text = lax.dynamic_index_in_dim(text, at_seq, 1, keepdims=False)
 
     away_weight = flip(frozen_output_weight, "mp")
-    weight_here = lax.all_gather(frozen_output_weight, "batch", axis=0, tiled=True)
-    weight_away = lax.all_gather(away_weight, "batch", axis=0, tiled=True)
 
     onehot = (timestep[:, None] == jnp.arange(steps_all, dtype=jnp.int32)[None, :]).astype(
         jnp.float32
@@ -177,23 +177,34 @@
 
     piece = swap_pair(normed, 1, 0)
     piece = lax.all_to_all(piece, "seq", 0, 0, tiled=True)
-    text = lax.all_to_all(text, "seq", 0, 0, tiled=True)
     piece_rows = piece.shape[1]
-    whole = lax.all_gather(
-        piece.reshape(n_seq * piece_rows, width), ("mp", "batch"), axis=0, tiled=True
-    )
-
-    triple = []
+    piece = piece.reshape(n_seq * piece_rows, width)
+    piece_mp = flip(piece, "mp")
+    piece_core = flip(piece, "batch")
+    piece_both = flip(piece_mp, "batch")
+    merged = []
     for which in range(3):
         chosen = lax.dynamic_index_in_dim(packed, owner[which], 0, keepdims=False)
         delta = jnp.einsum(
             "rd,rn->dn", chosen[:, :width], chosen[:, width:], preferred_element_type=jnp.float32
         )
-        merged = (frozen_query_key_value[:, which].astype(jnp.float32) + delta).astype(jnp.bfloat16)
-        triple.append(
-            jnp.dot(whole, merged, preferred_element_type=jnp.float32).astype(jnp.bfloat16)
-        )
+        merged.append(
+            (frozen_query_key_value[:, which].astype(jnp.float32) + delta).astype(jnp.bfloat16)
+        )
+    merged = lax.optimization_barrier(merged)
+    early = jnp.concatenate([piece, piece_core], axis=0)
+    late = jnp.concatenate([piece_mp, piece_both], axis=0)
+    triple = []
+    halves = [
+        [jnp.dot(rows, m, preferred_element_type=jnp.float32).astype(jnp.bfloat16) for m in merged]
+        for rows in (early, late)
+    ]
+    for which in range(3):
+        triple.append(jnp.concatenate([halves[0][which], halves[1][which]], axis=0))
     queries, keys, values = triple
+    away_weight, queries = lax.optimization_barrier((away_weight, queries))
+    weight_here = lax.all_gather(frozen_output_weight, "batch", axis=0, tiled=True)
+    weight_away = lax.all_gather(away_weight, "batch", axis=0, tiled=True)
     tokens = queries.shape[0]
     text_keys = text[:, 0, :txt_rows].reshape(n_seq * txt_rows, columns)
     text_values = text[:, 1, :txt_rows].reshape(n_seq * txt_rows, columns)
@@ -223,7 +234,10 @@
     )
     attn = (summed / total.T[:, :, None]).reshape(tokens, columns).astype(jnp.bfloat16)
 
-    attn = attn.reshape(-1, n_seq, piece_rows, columns).transpose(1, 0, 2, 3)
+    attn = attn.reshape(2, 2, n_seq, piece_rows, columns)
+    attn = jnp.where(at_mp == 0, attn, attn[::-1])
+    attn = jnp.where(at_core == 0, attn, attn[:, ::-1])
+    attn = attn.reshape(4, n_seq, piece_rows, columns).transpose(1, 0, 2, 3)
     attn = lax.all_to_all(attn.reshape(n_seq, img_rows, columns), "seq", 0, 0, tiled=True)
     attn = swap_pair(attn, 0, 2)
     attn_away = flip(attn, "mp")

time: 206 us -> 181 us (0.88)
  waiting for transfers between devices: 84.4 us -> 36.5 us
  matrix products: 28.9 us -> 42.9 us
  local copies, waits for them, and re-layouts: 8.19 us -> 13 us
  starting transfers between devices: 10.8 us -> 14.3 us
    ppermute x5 -> x8, waiting for transfers between devices: 68.7 us -> 26 us  [flip(): return lax.ppermute(block, axis, [(0, 1), (1, 0)])]
    all_to_all x1 -> x0, blocking collectives: 26.4 us -> none  [body_by_sample(): piece = lax.all_to_all(piece, 'seq', 0, 0, tiled=True)]
    all_gather x0 -> x1, blocking collectives: none -> 16.2 us  [body_by_sample(): text = lax.all_gather(text, 'seq', axis=0)]
    all_gather x1, blocking collectives: 17.6 us -> 27.2 us  [body_by_sample(): packed = lax.all_gather(packed, 'seq', axis=0)]
    dot_general x3 -> x9, matrix products: 13.6 us -> 22.4 us  [the longest x6 12.1 us: body_by_sample(): jnp.dot(rows, m, preferred_element_type=jnp.float32).astype(jnp.bfloat16)]
    all_to_all x1, waiting for transfers between devices: 5.68 us -> 0.01 us  [body_by_sample(): piece = lax.all_to_all(piece, 'seq', 0, 0, tiled=True)]
    dot_general x1, matrix products: 2.6 us -> 6.79 us  [body_by_sample(): jnp.einsum('hin,nhe->ihe', expo.astype(jnp.bfloat16), values.reshape(-1,...]
    unnamed x16 -> x32, local copies, waits for them, and re-layouts: 0.74 us -> 3.42 us
  transfers between devices with their start and end apart: 10 -> 12, of which waited for: 6 -> 6; matrix products, arithmetic and copies ran while one was open for 16% -> 28% of each run, Pallas kernels for 0% -> 0%
where the time goes in v2:
time: 181 us; the launch traced here: 180 us
  blocking collectives  43.5 us (24%)
  matrix products  42.9 us (24%)
  waiting for transfers between devices  36.5 us (20%)
  between operations  21.9 us (12%)
  starting transfers between devices  14.3 us (8%)
  local copies, waits for them, and re-layouts  13 us (7%)
  other arithmetic  7.81 us (4%)
    all_gather x1, blocking collectives, body_by_sample(): packed = lax.all_gather(packed, 'seq', axis=0)  27.2 us
    ppermute x8, waiting for transfers between devices, flip(): return lax.ppermute(block, axis, [(0, 1), (1, 0)])  26 us
    all_gather x1, blocking collectives, body_by_sample(): text = lax.all_gather(text, 'seq', axis=0)  16.2 us
    dot_general x6, matrix products, body_by_sample(): jnp.dot(rows, m, preferred_element_type=jnp.float32).astype(jnp.bfloat16)  12.1 us
    all_to_all x1, waiting for transfers between devices, body_by_sample(): lax.all_to_all(attn.reshape(n_seq, img_rows, columns), 'seq', 0, 0, tiled...  10.5 us
    dot_general x3, matrix products, body_by_sample(): jnp.einsum('rd,rn->dn', chosen[:, :width], chosen[:, width:], preferred_e...  10.3 us
    dot_general x1, matrix products, body_by_sample(): jnp.einsum('hin,nhe->ihe', expo.astype(jnp.bfloat16), values.reshape(-1,...  6.79 us
    dot_general x1, matrix products, body_by_sample(): jnp.einsum('sin,nd->sid', attn, weight_here, preferred_element_type=jnp.f...  5.08 us
  transfers between devices with their start and end apart: 12, of which 6 were waited for; matrix products, arithmetic and copies ran while one was open for 28% of the time, Pallas kernels for 0%

profile of v2, /device:TPU:0, one launch (start us, length us, event | category | flops | bytes accessed | tf_op | source)
XLA Modules:
  0.0 179.9 jit_solution(15710901648179511367)
XLA Ops:
  6.5 1.4 convert_reduce_fusion
  8.0 1.5 fusion.17
  11.8 2.6 %collective-permute-start.5 = (bf16[384,2432]{1,0:T(8,128)(2,1)}, bf16[384,2432]{1,0:T(8,128)(2,1)}, u32[]{:S(2)}, u32[]{:S(2)}) collective-permute-start(bf16[384,2432]{1,0:T(8,128)(2,1)} %param.16), channel_id=1, source_target_pairs={{0,2},{2,0},{1,3},{3,1},{4,6},{6,4},{5,7},{7,5},{8,10},{10,8},{9,1... | collective-permute-start | bytes 5603336 | tf_op jit(solution)/shard_map/ppermute | solution.py:107
  18.1 4.9 %all-to-all-start = ((bf16[4,36,2432]{2,1,0:T(8,128)(2,1)}), bf16[4,36,2432]{2,1,0:T(8,128)(2,1)S(1)}, u32[]{:S(2)}, u32[]{:S(2)}) async-start(bf16[4,36,2432]{2,1,0:T(8,128)(2,1)} %pad_maximum_fusion), calls=%async_computation | async-start | bytes 1556480 | tf_op jit(solution)/shard_map/all_to_all | solution.py:179
  28.6 27.2 %all-gather = bf16[128,2816]{1,0:T(8,128)(2,1)S(1)} all-gather(bf16[32,2816]{1,0:T(8,128)(2,1)S(1)} %pad_maximum_fusion.3), channel_id=2, replica_groups=mesh['groups'=2,'seq'=4,'mp'=2,'batch'=2] {'seq'}, dimensions={0}, use_global_device_ids=true | all-gather | bytes 901120 | tf_op jit(solution)/shard_map/all_gather | solution.py:148
  55.9 3.5 %fusion.7 = bf16[2432,384]{1,0:T(8,128)(2,1)} fusion(bf16[2432,3,384]{2,0,1:T(8,128)(2,1)} %param.15, bf16[32,2816]{1,0:T(8,128)(2,1)S(1)} %get-tuple-element.21), kind=kOutput, calls=%fused_computation.12 | convolution fusion | flops 62570496 | bytes 3915776 | tf_op jit(solution)/shard_map/rd,rn->dn/dot_general | solution.py:188
  60.2 3.4 %fusion.8 = bf16[2432,384]{1,0:T(8,128)(2,1)} fusion(bf16[2432,3,384]{2,0,1:T(8,128)(2,1)} %param.15, bf16[32,2816]{1,0:T(8,128)(2,1)S(1)} %get-tuple-element.20), kind=kOutput, calls=%fused_computation.13 | convolution fusion | flops 62570496 | bytes 3915776 | tf_op jit(solution)/shard_map/rd,rn->dn/dot_general | solution.py:188
  63.7 3.4 %fusion.9 = bf16[2432,384]{1,0:T(8,128)(2,1)} fusion(bf16[2432,3,384]{2,0,1:T(8,128)(2,1)} %param.15, bf16[32,2816]{1,0:T(8,128)(2,1)S(1)} %get-tuple-element.19), kind=kOutput, calls=%fused_computation.14 | convolution fusion | flops 62570496 | bytes 3915776 | tf_op jit(solution)/shard_map/rd,rn->dn/dot_general | solution.py:188
  67.2 10.6 %collective-permute-done.2 = bf16[144,2432]{1,0:T(8,128)(2,1)S(1)} collective-permute-done((bf16[144,2432]{1,0:T(8,128)(2,1)S(1)}, bf16[144,2432]{1,0:T(8,128)(2,1)S(1)}, u32[]{:S(2)}, u32[]{:S(2)}) %collective-permute-start.2) | collective-permute-done | bytes 700448 | tf_op jit(solution)/shard_map/ppermute | solution.py:107
  83.8 16.2 %all-gather.1 = bf16[16,2,22,384]{3,1,2,0:T(2,128)(2,1)S(1)} all-gather(bf16[4,2,22,384]{3,1,2,0:T(2,128)(2,1)S(1)} %pad_maximum_fusion.4), channel_id=3, replica_groups=mesh['groups'=2,'seq'=4,'mp'=2,'batch'=2] {'seq'}, dimensions={0}, use_global_device_ids=true | all-gather | bytes 675840 | tf_op jit(solution)/shard_map/all_gather | solution.py:155
  103.1 3.4 %convolution_convert_fusion.1 = bf16[288,384]{1,0:T(8,128)(2,1)S(1)} fusion(bf16[288,2432]{1,0:T(8,128)(2,1)} %copy-done.7, bf16[2432,384]{1,0:T(8,128)(2,1)} %fusion.8), kind=kOutput, calls=%fused_computation.30 | convolution fusion | flops 538030080 | bytes 3489792 | tf_op jit(solution)/shard_map/dot_general | solution.py:199
  107.5 2.3 %convolution_convert_fusion.5 = bf16[288,384]{1,0:T(8,128)(2,1)S(1)} fusion(bf16[288,2432]{1,0:T(8,128)(2,1)} %copy-done.7, bf16[2432,384]{1,0:T(8,128)(2,1)S(1)} %copy-done.4), kind=kOutput, calls=%fused_computation.34 | convolution fusion | flops 538030080 | bytes 3489792 | tf_op jit(solution)/shard_map/dot_general | solution.py:199
  110.0 3.6 %convolution_convert_fusion = bf16[288,384]{1,0:T(8,128)(2,1)} fusion(bf16[288,2432]{1,0:T(8,128)(2,1)} %copy-done.8, bf16[2432,384]{1,0:T(8,128)(2,1)} %fusion.8), kind=kOutput, calls=%fused_computation.29 | convolution fusion | flops 538030080 | bytes 3489792 | tf_op jit(solution)/shard_map/dot_general | solution.py:199
  115.0 4.2 %fusion = (f32[6,576]{1,0:T(8,128)S(1)}, f32[6,576,660]{1,2,0:T(8,128)S(1)}) fusion(pred[660]{0:T(1024)(128)(4,1)S(1)} %iota_compare_fusion, bf16[576,6,64]{0,2,1:T(8,128)(2,1)S(1)} %bitcast.81, bf16[84,6,64]{0,2,1:T(8,128)(2,1)} %copy.39, bf16[288,6,64]{0,2,1:T(8,128)(2,1)S(1)} %bitcast.85, bf16[288,6,64]{0,2,1:T(8,128)(2,1)} %bitcast.83), kind=kOutput, calls=%fused_computation.2 | convolution fusion | flops 300322944 | bytes 10087572 | tf_op jit(solution)/shard_map/ihe,nhe->hin/dot_general | solution.py:217
  119.2 2.3 %fusion.1 = f32[6,576]{1,0:T(8,128)S(1)} fusion(f32[6,576,660]{1,2,0:T(8,128)S(1)} %get-tuple-element.36, f32[6,576]{1,0:T(8,128)S(1)} %get-tuple-element.35, pred[660]{0:T(1024)(128)(4,1)S(1)} %iota_compare_fusion), kind=kLoop, calls=%fused_computation.3 | loop fusion | flops 9120384 | bytes 9152148 | tf_op jit(solution)/shard_map/reduce_sum | solution.py:228
  121.5 1.6 copy-done.1
  124.2 6.8 %divide_convert_fusion = bf16[576,6,64]{0,2,1:T(8,128)(2,1)S(1)} fusion(f32[6,576,660]{1,2,0:T(8,128)} %copy-done.1, f32[6,576]{1,0:T(8,128)S(1)} %get-tuple-element.35, pred[660]{0:T(1024)(128)(4,1)S(1)} %iota_compare_fusion, bf16[84,6,64]{0,2,1:T(8,128)(2,1)S(1)} %copy-done.12, bf16[288,6,64]{0,2,1:T(8,128)(2,1)S(1)} %bitcast.84, ...), kind=kOutput, calls=%fused_computation.35 | convolution fusion | flops 303049728 | bytes 10101396 | tf_op jit(solution)/shard_map/hin,nhe->ihe/dot_general | solution.py:229
  131.0 1.3 copy.40
  134.3 4.9 %all-to-all-start.1 = ((bf16[4,144,384]{2,1,0:T(8,128)(2,1)}), bf16[4,144,384]{2,1,0:T(8,128)(2,1)S(1)}, u32[]{:S(2)}, u32[]{:S(2)}) async-start(bf16[4,144,384]{2,1,0:T(8,128)(2,1)} %copy.42), calls=%async_computation.1 | async-start | bytes 884736 | tf_op jit(solution)/shard_map/all_to_all | solution.py:241
  139.2 10.5 %all-to-all-done.1 = bf16[4,144,384]{2,1,0:T(8,128)(2,1)S(1)} async-done(((bf16[4,144,384]{2,1,0:T(8,128)(2,1)}), bf16[4,144,384]{2,1,0:T(8,128)(2,1)S(1)}, u32[]{:S(2)}, u32[]{:S(2)}) %all-to-all-start.1) | async-done | bytes 442400 | tf_op jit(solution)/shard_map/all_to_all | solution.py:241
  149.8 1.5 collective-permute-done.6
  152.4 12.0 %collective-permute-done.7 = bf16[2,144,768]{2,1,0:T(8,128)(2,1)} collective-permute-done((bf16[2,144,768]{2,1,0:T(8,128)(2,1)S(1)}, bf16[2,144,768]{2,1,0:T(8,128)(2,1)}, u32[]{:S(2)}, u32[]{:S(2)}) %collective-permute-start.7) | collective-permute-done | bytes 442400 | tf_op jit(solution)/shard_map/ppermute | solution.py:107
  164.4 3.5 %fusion.12 = f32[2,144,2432]{2,1,0:T(8,128)S(1)} fusion(bf16[2,144,768]{2,1,0:T(8,128)(2,1)} %collective-permute-done.7, bf16[768,2432]{1,0:T(8,128)(2,1)} %all-gather.7.cloned.1.call-done), kind=kOutput, calls=%fused_computation.17 | convolution fusion | flops 1075838976 | bytes 6979584 | tf_op jit(solution)/shard_map/sin,nd->sid/dot_general | solution.py:245
  168.0 5.1 %fusion.11 = bf16[2,144,2432]{2,1,0:T(8,128)(2,1)} fusion(f32[2,144,2432]{2,1,0:T(8,128)S(1)} %fusion.12, bf16[768,2432]{1,0:T(8,128)(2,1)} %all-gather.5.cloned.1.call-done, bf16[2,144,2432]{2,1,0:T(8,128)(2,1)} %param.10, f32[2,2432]{1,0:T(2,128)S(1)} %get-tuple-element.29, bf16[2,144,384]{2,1,0:T(8,128)(2,1)} %copy-done.3, ...), kind=kOutput, calls=%fused_computation.16 | convolution fusion | flops 1080225792 | bytes 9800704 | tf_op jit(solution)/shard_map/sin,nd->sid/dot_general | solution.py:244
  (98 shorter events, 20.4 us)
Async XLA Ops:
  6.5 3.0 %copy-start = (f32[10,3,2432]{2,1,0:T(4,128)S(1)}, f32[10,3,2432]{2,1,0:T(4,128)}, u32[]{:S(2)}) copy-start(f32[10,3,2432]{2,1,0:T(4,128)} %param.13) | copy-start | bytes 875524
  6.5 4.0 %copy-start.2 = (bf16[2,144,2432]{2,1,0:T(8,128)(2,1)S(1)}, bf16[2,144,2432]{2,1,0:T(8,128)(2,1)}, u32[]{:S(2)}) copy-start(bf16[2,144,2432]{2,1,0:T(8,128)(2,1)} %param.10) | copy-start | bytes 4202500
  8.0 6.4 %copy-start.13 = (s32[3]{0:T(128)S(1)}, s32[3]{0:T(128)}, u32[]{:S(2)}) copy-start(s32[3]{0:T(128)} %param.19) | copy-start | bytes 40
  8.0 8.9 %copy-start.11 = (bf16[1,32,3,768]{3,1,2,0:T(8,128)(2,1)S(1)}, bf16[1,32,3,768]{3,1,2,0:T(8,128)(2,1)}, u32[]{:S(2)}) copy-start(bf16[1,32,3,768]{3,1,2,0:T(8,128)(2,1)} %param.18) | copy-start | bytes 442372
  11.2 5.7 %collective-permute-start = (bf16[2,36,2432]{2,1,0:T(8,128)(2,1)S(1)}, bf16[2,36,2432]{2,1,0:T(8,128)(2,1)S(1)}, u32[]{:S(2)}, u32[]{:S(2)}) collective-permute-start(bf16[2,36,2432]{2,1,0:T(8,128)(2,1)S(1)} %constant_dynamic-slice_fusion.2), channel_id=1, source_target_pairs={{0,1},{1,0},{2,3},{3,2},{4,5},{5,4},{6,7},{7,6},{8,9},{9,8},{10,11... | collective-permute-start | bytes 1050632 | tf_op jit(solution)/shard_map/ppermute | solution.py:107
  11.8 69.4 %collective-permute-start.5 = (bf16[384,2432]{1,0:T(8,128)(2,1)}, bf16[384,2432]{1,0:T(8,128)(2,1)}, u32[]{:S(2)}, u32[]{:S(2)}) collective-permute-start(bf16[384,2432]{1,0:T(8,128)(2,1)} %param.16), channel_id=1, source_target_pairs={{0,2},{2,0},{1,3},{3,1},{4,6},{6,4},{5,7},{7,5},{8,10},{10,8},{9,1... | collective-permute-start | bytes 5603336 | tf_op jit(solution)/shard_map/ppermute | solution.py:107
  17.1 5.9 %copy-start.10 = (bf16[1,32,2432]{2,1,0:T(8,128)(2,1)S(1)}, bf16[1,32,2432]{2,1,0:T(8,128)(2,1)}, u32[]{:S(2)}) copy-start(bf16[1,32,2432]{2,1,0:T(8,128)(2,1)} %param.17) | copy-start | bytes 466948
  18.1 41.3 %all-to-all-start = ((bf16[4,36,2432]{2,1,0:T(8,128)(2,1)}), bf16[4,36,2432]{2,1,0:T(8,128)(2,1)S(1)}, u32[]{:S(2)}, u32[]{:S(2)}) async-start(bf16[4,36,2432]{2,1,0:T(8,128)(2,1)} %pad_maximum_fusion), calls=%async_computation | async-start | bytes 1556480 | tf_op jit(solution)/shard_map/all_to_all | solution.py:179
  23.0 141.4 %all-gather.7.cloned.1.call-start = ((), (), s32[]{:S(2)}) async-start(), calls=%async_computation.3 | async-start | bytes 5603328 | tf_op jit(solution)/shard_map/all_gather | solution.py:207
  59.5 18.2 %collective-permute-start.1 = (bf16[144,2432]{1,0:T(8,128)(2,1)S(1)}, bf16[144,2432]{1,0:T(8,128)(2,1)S(1)}, u32[]{:S(2)}, u32[]{:S(2)}) collective-permute-start(bf16[144,2432]{1,0:T(8,128)(2,1)S(1)} %reshape.65), channel_id=1, source_target_pairs={{0,1},{1,0},{2,3},{3,2},{4,5},{5,4},{6,7},{7,6},{8,9},{9,8},{10,11... | collective-permute-start | bytes 2101256 | tf_op jit(solution)/shard_map/ppermute | solution.py:107
  59.6 18.1 %collective-permute-start.2 = (bf16[144,2432]{1,0:T(8,128)(2,1)S(1)}, bf16[144,2432]{1,0:T(8,128)(2,1)S(1)}, u32[]{:S(2)}, u32[]{:S(2)}) collective-permute-start(bf16[144,2432]{1,0:T(8,128)(2,1)S(1)} %reshape.65), channel_id=1, source_target_pairs={{0,2},{2,0},{1,3},{3,1},{4,6},{6,4},{5,7},{7,5},{8,10},{10,8},{9,1... | collective-permute-start | bytes 2101256 | tf_op jit(solution)/shard_map/ppermute | solution.py:107
  67.1 10.7 %copy-start.5 = (bf16[2432,384]{1,0:T(8,128)(2,1)S(1)}, bf16[2432,384]{1,0:T(8,128)(2,1)}, u32[]{:S(2)}) copy-start(bf16[2432,384]{1,0:T(8,128)(2,1)} %fusion.7) | copy-start | bytes 5603332
  77.7 2.2 %collective-permute-start.3 = (bf16[144,2432]{1,0:T(8,128)(2,1)S(1)}, bf16[144,2432]{1,0:T(8,128)(2,1)S(1)}, u32[]{:S(2)}, u32[]{:S(2)}) collective-permute-start(bf16[144,2432]{1,0:T(8,128)(2,1)S(1)} %collective-permute-done.2), channel_id=1, source_target_pairs={{0,1},{1,0},{2,3},{3,2},{4,5},{5,4},{6,7},{7,6},{8,9},{9,8},{10,11... | collective-permute-start | bytes 2101256 | tf_op jit(solution)/shard_map/ppermute | solution.py:107
  77.8 1.1 copy-start.7
  80.0 1.1 copy-start.8
  81.2 86.8 %all-gather.5.cloned.1.call-start = ((), (), s32[]{:S(2)}) async-start(), calls=%async_computation.2 | async-start | bytes 5603328 | tf_op jit(solution)/shard_map/all_gather | solution.py:206
  82.1 1.3 collective-permute-start.4
  103.1 4.4 %copy-start.4 = (bf16[2432,384]{1,0:T(8,128)(2,1)S(1)}, bf16[2432,384]{1,0:T(8,128)(2,1)}, u32[]{:S(2)}) copy-start(bf16[2432,384]{1,0:T(8,128)(2,1)} %fusion.9) | copy-start | bytes 5603332
  119.1 3.9 %copy-start.1 = (f32[6,576,660]{1,2,0:T(8,128)}, f32[6,576,660]{1,2,0:T(8,128)S(1)}, u32[]{:S(2)}) copy-start(f32[6,576,660]{1,2,0:T(8,128)S(1)} %get-tuple-element.36) | copy-start | bytes 27371524
  119.2 3.9 %copy-start.9 = (bf16[288,2432]{1,0:T(8,128)(2,1)S(1)}, bf16[288,2432]{1,0:T(8,128)(2,1)}, u32[]{:S(2)}) copy-start(bf16[288,2432]{1,0:T(8,128)(2,1)} %copy-done.8) | copy-start | bytes 4202500
  123.0 1.2 copy-start.12
  134.3 15.4 %all-to-all-start.1 = ((bf16[4,144,384]{2,1,0:T(8,128)(2,1)}), bf16[4,144,384]{2,1,0:T(8,128)(2,1)S(1)}, u32[]{:S(2)}, u32[]{:S(2)}) async-start(bf16[4,144,384]{2,1,0:T(8,128)(2,1)} %copy.42), calls=%async_computation.1 | async-start | bytes 884736 | tf_op jit(solution)/shard_map/all_to_all | solution.py:241
  149.7 1.5 collective-permute-start.6
  152.0 12.4 %collective-permute-start.7 = (bf16[2,144,768]{2,1,0:T(8,128)(2,1)S(1)}, bf16[2,144,768]{2,1,0:T(8,128)(2,1)}, u32[]{:S(2)}, u32[]{:S(2)}) collective-permute-start(bf16[2,144,768]{2,1,0:T(8,128)(2,1)S(1)} %pad_maximum_fusion.2), channel_id=1, source_target_pairs={{0,2},{2,0},{1,3},{3,1},{4,6},{6,4},{5,7},{7,5},{8,10},{10,8},{9,1... | collective-permute-start | bytes 1327112 | tf_op jit(solution)/shard_map/ppermute | solution.py:107
  (3 other events, 2.3 us)
Sparse Core Ops, SparseCore 0:
  81.3 12.9 all-gather.6
  95.8 14.1 all-gather.4

commit v3 on v2

--- a/solution.py
+++ b/solution.py
@@ -144,7 +144,9 @@
     for which in range(3):
         up_mine = jnp.where(owner[which] == at_seq, adapter_up_factors[0][:, which], up_mine)
     up_mine = lax.dynamic_slice_in_dim(up_mine, at_core * columns, columns, 1)
-    packed = jnp.concatenate([adapter_down_factors[0], up_mine], axis=1)
+    half_rank = up_mine.shape[0] // 2
+    down_mine = lax.dynamic_slice_in_dim(adapter_down_factors[0], at_core * half_rank, half_rank, 0)
+    packed = jnp.concatenate([down_mine, up_mine[:half_rank], up_mine[half_rank:]], axis=1)
     packed = lax.all_gather(packed, "seq", axis=0)
 
     length_row = jnp.broadcast_to(
@@ -152,8 +154,9 @@
         (samples, 2, 1, text_key_value.shape[3]),
     )
     text = swap_pair(jnp.concatenate([text_key_value, length_row], axis=2), 3, 0)
-    text = lax.all_gather(text, "seq", axis=0)
-    text = lax.dynamic_index_in_dim(text, at_seq, 1, keepdims=False)
+    text_shape = text.shape
+    text = text.reshape(n_seq, -1)
+    text_size = text.shape[1]
 
     away_weight = flip(frozen_output_weight, "mp")
 
@@ -176,17 +179,36 @@
     normed = (centred * lax.rsqrt(var + 1e-06) * (1.0 + scale) + shift).astype(jnp.bfloat16)
 
     piece = swap_pair(normed, 1, 0)
+    piece_rows = piece.shape[1]
+    extra = -(-text_size // width)
+    text = jnp.pad(text, ((0, 0), (0, extra * width - text_size))).reshape(n_seq, extra, width)
+    piece = jnp.concatenate([piece, text], axis=1)
     piece = lax.all_to_all(piece, "seq", 0, 0, tiled=True)
-    piece_rows = piece.shape[1]
+    text = piece[:, piece_rows:].reshape(n_seq, extra * width)[:, :text_size].reshape(text_shape)
+    piece = piece[:, :piece_rows]
     piece = piece.reshape(n_seq * piece_rows, width)
     piece_mp = flip(piece, "mp")
     piece_core = flip(piece, "batch")
     piece_both = flip(piece_mp, "batch")
     merged = []
+    chosen = jnp.stack(
+        [lax.dynamic_index_in_dim(packed, owner[which], 0, keepdims=False) for which in range(3)]
+    )
+    down_mine = chosen[:, :, :width]
+    down_came = flip(down_mine, "batch")
+    down_all = jnp.concatenate(
+        [
+            jnp.where(at_core == 0, down_mine, down_came),
+            jnp.where(at_core == 0, down_came, down_mine),
+        ],
+        axis=1,
+    )
+    up_all = jnp.concatenate(
+        [chosen[:, :, width : width + columns], chosen[:, :, width + columns :]], axis=1
+    )
     for which in range(3):
-        chosen = lax.dynamic_index_in_dim(packed, owner[which], 0, keepdims=False)
         delta = jnp.einsum(
-            "rd,rn->dn", chosen[:, :width], chosen[:, width:], preferred_element_type=jnp.float32
+            "rd,rn->dn", down_all[which], up_all[which], preferred_element_type=jnp.float32
         )
         merged.append(
             (frozen_query_key_value[:, which].astype(jnp.float32) + delta).astype(jnp.bfloat16)
@@ -242,6 +264,7 @@
     attn = swap_pair(attn, 0, 2)
     attn_away = flip(attn, "mp")
     proj = jnp.einsum("sin,nd->sid", attn, weight_here, preferred_element_type=jnp.float32)
+    proj = lax.optimization_barrier(proj)
     proj = proj + jnp.einsum(
         "sin,nd->sid", attn_away, weight_away, preferred_element_type=jnp.float32
     )
@@ -257,6 +280,7 @@
             and sizes["mp"] == 2
             and sizes["seq"] == 2 * image.shape[0]
             and image.shape[1] % 4 == 0
+            and arrays[7].shape[1] % 2 == 0
             and sizes["seq"] * text.shape[2] <= 256
         )
         return (body_by_sample if by_sample else body)(*arrays)

time: 181 us -> 165 us (0.912)
  blocking collectives: 43.5 us -> 14.9 us
  waiting for transfers between devices: 36.5 us -> 52.1 us
  matrix products: 42.9 us -> 36.7 us
  local copies, waits for them, and re-layouts: 13 us -> 15.5 us
    all_gather x1 -> x0, blocking collectives: 16.2 us -> none  [body_by_sample(): text = lax.all_gather(text, 'seq', axis=0)]
    all_to_all x1, waiting for transfers between devices: 0.01 us -> 13.4 us  [body_by_sample(): piece = lax.all_to_all(piece, 'seq', 0, 0, tiled=True)]
    all_gather x1, blocking collectives: 27.2 us -> 14.9 us  [body_by_sample(): packed = lax.all_gather(packed, 'seq', axis=0)]
    dot_general x1, matrix products: 6.79 us -> 2.73 us  [body_by_sample(): jnp.einsum('hin,nhe->ihe', expo.astype(jnp.bfloat16), values.reshape(-1,...]
    all_to_all x1, waiting for transfers between devices: 10.5 us -> 13.6 us  [body_by_sample(): lax.all_to_all(attn.reshape(n_seq, img_rows, columns), 'seq', 0, 0, tiled...]
    ppermute x8 -> x9, waiting for transfers between devices: 26 us -> 25.1 us  [flip(): return lax.ppermute(block, axis, [(0, 1), (1, 0)])]
    ppermute x8 -> x9, starting transfers between devices: 4.44 us -> 5.15 us  [flip(): return lax.ppermute(block, axis, [(0, 1), (1, 0)])]
  transfers between devices with their start and end apart: 12 -> 13, of which waited for: 6 -> 6; matrix products, arithmetic and copies ran while one was open for 28% -> 32% of each run, Pallas kernels for 0% -> 0%
where the time goes in v3:
time: 165 us; the launch traced here: 164 us
  waiting for transfers between devices  52.1 us (32%)
  matrix products  36.7 us (22%)
  between operations  22.2 us (13%)
  local copies, waits for them, and re-layouts  15.5 us (9%)
  blocking collectives  14.9 us (9%)
  starting transfers between devices  14 us (8%)
  other arithmetic  8.78 us (5%)
    ppermute x9, waiting for transfers between devices, flip(): return lax.ppermute(block, axis, [(0, 1), (1, 0)])  25.1 us
    all_gather x1, blocking collectives, body_by_sample(): packed = lax.all_gather(packed, 'seq', axis=0)  14.9 us
    all_to_all x1, waiting for transfers between devices, body_by_sample(): lax.all_to_all(attn.reshape(n_seq, img_rows, columns), 'seq', 0, 0, tiled...  13.6 us
    all_to_all x1, waiting for transfers between devices, body_by_sample(): piece = lax.all_to_all(piece, 'seq', 0, 0, tiled=True)  13.4 us
    dot_general x6, matrix products, body_by_sample(): jnp.dot(rows, m, preferred_element_type=jnp.float32).astype(jnp.bfloat16)  12.8 us
    dot_general x3, matrix products, body_by_sample(): jnp.einsum('rd,rn->dn', down_all[which], up_all[which], preferred_element...  10.3 us
    all_to_all x1, starting transfers between devices, body_by_sample(): piece = lax.all_to_all(piece, 'seq', 0, 0, tiled=True)  5.37 us
    ppermute x9, starting transfers between devices, flip(): return lax.ppermute(block, axis, [(0, 1), (1, 0)])  5.15 us
  transfers between devices with their start and end apart: 13, of which 6 were waited for; matrix products, arithmetic and copies ran while one was open for 32% of the time, Pallas kernels for 0%

profile of v3, /device:TPU:0, one launch (start us, length us, event | category | flops | bytes accessed | tf_op | source)
XLA Modules:
  0.0 164.2 jit_solution(1315177872261807872)
XLA Ops:
  6.6 3.0 %collective-permute-start.6 = (bf16[384,2432]{1,0:T(8,128)(2,1)}, bf16[384,2432]{1,0:T(8,128)(2,1)}, u32[]{:S(2)}, u32[]{:S(2)}) collective-permute-start(bf16[384,2432]{1,0:T(8,128)(2,1)} %param.16), channel_id=1, source_target_pairs={{0,2},{2,0},{1,3},{3,1},{4,6},{6,4},{5,7},{7,5},{8,10},{10,8},{9,1... | collective-permute-start | bytes 5603336 | tf_op jit(solution)/shard_map/ppermute | solution.py:107
  16.1 14.9 %all-gather = bf16[64,3200]{1,0:T(8,128)(2,1)S(1)} all-gather(bf16[16,3200]{1,0:T(8,128)(2,1)S(1)} %pad_maximum_fusion.6), channel_id=2, replica_groups=mesh['groups'=2,'seq'=4,'mp'=2,'batch'=2] {'seq'}, dimensions={0}, use_global_device_ids=true | all-gather | bytes 512000 | tf_op jit(solution)/shard_map/all_gather | solution.py:150
  39.9 5.4 %all-to-all-start = ((bf16[4,43,2432]{2,1,0:T(8,128)(2,1)}), bf16[4,43,2432]{2,1,0:T(8,128)(2,1)S(1)}, u32[]{:S(2)}, u32[]{:S(2)}) async-start(bf16[4,43,2432]{2,1,0:T(8,128)(2,1)} %pad_maximum_fusion), calls=%async_computation | async-start | bytes 1867776 | tf_op jit(solution)/shard_map/all_to_all | solution.py:186
  45.3 3.4 %fusion.8 = bf16[2432,384]{1,0:T(8,128)(2,1)} fusion(bf16[2432,3,384]{2,0,1:T(8,128)(2,1)} %param.15, bf16[3,16,2432]{2,1,0:T(8,128)(2,1)S(1)} %get-tuple-element.21, bf16[3,16,2432]{2,1,0:T(8,128)(2,1)S(1)} %get-tuple-element.22, bf16[3,32,384]{2,1,0:T(8,128)(2,1)S(1)} %fusion.46), kind=kOutput, calls=%fused_computation.12 | convolution fusion | flops 62881792 | bytes 4227072 | tf_op jit(solution)/shard_map/rd,rn->dn/dot_general | solution.py:210
  48.7 3.4 %fusion.7 = bf16[2432,384]{1,0:T(8,128)(2,1)} fusion(bf16[2432,3,384]{2,0,1:T(8,128)(2,1)} %param.15, bf16[3,16,2432]{2,1,0:T(8,128)(2,1)S(1)} %get-tuple-element.22, bf16[3,16,2432]{2,1,0:T(8,128)(2,1)S(1)} %get-tuple-element.21, bf16[3,32,384]{2,1,0:T(8,128)(2,1)S(1)} %fusion.46), kind=kOutput, calls=%fused_computation.11 | convolution fusion | flops 62881792 | bytes 4227072 | tf_op jit(solution)/shard_map/rd,rn->dn/dot_general | solution.py:210
  52.2 3.5 %fusion.6 = bf16[2432,384]{1,0:T(8,128)(2,1)} fusion(bf16[2432,3,384]{2,0,1:T(8,128)(2,1)} %param.15, bf16[3,16,2432]{2,1,0:T(8,128)(2,1)S(1)} %get-tuple-element.22, bf16[3,16,2432]{2,1,0:T(8,128)(2,1)S(1)} %get-tuple-element.21, bf16[3,32,384]{2,1,0:T(8,128)(2,1)S(1)} %fusion.46), kind=kOutput, calls=%fused_computation.10 | convolution fusion | flops 62881792 | bytes 4227072 | tf_op jit(solution)/shard_map/rd,rn->dn/dot_general | solution.py:210
  55.6 13.4 %all-to-all-done = bf16[4,43,2432]{2,1,0:T(8,128)(2,1)S(1)} async-done(((bf16[4,43,2432]{2,1,0:T(8,128)(2,1)}), bf16[4,43,2432]{2,1,0:T(8,128)(2,1)S(1)}, u32[]{:S(2)}, u32[]{:S(2)}) %all-to-all-start) | async-done | bytes 836640 | tf_op jit(solution)/shard_map/all_to_all | solution.py:186
  73.4 14.0 %collective-permute-done.4 = bf16[144,2432]{1,0:T(8,128)(2,1)S(1)} collective-permute-done((bf16[144,2432]{1,0:T(8,128)(2,1)S(1)}, bf16[144,2432]{1,0:T(8,128)(2,1)S(1)}, u32[]{:S(2)}, u32[]{:S(2)}) %collective-permute-start.4) | collective-permute-done | bytes 700448 | tf_op jit(solution)/shard_map/ppermute | solution.py:107
  88.6 3.0 %convolution_convert_fusion.1 = bf16[288,384]{1,0:T(8,128)(2,1)S(1)} fusion(bf16[288,2432]{1,0:T(8,128)(2,1)S(1)} %constant_dynamic-update-slice_fusion, bf16[2432,384]{1,0:T(8,128)(2,1)} %fusion.7), kind=kOutput, calls=%fused_computation.28 | convolution fusion | flops 538030080 | bytes 3489792 | tf_op jit(solution)/shard_map/dot_general | solution.py:221
  93.7 2.9 %convolution_convert_fusion.3 = bf16[288,384]{1,0:T(8,128)(2,1)S(1)} fusion(bf16[288,2432]{1,0:T(8,128)(2,1)} %copy-done.7, bf16[2432,384]{1,0:T(8,128)(2,1)} %fusion.6), kind=kOutput, calls=%fused_computation.30 | convolution fusion | flops 538030080 | bytes 3489792 | tf_op jit(solution)/shard_map/dot_general | solution.py:221
  96.6 1.3 constant_dynamic-update-slice_fusion.2
  100.9 2.9 %convolution_convert_fusion.2 = bf16[288,384]{1,0:T(8,128)(2,1)S(1)} fusion(bf16[288,2432]{1,0:T(8,128)(2,1)} %copy-done.8, bf16[2432,384]{1,0:T(8,128)(2,1)} %fusion.6), kind=kOutput, calls=%fused_computation.29 | convolution fusion | flops 538030080 | bytes 3489792 | tf_op jit(solution)/shard_map/dot_general | solution.py:221
  104.1 2.3 %convolution_convert_fusion.4 = bf16[288,384]{1,0:T(8,128)(2,1)S(1)} fusion(bf16[288,2432]{1,0:T(8,128)(2,1)} %copy-done.8, bf16[2432,384]{1,0:T(8,128)(2,1)S(1)} %copy-done.4), kind=kOutput, calls=%fused_computation.31 | convolution fusion | flops 538030080 | bytes 3489792 | tf_op jit(solution)/shard_map/dot_general | solution.py:221
  107.4 3.4 %fusion = (f32[6,576]{1,0:T(8,128)S(1)}, f32[6,576,660]{1,2,0:T(8,128)S(1)}) fusion(pred[660]{0:T(1024)(128)(4,1)S(1)} %iota_compare_fusion, bf16[576,6,64]{0,2,1:T(8,128)(2,1)S(1)} %bitcast.89, bf16[84,6,64]{0,2,1:T(8,128)(2,1)S(1)} %copy-done.12, bf16[288,6,64]{0,2,1:T(8,128)(2,1)S(1)} %bitcast.92, bf16[288,6,64]{0,2,1:T(8,128)(2,1)S(1)} %bitcast.91), kind=kOutput, calls=%fused_computation.2 | convolution fusion | flops 300322944 | bytes 10087572 | tf_op jit(solution)/shard_map/ihe,nhe->hin/dot_general | solution.py:239
  110.8 2.5 %fusion.1 = f32[6,576]{1,0:T(8,128)S(1)} fusion(f32[6,576,660]{1,2,0:T(8,128)S(1)} %get-tuple-element.40, f32[6,576]{1,0:T(8,128)S(1)} %get-tuple-element.39, pred[660]{0:T(1024)(128)(4,1)S(1)} %iota_compare_fusion), kind=kLoop, calls=%fused_computation.3 | loop fusion | flops 9120384 | bytes 9152148 | tf_op jit(solution)/shard_map/reduce_sum | solution.py:250
  113.3 2.7 %divide_convert_fusion = bf16[576,6,64]{0,2,1:T(8,128)(2,1)S(1)} fusion(f32[6,576,660]{1,2,0:T(8,128)S(1)} %get-tuple-element.40, f32[6,576]{1,0:T(8,128)S(1)} %get-tuple-element.39, pred[660]{0:T(1024)(128)(4,1)S(1)} %iota_compare_fusion, bf16[84,6,64]{0,2,1:T(8,128)(2,1)S(1)} %copy-done.13, bf16[288,6,64]{0,2,1:T(8,128)(2,1)S(1)} %bitcast.93, ...), kind=kOutput, calls=%fused_computation.33 | convolution fusion | flops 303049728 | bytes 10101396 | tf_op jit(solution)/shard_map/hin,nhe->ihe/dot_general | solution.py:251
  116.1 1.3 copy.39
  119.3 3.5 %all-to-all-start.1 = ((bf16[4,144,384]{2,1,0:T(8,128)(2,1)}), bf16[4,144,384]{2,1,0:T(8,128)(2,1)S(1)}, u32[]{:S(2)}, u32[]{:S(2)}) async-start(bf16[4,144,384]{2,1,0:T(8,128)(2,1)} %copy.41), calls=%async_computation.1 | async-start | bytes 884736 | tf_op jit(solution)/shard_map/all_to_all | solution.py:263
  122.8 13.6 %all-to-all-done.1 = bf16[4,144,384]{2,1,0:T(8,128)(2,1)S(1)} async-done(((bf16[4,144,384]{2,1,0:T(8,128)(2,1)}), bf16[4,144,384]{2,1,0:T(8,128)(2,1)S(1)}, u32[]{:S(2)}, u32[]{:S(2)}) %all-to-all-start.1) | async-done | bytes 442400 | tf_op jit(solution)/shard_map/all_to_all | solution.py:263
  136.5 1.5 collective-permute-done.7
  140.2 3.5 %fusion.11 = f32[2,144,2432]{2,1,0:T(8,128)S(1)} fusion(bf16[768,2432]{1,0:T(8,128)(2,1)} %all-gather.4.cloned.1.call-done, bf16[2,144,384]{2,1,0:T(8,128)(2,1)} %copy-done.3, bf16[2,144,384]{2,1,0:T(8,128)(2,1)S(1)} %get-tuple-element.19), kind=kOutput, calls=%fused_computation.15 | convolution fusion | flops 1076723712 | bytes 6979584 | tf_op jit(solution)/shard_map/sin,nd->sid/dot_general | solution.py:266
  143.7 8.4 %collective-permute-done.8 = bf16[2,144,768]{2,1,0:T(8,128)(2,1)} collective-permute-done((bf16[2,144,768]{2,1,0:T(8,128)(2,1)}, bf16[2,144,768]{2,1,0:T(8,128)(2,1)}, u32[]{:S(2)}, u32[]{:S(2)}) %collective-permute-start.8) | collective-permute-done | bytes 442400 | tf_op jit(solution)/shard_map/ppermute | solution.py:107
  152.1 3.6 %fusion.9 = f32[2,144,2432]{2,1,0:T(8,128)S(1)} fusion(bf16[2,144,768]{2,1,0:T(8,128)(2,1)} %collective-permute-done.8, bf16[768,2432]{1,0:T(8,128)(2,1)} %all-gather.6.cloned.1.call-done), kind=kOutput, calls=%fused_computation.13 | convolution fusion | flops 1075838976 | bytes 6979584 | tf_op jit(solution)/shard_map/sin,nd->sid/dot_general | solution.py:268
  155.7 1.6 add_convert_fusion
  (121 shorter events, 23.2 us)
Async XLA Ops:
  6.5 27.7 %copy-start = (f32[10,3,2432]{2,1,0:T(4,128)S(1)}, f32[10,3,2432]{2,1,0:T(4,128)}, u32[]{:S(2)}) copy-start(f32[10,3,2432]{2,1,0:T(4,128)} %param.13) | copy-start | bytes 875524
  6.5 3.1 %copy-start.16 = (s32[3]{0:T(128)S(1)}, s32[3]{0:T(128)}, u32[]{:S(2)}) copy-start(s32[3]{0:T(128)} %param.19) | copy-start | bytes 40
  6.5 9.4 %copy-start.11 = (bf16[1,32,3,768]{3,1,2,0:T(8,128)(2,1)S(1)}, bf16[1,32,3,768]{3,1,2,0:T(8,128)(2,1)}, u32[]{:S(2)}) copy-start(bf16[1,32,3,768]{3,1,2,0:T(8,128)(2,1)} %param.18) | copy-start | bytes 442372
  6.5 9.5 %copy-start.15 = (bf16[1,32,2432]{2,1,0:T(8,128)(2,1)S(1)}, bf16[1,32,2432]{2,1,0:T(8,128)(2,1)}, u32[]{:S(2)}) copy-start(bf16[1,32,2432]{2,1,0:T(8,128)(2,1)} %param.17) | copy-start | bytes 466948
  6.5 133.6 %all-gather.4.cloned.1.call-start = ((), (), s32[]{:S(2)}) async-start(), calls=%async_computation.2 | async-start | bytes 5603328 | tf_op jit(solution)/shard_map/all_gather | solution.py:228
  6.6 97.2 %collective-permute-start.6 = (bf16[384,2432]{1,0:T(8,128)(2,1)}, bf16[384,2432]{1,0:T(8,128)(2,1)}, u32[]{:S(2)}, u32[]{:S(2)}) collective-permute-start(bf16[384,2432]{1,0:T(8,128)(2,1)} %param.16), channel_id=1, source_target_pairs={{0,2},{2,0},{1,3},{3,1},{4,6},{6,4},{5,7},{7,5},{8,10},{10,8},{9,1... | collective-permute-start | bytes 5603336 | tf_op jit(solution)/shard_map/ppermute | solution.py:107
  9.6 24.0 %copy-start.1 = (bf16[2,144,2432]{2,1,0:T(8,128)(2,1)S(1)}, bf16[2,144,2432]{2,1,0:T(8,128)(2,1)}, u32[]{:S(2)}) copy-start(bf16[2,144,2432]{2,1,0:T(8,128)(2,1)} %param.10) | copy-start | bytes 4202500
  16.1 18.2 %copy-start.17 = (s32[2]{0:T(128)S(1)}, s32[2]{0:T(128)}, u32[]{:S(2)}) copy-start(s32[2]{0:T(128)} %param.11) | copy-start | bytes 28
  33.6 11.6 %collective-permute-start.3 = (bf16[3,16,2432]{2,1,0:T(8,128)(2,1)}, bf16[3,16,2432]{2,1,0:T(8,128)(2,1)S(1)}, u32[]{:S(2)}, u32[]{:S(2)}) collective-permute-start(bf16[3,16,2432]{2,1,0:T(8,128)(2,1)} %slice.136), channel_id=1, source_target_pairs={{0,1},{1,0},{2,3},{3,2},{4,5},{5,4},{6,7},{7,6},{8,9},{9,8},{10,11... | collective-permute-start | bytes 700424 | tf_op jit(solution)/shard_map/ppermute | solution.py:107
  33.8 2.7 %copy-start.6 = (bf16[2,2,21,768]{3,1,2,0:T(2,128)(2,1)S(1)}, bf16[2,2,21,768]{3,1,2,0:T(2,128)(2,1)}, u32[]{:S(2)}) copy-start(bf16[2,2,21,768]{3,1,2,0:T(2,128)(2,1)} %param.14) | copy-start | bytes 387076
  35.9 2.7 %collective-permute-start = (bf16[2,36,2432]{2,1,0:T(8,128)(2,1)S(1)}, bf16[2,36,2432]{2,1,0:T(8,128)(2,1)S(1)}, u32[]{:S(2)}, u32[]{:S(2)}) collective-permute-start(bf16[2,36,2432]{2,1,0:T(8,128)(2,1)S(1)} %constant_dynamic-slice_fusion.4), channel_id=1, source_target_pairs={{0,1},{1,0},{2,3},{3,2},{4,5},{5,4},{6,7},{7,6},{8,9},{9,8},{10,11... | collective-permute-start | bytes 1050632 | tf_op jit(solution)/shard_map/ppermute | solution.py:107
  36.6 1.3 collective-permute-start.1
  39.9 29.1 %all-to-all-start = ((bf16[4,43,2432]{2,1,0:T(8,128)(2,1)}), bf16[4,43,2432]{2,1,0:T(8,128)(2,1)S(1)}, u32[]{:S(2)}, u32[]{:S(2)}) async-start(bf16[4,43,2432]{2,1,0:T(8,128)(2,1)} %pad_maximum_fusion), calls=%async_computation | async-start | bytes 1867776 | tf_op jit(solution)/shard_map/all_to_all | solution.py:186
  45.2 106.8 %all-gather.6.cloned.1.call-start = ((), (), s32[]{:S(2)}) async-start(), calls=%async_computation.3 | async-start | bytes 5603328 | tf_op jit(solution)/shard_map/all_gather | solution.py:229
  69.2 18.2 %collective-permute-start.2 = (bf16[144,2432]{1,0:T(8,128)(2,1)S(1)}, bf16[144,2432]{1,0:T(8,128)(2,1)}, u32[]{:S(2)}, u32[]{:S(2)}) collective-permute-start(bf16[144,2432]{1,0:T(8,128)(2,1)S(1)} %reshape.82), channel_id=1, source_target_pairs={{0,1},{1,0},{2,3},{3,2},{4,5},{5,4},{6,7},{7,6},{8,9},{9,8},{10,11... | collective-permute-start | bytes 2101256 | tf_op jit(solution)/shard_map/ppermute | solution.py:107
  69.3 18.1 %collective-permute-start.4 = (bf16[144,2432]{1,0:T(8,128)(2,1)S(1)}, bf16[144,2432]{1,0:T(8,128)(2,1)S(1)}, u32[]{:S(2)}, u32[]{:S(2)}) collective-permute-start(bf16[144,2432]{1,0:T(8,128)(2,1)S(1)} %reshape.82), channel_id=1, source_target_pairs={{0,2},{2,0},{1,3},{3,1},{4,6},{6,4},{5,7},{7,5},{8,10},{10,8},{9,1... | collective-permute-start | bytes 2101256 | tf_op jit(solution)/shard_map/ppermute | solution.py:107
  87.4 9.2 %collective-permute-start.5 = (bf16[144,2432]{1,0:T(8,128)(2,1)S(1)}, bf16[144,2432]{1,0:T(8,128)(2,1)}, u32[]{:S(2)}, u32[]{:S(2)}) collective-permute-start(bf16[144,2432]{1,0:T(8,128)(2,1)S(1)} %collective-permute-done.4), channel_id=1, source_target_pairs={{0,1},{1,0},{2,3},{3,2},{4,5},{5,4},{6,7},{7,6},{8,9},{9,8},{10,11... | collective-permute-start | bytes 2101256 | tf_op jit(solution)/shard_map/ppermute | solution.py:107
  88.6 3.0 %copy-start.7 = (bf16[288,2432]{1,0:T(8,128)(2,1)}, bf16[288,2432]{1,0:T(8,128)(2,1)S(1)}, u32[]{:S(2)}) copy-start(bf16[288,2432]{1,0:T(8,128)(2,1)S(1)} %constant_dynamic-update-slice_fusion) | copy-start | bytes 4202500
  88.6 3.0 %copy-start.4 = (bf16[2432,384]{1,0:T(8,128)(2,1)S(1)}, bf16[2432,384]{1,0:T(8,128)(2,1)}, u32[]{:S(2)}) copy-start(bf16[2432,384]{1,0:T(8,128)(2,1)} %fusion.8) | copy-start | bytes 5603332
  119.3 17.1 %all-to-all-start.1 = ((bf16[4,144,384]{2,1,0:T(8,128)(2,1)}), bf16[4,144,384]{2,1,0:T(8,128)(2,1)S(1)}, u32[]{:S(2)}, u32[]{:S(2)}) async-start(bf16[4,144,384]{2,1,0:T(8,128)(2,1)} %copy.41), calls=%async_computation.1 | async-start | bytes 884736 | tf_op jit(solution)/shard_map/all_to_all | solution.py:263
  136.4 1.5 collective-permute-start.7
  139.5 12.5 %collective-permute-start.8 = (bf16[2,144,768]{2,1,0:T(8,128)(2,1)}, bf16[2,144,768]{2,1,0:T(8,128)(2,1)}, u32[]{:S(2)}, u32[]{:S(2)}) collective-permute-start(bf16[2,144,768]{2,1,0:T(8,128)(2,1)} %pad_maximum_fusion.2), channel_id=1, source_target_pairs={{0,2},{2,0},{1,3},{3,1},{4,6},{6,4},{5,7},{7,5},{8,10},{10,8},{9,1... | collective-permute-start | bytes 1327112 | tf_op jit(solution)/shard_map/ppermute | solution.py:107
  143.7 12.0 %copy-start.14 = (f32[2,2432]{1,0:T(2,128)S(1)}, f32[2,2432]{1,0:T(2,128)}, u32[]{:S(2)}) copy-start(f32[2,2432]{1,0:T(2,128)} %get-tuple-element.31) | copy-start | bytes 58372
  152.1 3.6 %copy-start.2 = (bf16[2,144,2432]{2,1,0:T(8,128)(2,1)S(1)}, bf16[2,144,2432]{2,1,0:T(8,128)(2,1)}, u32[]{:S(2)}) copy-start(bf16[2,144,2432]{2,1,0:T(8,128)(2,1)} %param.10) | copy-start | bytes 4202500
  (8 other events, 12.5 us)
Sparse Core Ops, SparseCore 0:
  9.7 14.8 all-gather.3
  106.7 11.3 all-gather.5

commit v4 on v3

--- a/solution.py
+++ b/solution.py
@@ -221,6 +221,7 @@
         [jnp.dot(rows, m, preferred_element_type=jnp.float32).astype(jnp.bfloat16) for m in merged]
         for rows in (early, late)
     ]
+    halves[0] = lax.optimization_barrier(halves[0])
     for which in range(3):
         triple.append(jnp.concatenate([halves[0][which], halves[1][which]], axis=0))
     queries, keys, values = triple

time: 165 us -> 163 us (0.988)
  matrix products: 36.7 us -> 33.4 us
  local copies, waits for them, and re-layouts: 15.5 us -> 18 us
    dot_general x6, matrix products: 12.8 us -> 9.53 us  [body_by_sample(): jnp.dot(rows, m, preferred_element_type=jnp.float32).astype(jnp.bfloat16)]
    optimization_barrier x0 -> x2, local copies, waits for them, and re-layouts: none -> 1.8 us  [body_by_sample(): halves[0] = lax.optimization_barrier(halves[0])]
    unnamed x42 -> x44, local copies, waits for them, and re-layouts: 2.85 us -> 4.42 us
where the time goes in v4:
time: 163 us
  waiting for transfers between devices  51.4 us (32%)
  matrix products  33.4 us (20%)
  between operations  22.4 us (14%)
  local copies, waits for them, and re-layouts  18 us (11%)
  blocking collectives  14.9 us (9%)
  starting transfers between devices  14 us (9%)
  other arithmetic  8.77 us (5%)
    ppermute x9, waiting for transfers between devices, flip(): return lax.ppermute(block, axis, [(0, 1), (1, 0)])  24.4 us
    all_gather x1, blocking collectives, body_by_sample(): packed = lax.all_gather(packed, 'seq', axis=0)  14.9 us
    all_to_all x1, waiting for transfers between devices, body_by_sample(): lax.all_to_all(attn.reshape(n_seq, img_rows, columns), 'seq', 0, 0, tiled...  13.6 us
    all_to_all x1, waiting for transfers between devices, body_by_sample(): piece = lax.all_to_all(piece, 'seq', 0, 0, tiled=True)  13.4 us
    dot_general x3, matrix products, body_by_sample(): jnp.einsum('rd,rn->dn', down_all[which], up_all[which], preferred_element...  10.3 us
    dot_general x6, matrix products, body_by_sample(): jnp.dot(rows, m, preferred_element_type=jnp.float32).astype(jnp.bfloat16)  9.53 us
    all_to_all x1, starting transfers between devices, body_by_sample(): piece = lax.all_to_all(piece, 'seq', 0, 0, tiled=True)  5.37 us
    ppermute x9, starting transfers between devices, flip(): return lax.ppermute(block, axis, [(0, 1), (1, 0)])  5.09 us
  transfers between devices with their start and end apart: 13, of which 6 were waited for; matrix products, arithmetic and copies ran while one was open for 32% of the time, Pallas kernels for 0%

profile of v4, /device:TPU:0, one launch (start us, length us, event | category | flops | bytes accessed | tf_op | source)
XLA Modules:
  0.0 162.8 jit_solution(611430676812007817)
XLA Ops:
  6.6 3.0 %collective-permute-start.6 = (bf16[384,2432]{1,0:T(8,128)(2,1)}, bf16[384,2432]{1,0:T(8,128)(2,1)}, u32[]{:S(2)}, u32[]{:S(2)}) collective-permute-start(bf16[384,2432]{1,0:T(8,128)(2,1)} %param.16), channel_id=1, source_target_pairs={{0,2},{2,0},{1,3},{3,1},{4,6},{6,4},{5,7},{7,5},{8,10},{10,8},{9,1... | collective-permute-start | bytes 5603336 | tf_op jit(solution)/shard_map/ppermute | solution.py:107
  16.1 14.9 %all-gather = bf16[64,3200]{1,0:T(8,128)(2,1)S(1)} all-gather(bf16[16,3200]{1,0:T(8,128)(2,1)S(1)} %pad_maximum_fusion.6), channel_id=2, replica_groups=mesh['groups'=2,'seq'=4,'mp'=2,'batch'=2] {'seq'}, dimensions={0}, use_global_device_ids=true | all-gather | bytes 512000 | tf_op jit(solution)/shard_map/all_gather | solution.py:150
  36.8 1.2 collective-permute-done.1
  39.9 5.4 %all-to-all-start = ((bf16[4,43,2432]{2,1,0:T(8,128)(2,1)}), bf16[4,43,2432]{2,1,0:T(8,128)(2,1)S(1)}, u32[]{:S(2)}, u32[]{:S(2)}) async-start(bf16[4,43,2432]{2,1,0:T(8,128)(2,1)} %pad_maximum_fusion), calls=%async_computation | async-start | bytes 1867776 | tf_op jit(solution)/shard_map/all_to_all | solution.py:186
  45.4 3.4 %fusion.8 = bf16[2432,384]{1,0:T(8,128)(2,1)} fusion(bf16[2432,3,384]{2,0,1:T(8,128)(2,1)} %param.15, bf16[3,16,2432]{2,1,0:T(8,128)(2,1)S(1)} %get-tuple-element.27, bf16[3,16,2432]{2,1,0:T(8,128)(2,1)S(1)} %get-tuple-element.28, bf16[3,32,384]{2,1,0:T(8,128)(2,1)S(1)} %fusion.46), kind=kOutput, calls=%fused_computation.12 | convolution fusion | flops 62881792 | bytes 4227072 | tf_op jit(solution)/shard_map/rd,rn->dn/dot_general | solution.py:210
  48.8 3.4 %fusion.7 = bf16[2432,384]{1,0:T(8,128)(2,1)} fusion(bf16[2432,3,384]{2,0,1:T(8,128)(2,1)} %param.15, bf16[3,16,2432]{2,1,0:T(8,128)(2,1)S(1)} %get-tuple-element.28, bf16[3,16,2432]{2,1,0:T(8,128)(2,1)S(1)} %get-tuple-element.27, bf16[3,32,384]{2,1,0:T(8,128)(2,1)S(1)} %fusion.46), kind=kOutput, calls=%fused_computation.11 | convolution fusion | flops 62881792 | bytes 4227072 | tf_op jit(solution)/shard_map/rd,rn->dn/dot_general | solution.py:210
  52.2 3.4 %fusion.6 = bf16[2432,384]{1,0:T(8,128)(2,1)} fusion(bf16[2432,3,384]{2,0,1:T(8,128)(2,1)} %param.15, bf16[3,16,2432]{2,1,0:T(8,128)(2,1)S(1)} %get-tuple-element.28, bf16[3,16,2432]{2,1,0:T(8,128)(2,1)S(1)} %get-tuple-element.27, bf16[3,32,384]{2,1,0:T(8,128)(2,1)S(1)} %fusion.46), kind=kOutput, calls=%fused_computation.10 | convolution fusion | flops 62881792 | bytes 4227072 | tf_op jit(solution)/shard_map/rd,rn->dn/dot_general | solution.py:210
  55.7 13.4 %all-to-all-done = bf16[4,43,2432]{2,1,0:T(8,128)(2,1)S(1)} async-done(((bf16[4,43,2432]{2,1,0:T(8,128)(2,1)}), bf16[4,43,2432]{2,1,0:T(8,128)(2,1)S(1)}, u32[]{:S(2)}, u32[]{:S(2)}) %all-to-all-start) | async-done | bytes 836640 | tf_op jit(solution)/shard_map/all_to_all | solution.py:186
  73.0 13.3 %collective-permute-done.4 = bf16[144,2432]{1,0:T(8,128)(2,1)} collective-permute-done((bf16[144,2432]{1,0:T(8,128)(2,1)S(1)}, bf16[144,2432]{1,0:T(8,128)(2,1)}, u32[]{:S(2)}, u32[]{:S(2)}) %collective-permute-start.4) | collective-permute-done | bytes 700448 | tf_op jit(solution)/shard_map/ppermute | solution.py:107
  93.2 1.3 constant_dynamic-update-slice_fusion.3
  98.6 2.9 %convolution_convert_fusion.1 = bf16[288,384]{1,0:T(8,128)(2,1)S(1)} fusion(bf16[288,2432]{1,0:T(8,128)(2,1)} %copy-done.9, bf16[2432,384]{1,0:T(8,128)(2,1)} %fusion.6), kind=kOutput, calls=%fused_computation.28 | convolution fusion | flops 538030080 | bytes 3489792 | tf_op jit(solution)/shard_map/dot_general | solution.py:221
  101.8 3.0 %convolution_convert_fusion.2 = bf16[288,384]{1,0:T(8,128)(2,1)} fusion(bf16[288,2432]{1,0:T(8,128)(2,1)} %copy-done.9, bf16[2432,384]{1,0:T(8,128)(2,1)S(1)} %copy-done.4), kind=kOutput, calls=%fused_computation.29 | convolution fusion | flops 538030080 | bytes 3489792 | tf_op jit(solution)/shard_map/dot_general | solution.py:221
  104.8 1.2 copy.33
  106.1 3.4 %fusion = (f32[6,576]{1,0:T(8,128)S(1)}, f32[6,576,660]{1,2,0:T(8,128)S(1)}) fusion(pred[660]{0:T(1024)(128)(4,1)S(1)} %iota_compare_fusion, bf16[576,6,64]{0,2,1:T(8,128)(2,1)S(1)} %bitcast.89, bf16[84,6,64]{0,2,1:T(8,128)(2,1)S(1)} %copy.38, bf16[288,6,64]{0,2,1:T(8,128)(2,1)S(1)} %bitcast.92, bf16[288,6,64]{0,2,1:T(8,128)(2,1)S(1)} %bitcast.91), kind=kOutput, calls=%fused_computation.2 | convolution fusion | flops 300322944 | bytes 10087572 | tf_op jit(solution)/shard_map/ihe,nhe->hin/dot_general | solution.py:240
  109.5 2.5 %fusion.1 = f32[6,576]{1,0:T(8,128)S(1)} fusion(f32[6,576,660]{1,2,0:T(8,128)S(1)} %get-tuple-element.46, f32[6,576]{1,0:T(8,128)S(1)} %get-tuple-element.45, pred[660]{0:T(1024)(128)(4,1)S(1)} %iota_compare_fusion), kind=kLoop, calls=%fused_computation.3 | loop fusion | flops 9120384 | bytes 9152148 | tf_op jit(solution)/shard_map/reduce_sum | solution.py:251
  112.0 2.7 %divide_convert_fusion = bf16[576,6,64]{0,2,1:T(8,128)(2,1)S(1)} fusion(f32[6,576,660]{1,2,0:T(8,128)S(1)} %get-tuple-element.46, f32[6,576]{1,0:T(8,128)S(1)} %get-tuple-element.45, pred[660]{0:T(1024)(128)(4,1)S(1)} %iota_compare_fusion, bf16[84,6,64]{0,2,1:T(8,128)(2,1)S(1)} %copy-done.14, bf16[288,6,64]{0,2,1:T(8,128)(2,1)S(1)} %bitcast.93, ...), kind=kOutput, calls=%fused_computation.33 | convolution fusion | flops 303049728 | bytes 10101396 | tf_op jit(solution)/shard_map/hin,nhe->ihe/dot_general | solution.py:252
  114.7 1.3 copy.39
  117.9 3.5 %all-to-all-start.1 = ((bf16[4,144,384]{2,1,0:T(8,128)(2,1)}), bf16[4,144,384]{2,1,0:T(8,128)(2,1)S(1)}, u32[]{:S(2)}, u32[]{:S(2)}) async-start(bf16[4,144,384]{2,1,0:T(8,128)(2,1)} %copy.41), calls=%async_computation.1 | async-start | bytes 884736 | tf_op jit(solution)/shard_map/all_to_all | solution.py:264
  121.4 13.6 %all-to-all-done.1 = bf16[4,144,384]{2,1,0:T(8,128)(2,1)S(1)} async-done(((bf16[4,144,384]{2,1,0:T(8,128)(2,1)}), bf16[4,144,384]{2,1,0:T(8,128)(2,1)S(1)}, u32[]{:S(2)}, u32[]{:S(2)}) %all-to-all-start.1) | async-done | bytes 442400 | tf_op jit(solution)/shard_map/all_to_all | solution.py:264
  135.2 1.5 collective-permute-done.7
  138.8 3.5 %fusion.11 = f32[2,144,2432]{2,1,0:T(8,128)S(1)} fusion(bf16[768,2432]{1,0:T(8,128)(2,1)} %all-gather.4.cloned.1.call-done, bf16[2,144,384]{2,1,0:T(8,128)(2,1)} %copy-done.3, bf16[2,144,384]{2,1,0:T(8,128)(2,1)S(1)} %get-tuple-element.25), kind=kOutput, calls=%fused_computation.15 | convolution fusion | flops 1076723712 | bytes 6979584 | tf_op jit(solution)/shard_map/sin,nd->sid/dot_general | solution.py:267
  142.3 8.4 %collective-permute-done.8 = bf16[2,144,768]{2,1,0:T(8,128)(2,1)} collective-permute-done((bf16[2,144,768]{2,1,0:T(8,128)(2,1)}, bf16[2,144,768]{2,1,0:T(8,128)(2,1)}, u32[]{:S(2)}, u32[]{:S(2)}) %collective-permute-start.8) | collective-permute-done | bytes 442400 | tf_op jit(solution)/shard_map/ppermute | solution.py:107
  150.7 3.6 %fusion.9 = f32[2,144,2432]{2,1,0:T(8,128)S(1)} fusion(bf16[2,144,768]{2,1,0:T(8,128)(2,1)} %collective-permute-done.8, bf16[768,2432]{1,0:T(8,128)(2,1)} %all-gather.6.cloned.1.call-done), kind=kOutput, calls=%fused_computation.13 | convolution fusion | flops 1075838976 | bytes 6979584 | tf_op jit(solution)/shard_map/sin,nd->sid/dot_general | solution.py:269
  154.3 1.6 add_convert_fusion
  (123 shorter events, 25.0 us)
Async XLA Ops:
  6.5 27.7 %copy-start = (f32[10,3,2432]{2,1,0:T(4,128)S(1)}, f32[10,3,2432]{2,1,0:T(4,128)}, u32[]{:S(2)}) copy-start(f32[10,3,2432]{2,1,0:T(4,128)} %param.13) | copy-start | bytes 875524
  6.5 3.1 %copy-start.17 = (s32[3]{0:T(128)S(1)}, s32[3]{0:T(128)}, u32[]{:S(2)}) copy-start(s32[3]{0:T(128)} %param.19) | copy-start | bytes 40
  6.5 9.5 %copy-start.13 = (bf16[1,32,3,768]{3,1,2,0:T(8,128)(2,1)S(1)}, bf16[1,32,3,768]{3,1,2,0:T(8,128)(2,1)}, u32[]{:S(2)}) copy-start(bf16[1,32,3,768]{3,1,2,0:T(8,128)(2,1)} %param.18) | copy-start | bytes 442372
  6.5 9.5 %copy-start.16 = (bf16[1,32,2432]{2,1,0:T(8,128)(2,1)S(1)}, bf16[1,32,2432]{2,1,0:T(8,128)(2,1)}, u32[]{:S(2)}) copy-start(bf16[1,32,2432]{2,1,0:T(8,128)(2,1)} %param.17) | copy-start | bytes 466948
  6.5 132.3 %all-gather.4.cloned.1.call-start = ((), (), s32[]{:S(2)}) async-start(), calls=%async_computation.2 | async-start | bytes 5603328 | tf_op jit(solution)/shard_map/all_gather | solution.py:229
  6.6 95.0 %collective-permute-start.6 = (bf16[384,2432]{1,0:T(8,128)(2,1)}, bf16[384,2432]{1,0:T(8,128)(2,1)}, u32[]{:S(2)}, u32[]{:S(2)}) collective-permute-start(bf16[384,2432]{1,0:T(8,128)(2,1)} %param.16), channel_id=1, source_target_pairs={{0,2},{2,0},{1,3},{3,1},{4,6},{6,4},{5,7},{7,5},{8,10},{10,8},{9,1... | collective-permute-start | bytes 5603336 | tf_op jit(solution)/shard_map/ppermute | solution.py:107
  9.6 24.1 %copy-start.1 = (bf16[2,144,2432]{2,1,0:T(8,128)(2,1)S(1)}, bf16[2,144,2432]{2,1,0:T(8,128)(2,1)}, u32[]{:S(2)}) copy-start(bf16[2,144,2432]{2,1,0:T(8,128)(2,1)} %param.10) | copy-start | bytes 4202500
  16.1 18.2 %copy-start.18 = (s32[2]{0:T(128)S(1)}, s32[2]{0:T(128)}, u32[]{:S(2)}) copy-start(s32[2]{0:T(128)} %param.11) | copy-start | bytes 28
  33.7 11.6 %collective-permute-start.3 = (bf16[3,16,2432]{2,1,0:T(8,128)(2,1)}, bf16[3,16,2432]{2,1,0:T(8,128)(2,1)S(1)}, u32[]{:S(2)}, u32[]{:S(2)}) collective-permute-start(bf16[3,16,2432]{2,1,0:T(8,128)(2,1)} %slice.136), channel_id=1, source_target_pairs={{0,1},{1,0},{2,3},{3,2},{4,5},{5,4},{6,7},{7,6},{8,9},{9,8},{10,11... | collective-permute-start | bytes 700424 | tf_op jit(solution)/shard_map/ppermute | solution.py:107
  33.9 2.7 %copy-start.8 = (bf16[2,2,21,768]{3,1,2,0:T(2,128)(2,1)S(1)}, bf16[2,2,21,768]{3,1,2,0:T(2,128)(2,1)}, u32[]{:S(2)}) copy-start(bf16[2,2,21,768]{3,1,2,0:T(2,128)(2,1)} %param.14) | copy-start | bytes 387076
  35.9 2.7 %collective-permute-start = (bf16[2,36,2432]{2,1,0:T(8,128)(2,1)S(1)}, bf16[2,36,2432]{2,1,0:T(8,128)(2,1)S(1)}, u32[]{:S(2)}, u32[]{:S(2)}) collective-permute-start(bf16[2,36,2432]{2,1,0:T(8,128)(2,1)S(1)} %constant_dynamic-slice_fusion.4), channel_id=1, source_target_pairs={{0,1},{1,0},{2,3},{3,2},{4,5},{5,4},{6,7},{7,6},{8,9},{9,8},{10,11... | collective-permute-start | bytes 1050632 | tf_op jit(solution)/shard_map/ppermute | solution.py:107
  36.7 1.3 collective-permute-start.1
  39.9 29.1 %all-to-all-start = ((bf16[4,43,2432]{2,1,0:T(8,128)(2,1)}), bf16[4,43,2432]{2,1,0:T(8,128)(2,1)S(1)}, u32[]{:S(2)}, u32[]{:S(2)}) async-start(bf16[4,43,2432]{2,1,0:T(8,128)(2,1)} %pad_maximum_fusion), calls=%async_computation | async-start | bytes 1867776 | tf_op jit(solution)/shard_map/all_to_all | solution.py:186
  45.3 105.4 %all-gather.6.cloned.1.call-start = ((), (), s32[]{:S(2)}) async-start(), calls=%async_computation.3 | async-start | bytes 5603328 | tf_op jit(solution)/shard_map/all_gather | solution.py:230
  69.3 17.0 %collective-permute-start.4 = (bf16[144,2432]{1,0:T(8,128)(2,1)S(1)}, bf16[144,2432]{1,0:T(8,128)(2,1)}, u32[]{:S(2)}, u32[]{:S(2)}) collective-permute-start(bf16[144,2432]{1,0:T(8,128)(2,1)S(1)} %reshape.82), channel_id=1, source_target_pairs={{0,2},{2,0},{1,3},{3,1},{4,6},{6,4},{5,7},{7,5},{8,10},{10,8},{9,1... | collective-permute-start | bytes 2101256 | tf_op jit(solution)/shard_map/ppermute | solution.py:107
  70.0 16.3 %collective-permute-start.2 = (bf16[144,2432]{1,0:T(8,128)(2,1)S(1)}, bf16[144,2432]{1,0:T(8,128)(2,1)}, u32[]{:S(2)}, u32[]{:S(2)}) collective-permute-start(bf16[144,2432]{1,0:T(8,128)(2,1)S(1)} %reshape.82), channel_id=1, source_target_pairs={{0,1},{1,0},{2,3},{3,2},{4,5},{5,4},{6,7},{7,6},{8,9},{9,8},{10,11... | collective-permute-start | bytes 2101256 | tf_op jit(solution)/shard_map/ppermute | solution.py:107
  70.8 16.7 %copy-start.4 = (bf16[2432,384]{1,0:T(8,128)(2,1)S(1)}, bf16[2432,384]{1,0:T(8,128)(2,1)}, u32[]{:S(2)}) copy-start(bf16[2432,384]{1,0:T(8,128)(2,1)} %fusion.8) | copy-start | bytes 5603332
  86.3 8.2 %collective-permute-start.5 = (bf16[144,2432]{1,0:T(8,128)(2,1)}, bf16[144,2432]{1,0:T(8,128)(2,1)}, u32[]{:S(2)}, u32[]{:S(2)}) collective-permute-start(bf16[144,2432]{1,0:T(8,128)(2,1)} %collective-permute-done.4), channel_id=1, source_target_pairs={{0,1},{1,0},{2,3},{3,2},{4,5},{5,4},{6,7},{7,6},{8,9},{9,8},{10,11... | collective-permute-start | bytes 2101256 | tf_op jit(solution)/shard_map/ppermute | solution.py:107
  93.2 3.6 %copy-start.7 = (bf16[2432,384]{1,0:T(8,128)(2,1)S(1)}, bf16[2432,384]{1,0:T(8,128)(2,1)}, u32[]{:S(2)}) copy-start(bf16[2432,384]{1,0:T(8,128)(2,1)} %fusion.7) | copy-start | bytes 5603332
  117.9 17.1 %all-to-all-start.1 = ((bf16[4,144,384]{2,1,0:T(8,128)(2,1)}), bf16[4,144,384]{2,1,0:T(8,128)(2,1)S(1)}, u32[]{:S(2)}, u32[]{:S(2)}) async-start(bf16[4,144,384]{2,1,0:T(8,128)(2,1)} %copy.41), calls=%async_computation.1 | async-start | bytes 884736 | tf_op jit(solution)/shard_map/all_to_all | solution.py:264
  135.1 1.5 collective-permute-start.7
  138.2 12.5 %collective-permute-start.8 = (bf16[2,144,768]{2,1,0:T(8,128)(2,1)}, bf16[2,144,768]{2,1,0:T(8,128)(2,1)}, u32[]{:S(2)}, u32[]{:S(2)}) collective-permute-start(bf16[2,144,768]{2,1,0:T(8,128)(2,1)} %pad_maximum_fusion.2), channel_id=1, source_target_pairs={{0,2},{2,0},{1,3},{3,1},{4,6},{6,4},{5,7},{7,5},{8,10},{10,8},{9,1... | collective-permute-start | bytes 1327112 | tf_op jit(solution)/shard_map/ppermute | solution.py:107
  142.3 12.0 %copy-start.15 = (f32[2,2432]{1,0:T(2,128)S(1)}, f32[2,2432]{1,0:T(2,128)}, u32[]{:S(2)}) copy-start(f32[2,2432]{1,0:T(2,128)} %get-tuple-element.37) | copy-start | bytes 58372
  150.7 3.6 %copy-start.2 = (bf16[2,144,2432]{2,1,0:T(8,128)(2,1)S(1)}, bf16[2,144,2432]{2,1,0:T(8,128)(2,1)}, u32[]{:S(2)}) copy-start(bf16[2,144,2432]{2,1,0:T(8,128)(2,1)} %param.10) | copy-start | bytes 4202500
  (9 other events, 15.0 us)
Sparse Core Ops, SparseCore 0:
  9.7 14.8 all-gather.3
  106.2 11.3 all-gather.5

commit v5 on v4

--- a/solution.py
+++ b/solution.py
@@ -118,6 +118,10 @@
     return jnp.concatenate([first, second], axis=concat_axis)
 
 
+def shifted(block, step, count):
+    return lax.ppermute(block, "seq", [(i, (i + step) % count) for i in range(count)])
+
+
 def body_by_sample(
     image_token_states,
     timestep,
@@ -147,7 +151,7 @@
     half_rank = up_mine.shape[0] // 2
     down_mine = lax.dynamic_slice_in_dim(adapter_down_factors[0], at_core * half_rank, half_rank, 0)
     packed = jnp.concatenate([down_mine, up_mine[:half_rank], up_mine[half_rank:]], axis=1)
-    packed = lax.all_gather(packed, "seq", axis=0)
+    packed = jnp.stack([packed] + [shifted(packed, k, n_seq) for k in range(1, n_seq)])
 
     length_row = jnp.broadcast_to(
         prompt_token_length.astype(jnp.bfloat16)[:, None, None, None],
@@ -183,16 +187,25 @@
     extra = -(-text_size // width)
     text = jnp.pad(text, ((0, 0), (0, extra * width - text_size))).reshape(n_seq, extra, width)
     piece = jnp.concatenate([piece, text], axis=1)
-    piece = lax.all_to_all(piece, "seq", 0, 0, tiled=True)
-    text = piece[:, piece_rows:].reshape(n_seq, extra * width)[:, :text_size].reshape(text_shape)
-    piece = piece[:, :piece_rows]
-    piece = piece.reshape(n_seq * piece_rows, width)
-    piece_mp = flip(piece, "mp")
+    blocks = []
+    for k in range(n_seq):
+        block = lax.dynamic_index_in_dim(piece, (at_seq + k) % n_seq, 0, keepdims=False)
+        blocks.append(shifted(block, k, n_seq) if k else block)
+    text = [
+        block[piece_rows:].reshape(extra * width)[:text_size].reshape(text_shape[1:])
+        for block in blocks
+    ]
+    blocks = [block[:piece_rows] for block in blocks]
+    piece = jnp.concatenate(blocks, axis=0)
+    piece_mp = jnp.concatenate([flip(block, "mp") for block in blocks], axis=0)
     piece_core = flip(piece, "batch")
     piece_both = flip(piece_mp, "batch")
     merged = []
     chosen = jnp.stack(
-        [lax.dynamic_index_in_dim(packed, owner[which], 0, keepdims=False) for which in range(3)]
+        [
+            lax.dynamic_index_in_dim(packed, (at_seq - owner[which]) % n_seq, 0, keepdims=False)
+            for which in range(3)
+        ]
     )
     down_mine = chosen[:, :, :width]
     down_came = flip(down_mine, "batch")
@@ -229,13 +242,16 @@
     weight_here = lax.all_gather(frozen_output_weight, "batch", axis=0, tiled=True)
     weight_away = lax.all_gather(away_weight, "batch", axis=0, tiled=True)
     tokens = queries.shape[0]
-    text_keys = text[:, 0, :txt_rows].reshape(n_seq * txt_rows, columns)
-    text_values = text[:, 1, :txt_rows].reshape(n_seq * txt_rows, columns)
-    length = text[0, 0, txt_rows, 0].astype(jnp.int32)
+    text_keys = jnp.concatenate([block[0, :txt_rows] for block in text], axis=0)
+    text_values = jnp.concatenate([block[1, :txt_rows] for block in text], axis=0)
+    length = text[0][0, txt_rows, 0].astype(jnp.int32)
     keys = jnp.concatenate([keys, text_keys], axis=0)
     values = jnp.concatenate([values, text_values], axis=0)
-    position = jnp.arange(keys.shape[0], dtype=jnp.int32)
-    live = position < tokens + length
+    text_place = (
+        (at_seq - jnp.arange(n_seq, dtype=jnp.int32)[:, None]) % n_seq * txt_rows
+        + jnp.arange(txt_rows, dtype=jnp.int32)[None, :]
+    ).reshape(-1)
+    live = jnp.concatenate([jnp.ones((tokens,), bool), text_place < length])
     scores = (
         jnp.einsum(
             "ihe,nhe->hin",
@@ -261,9 +277,13 @@
     attn = jnp.where(at_mp == 0, attn, attn[::-1])
     attn = jnp.where(at_core == 0, attn, attn[:, ::-1])
     attn = attn.reshape(4, n_seq, piece_rows, columns).transpose(1, 0, 2, 3)
-    attn = lax.all_to_all(attn.reshape(n_seq, img_rows, columns), "seq", 0, 0, tiled=True)
-    attn = swap_pair(attn, 0, 2)
-    attn_away = flip(attn, "mp")
+    attn = attn.reshape(n_seq, img_rows, columns)
+    back = [shifted(attn[k], -k, n_seq) if k else attn[k] for k in range(n_seq)]
+    back_mp = [flip(block, "mp") for block in back]
+    back = lax.dynamic_slice_in_dim(jnp.stack(back + back), n_seq - at_seq, n_seq, 0)
+    back_mp = lax.dynamic_slice_in_dim(jnp.stack(back_mp + back_mp), n_seq - at_seq, n_seq, 0)
+    attn = swap_pair(back, 0, 2)
+    attn_away = swap_pair(back_mp, 0, 2)
     proj = jnp.einsum("sin,nd->sid", attn, weight_here, preferred_element_type=jnp.float32)
     proj = lax.optimization_barrier(proj)
     proj = proj + jnp.einsum(

time: 163 us -> 173 us (1.061)
  local copies, waits for them, and re-layouts: 18 us -> 45.8 us
  waiting for transfers between devices: 51.4 us -> 27.6 us
  starting transfers between devices: 14 us -> 30.7 us
  blocking collectives: 14.9 us -> 0 us
  matrix products: 33.4 us -> 37.5 us
  between operations: 22.4 us -> 18.9 us
  other arithmetic: 8.77 us -> 11.3 us
    all_to_all x2 -> x0, waiting for transfers between devices: 27 us -> none  [the longest x1 13.6 us: body_by_sample(): lax.all_to_all(attn.reshape(n_seq, img_rows, columns), 'seq', 0, 0, tiled...]
    ppermute x0 -> x9, starting transfers between devices: none -> 18.9 us  [shifted(): lax.ppermute(block, 'seq', [(i, (i + step) % count) for i in range(count)])]
    ppermute x0 -> x9, waiting for transfers between devices: none -> 18.6 us  [shifted(): lax.ppermute(block, 'seq', [(i, (i + step) % count) for i in range(count)])]
    ppermute x9 -> x16, waiting for transfers between devices: 24.4 us -> 8.93 us  [flip(): return lax.ppermute(block, axis, [(0, 1), (1, 0)])]
    all_gather x1 -> x0, blocking collectives: 14.9 us -> none  [body_by_sample(): packed = lax.all_gather(packed, 'seq', axis=0)]
    slice x4 -> x23, local copies, waits for them, and re-layouts: 0.64 us -> 10.5 us  [the longest x8 3.08 us: body_by_sample(): text_keys = jnp.concatenate([block[0, :txt_rows] for block in text], axis=0)]
    concatenate x1, local copies, waits for them, and re-layouts: 1.18 us -> 10.6 us  [body_by_sample(): late = jnp.concatenate([piece_mp, piece_both], axis=0)]
    concatenate x1, local copies, waits for them, and re-layouts: 1.18 us -> 10.3 us  [body_by_sample(): early = jnp.concatenate([piece, piece_core], axis=0)]
  transfers between devices with their start and end apart: 13 -> 27, of which waited for: 6 -> 9; matrix products, arithmetic and copies ran while one was open for 32% -> 49% of each run, Pallas kernels for 0% -> 0%
where the time goes in v5:
time: 173 us; the launch traced here: 172 us
  local copies, waits for them, and re-layouts  45.8 us (26%)
  matrix products  37.5 us (22%)
  starting transfers between devices  30.7 us (18%)
  waiting for transfers between devices  27.6 us (16%)
  between operations  18.9 us (11%)
  other arithmetic  11.3 us (7%)
    ppermute x9, starting transfers between devices, shifted(): lax.ppermute(block, 'seq', [(i, (i + step) % count) for i in range(count)])  18.9 us
    ppermute x9, waiting for transfers between devices, shifted(): lax.ppermute(block, 'seq', [(i, (i + step) % count) for i in range(count)])  18.6 us
    dot_general x6, matrix products, body_by_sample(): jnp.dot(rows, m, preferred_element_type=jnp.float32).astype(jnp.bfloat16)  14.2 us
    ppermute x16, starting transfers between devices, flip(): return lax.ppermute(block, axis, [(0, 1), (1, 0)])  11.7 us
    dot_general x3, matrix products, body_by_sample(): jnp.einsum('rd,rn->dn', down_all[which], up_all[which], preferred_element...  10.9 us
    concatenate x1, local copies, waits for them, and re-layouts, body_by_sample(): late = jnp.concatenate([piece_mp, piece_both], axis=0)  10.6 us
    concatenate x1, local copies, waits for them, and re-layouts, body_by_sample(): early = jnp.concatenate([piece, piece_core], axis=0)  10.3 us
    ppermute x16, waiting for transfers between devices, flip(): return lax.ppermute(block, axis, [(0, 1), (1, 0)])  8.93 us
  transfers between devices with their start and end apart: 27, of which 9 were waited for; matrix products, arithmetic and copies ran while one was open for 49% of the time, Pallas kernels for 0%

profile of v5, /device:TPU:0, one launch (start us, length us, event | category | flops | bytes accessed | tf_op | source)
XLA Modules:
  0.0 171.7 jit_solution(9292993934933036861)
XLA Ops:
  11.8 3.1 %collective-permute-start.6 = (bf16[16,3200]{1,0:T(8,128)(2,1)S(1)}, bf16[16,3200]{1,0:T(8,128)(2,1)S(1)}, u32[]{:S(2)}, u32[]{:S(2)}) collective-permute-start(bf16[16,3200]{1,0:T(8,128)(2,1)S(1)} %get-tuple-element.45), channel_id=1, source_target_pairs={{0,4},{4,8},{8,12},{12,0},{1,5},{5,9},{9,13},{13,1},{2,6},{6,10},{... | collective-permute-start | bytes 307208 | tf_op jit(solution)/shard_map/ppermute | solution.py:122
  14.8 2.6 %collective-permute-start.7 = (bf16[16,3200]{1,0:T(8,128)(2,1)S(1)}, bf16[16,3200]{1,0:T(8,128)(2,1)S(1)}, u32[]{:S(2)}, u32[]{:S(2)}) collective-permute-start(bf16[16,3200]{1,0:T(8,128)(2,1)S(1)} %get-tuple-element.45), channel_id=1, source_target_pairs={{0,8},{4,12},{8,0},{12,4},{1,9},{5,13},{9,1},{13,5},{2,10},{6,14},... | collective-permute-start | bytes 307208 | tf_op jit(solution)/shard_map/ppermute | solution.py:122
  26.5 3.7 %fusion.8 = bf16[2432,384]{1,0:T(8,128)(2,1)} fusion(bf16[2432,3,384]{2,0,1:T(8,128)(2,1)} %param.15, bf16[3,16,2432]{2,1,0:T(8,128)(2,1)S(1)} %get-tuple-element.32, bf16[3,16,2432]{2,1,0:T(8,128)(2,1)S(1)} %get-tuple-element.33, bf16[3,32,384]{2,1,0:T(8,128)(2,1)S(1)} %fusion.41), kind=kOutput, calls=%fused_computation.12 | convolution fusion | flops 62881792 | bytes 4227072 | tf_op jit(solution)/shard_map/rd,rn->dn/dot_general | solution.py:223
  30.2 3.8 %fusion.7 = bf16[2432,384]{1,0:T(8,128)(2,1)} fusion(bf16[2432,3,384]{2,0,1:T(8,128)(2,1)} %param.15, bf16[3,16,2432]{2,1,0:T(8,128)(2,1)S(1)} %get-tuple-element.33, bf16[3,16,2432]{2,1,0:T(8,128)(2,1)S(1)} %get-tuple-element.32, bf16[3,32,384]{2,1,0:T(8,128)(2,1)S(1)} %fusion.41), kind=kOutput, calls=%fused_computation.11 | convolution fusion | flops 62881792 | bytes 4227072 | tf_op jit(solution)/shard_map/rd,rn->dn/dot_general | solution.py:223
  34.0 3.4 %fusion.6 = bf16[2432,384]{1,0:T(8,128)(2,1)} fusion(bf16[2432,3,384]{2,0,1:T(8,128)(2,1)} %param.15, bf16[3,16,2432]{2,1,0:T(8,128)(2,1)S(1)} %get-tuple-element.33, bf16[3,16,2432]{2,1,0:T(8,128)(2,1)S(1)} %get-tuple-element.32, bf16[3,32,384]{2,1,0:T(8,128)(2,1)S(1)} %fusion.41), kind=kOutput, calls=%fused_computation.10 | convolution fusion | flops 62881792 | bytes 4227072 | tf_op jit(solution)/shard_map/rd,rn->dn/dot_general | solution.py:223
  39.4 2.3 %collective-permute-start.2 = (bf16[43,2432]{1,0:T(8,128)(2,1)S(1)}, bf16[43,2432]{1,0:T(8,128)(2,1)S(1)}, u32[]{:S(2)}, u32[]{:S(2)}) collective-permute-start(bf16[43,2432]{1,0:T(8,128)(2,1)S(1)} %get-tuple-element.31), channel_id=1, source_target_pairs={{0,4},{4,8},{8,12},{12,0},{1,5},{5,9},{9,13},{13,1},{2,6},{6,10},{... | collective-permute-start | bytes 627464 | tf_op jit(solution)/shard_map/ppermute | solution.py:122
  51.2 7.7 %collective-permute-done.3 = bf16[43,2432]{1,0:T(8,128)(2,1)S(1)} collective-permute-done((bf16[43,2432]{1,0:T(8,128)(2,1)}, bf16[43,2432]{1,0:T(8,128)(2,1)S(1)}, u32[]{:S(2)}, u32[]{:S(2)}) %collective-permute-start.3) | collective-permute-done | bytes 209184 | tf_op jit(solution)/shard_map/ppermute | solution.py:122
  75.0 10.3 %concatenate.84 = bf16[288,2432]{1,0:T(8,128)(2,1)} concatenate(bf16[36,2432]{1,0:T(8,128)(2,1)S(1)} %dynamic-slice_bitcast_fusion.3, bf16[36,2432]{1,0:T(8,128)(2,1)S(1)} %slice.218, bf16[36,2432]{1,0:T(8,128)(2,1)S(1)} %slice.219, bf16[36,2432]{1,0:T(8,128)(2,1)S(1)} %slice.220, bf16[144,2432]{1,0:T(8,128)(2,1)} %collective-permute-done.5), dimensions={0} | concatenate | bytes 2801664 | tf_op jit(solution)/shard_map/concatenate | solution.py:230
  85.4 3.0 %convolution_convert_fusion.3 = bf16[288,384]{1,0:T(8,128)(2,1)S(1)} fusion(bf16[288,2432]{1,0:T(8,128)(2,1)} %concatenate.84, bf16[2432,384]{1,0:T(8,128)(2,1)} %fusion.8), kind=kOutput, calls=%fused_computation.30 | convolution fusion | flops 538030080 | bytes 3489792 | tf_op jit(solution)/shard_map/dot_general | solution.py:234
  92.0 10.6 %concatenate.90 = bf16[288,2432]{1,0:T(8,128)(2,1)} concatenate(bf16[36,2432]{1,0:T(8,128)(2,1)S(1)} %collective-permute-done.10, bf16[36,2432]{1,0:T(8,128)(2,1)S(1)} %collective-permute-done.11, bf16[36,2432]{1,0:T(8,128)(2,1)S(1)} %copy-done.9, bf16[36,2432]{1,0:T(8,128)(2,1)} %collective-permute-done.13, bf16[144,2432]{1,0:T(8,128)(2,1)} %collective-permute-done.14), dimensions={0} | concatenate | bytes 2801664 | tf_op jit(solution)/shard_map/concatenate | solution.py:231
  102.6 2.9 %convolution_convert_fusion = bf16[288,384]{1,0:T(8,128)(2,1)S(1)} fusion(bf16[288,2432]{1,0:T(8,128)(2,1)} %concatenate.90, bf16[2432,384]{1,0:T(8,128)(2,1)} %fusion.7), kind=kOutput, calls=%fused_computation.27 | convolution fusion | flops 538030080 | bytes 3489792 | tf_op jit(solution)/shard_map/dot_general | solution.py:234
  106.4 2.9 %convolution_convert_fusion.2 = bf16[288,384]{1,0:T(8,128)(2,1)S(1)} fusion(bf16[288,2432]{1,0:T(8,128)(2,1)} %concatenate.90, bf16[2432,384]{1,0:T(8,128)(2,1)} %fusion.8), kind=kOutput, calls=%fused_computation.29 | convolution fusion | flops 538030080 | bytes 3489792 | tf_op jit(solution)/shard_map/dot_general | solution.py:234
  110.9 2.0 %concatenate.96 = bf16[660,6,64]{0,2,1:T(8,128)(2,1)} concatenate(bf16[288,6,64]{0,2,1:T(8,128)(2,1)S(1)} %bitcast.131, bf16[288,6,64]{0,2,1:T(8,128)(2,1)S(1)} %bitcast.133, bf16[21,6,64]{0,2,1:T(8,128)(2,1)} %bitcast.136, bf16[21,6,64]{0,2,1:T(8,128)(2,1)} %bitcast.139, bf16[21,6,64]{0,2,1:T(8,128)(2,1)} %bitcast.141, bf16[21,6,64]{0,2,1:T(8,128)(2,1)} %bitcast.142), dimensions={0} | concatenate | bytes 1013760 | tf_op jit(solution)/shard_map/concatenate | solution.py:249
  112.9 2.9 %convolution_convert_fusion.1 = bf16[288,384]{1,0:T(8,128)(2,1)S(1)} fusion(bf16[288,2432]{1,0:T(8,128)(2,1)} %concatenate.90, bf16[2432,384]{1,0:T(8,128)(2,1)} %fusion.6), kind=kOutput, calls=%fused_computation.28 | convolution fusion | flops 538030080 | bytes 3489792 | tf_op jit(solution)/shard_map/dot_general | solution.py:234
  116.2 2.4 %fusion = (f32[6,576]{1,0:T(8,128)S(1)}, f32[6,576,660]{1,2,0:T(8,128)S(1)}) fusion(pred[660]{0:T(1024)(128)(4,1)S(1)} %concatenate.97, bf16[576,6,64]{0,2,1:T(8,128)(2,1)S(1)} %bitcast.130, bf16[660,6,64]{0,2,1:T(8,128)(2,1)S(1)} %concatenate.105), kind=kOutput, calls=%fused_computation.2 | convolution fusion | flops 298802304 | bytes 10087572 | tf_op jit(solution)/shard_map/ihe,nhe->hin/dot_general | solution.py:256
  118.6 2.3 %fusion.1 = f32[6,576]{1,0:T(8,128)S(1)} fusion(f32[6,576,660]{1,2,0:T(8,128)S(1)} %get-tuple-element.63, f32[6,576]{1,0:T(8,128)S(1)} %get-tuple-element.62, pred[660]{0:T(1024)(128)(4,1)S(1)} %concatenate.97), kind=kLoop, calls=%fused_computation.3 | loop fusion | flops 9120384 | bytes 9152148 | tf_op jit(solution)/shard_map/reduce_sum | solution.py:267
  120.9 2.6 %divide_convert_fusion = bf16[576,6,64]{0,2,1:T(8,128)(2,1)S(1)} fusion(bf16[660,6,64]{0,2,1:T(8,128)(2,1)S(1)} %copy-done.10, f32[6,576,660]{1,2,0:T(8,128)S(1)} %get-tuple-element.63, f32[6,576]{1,0:T(8,128)S(1)} %get-tuple-element.62, pred[660]{0:T(1024)(128)(4,1)S(1)} %concatenate.97, f32[576,6]{0,1:T(8,128)S(1)} %bitcast.151), kind=kOutput, calls=%fused_computation.33 | convolution fusion | flops 301529088 | bytes 10101396 | tf_op jit(solution)/shard_map/hin,nhe->ihe/dot_general | solution.py:268
  126.7 6.3 %collective-permute-start.16 = (bf16[144,384]{1,0:T(8,128)(2,1)S(1)}, bf16[144,384]{1,0:T(8,128)(2,1)S(1)}, u32[]{:S(2)}, u32[]{:S(2)}) collective-permute-start(bf16[144,384]{1,0:T(8,128)(2,1)S(1)} %squeeze.91), channel_id=1, source_target_pairs={{0,12},{4,0},{8,4},{12,8},{1,13},{5,1},{9,5},{13,9},{2,14},{6,2},{... | collective-permute-start | bytes 331784 | tf_op jit(solution)/shard_map/ppermute | solution.py:122
  134.0 2.4 %collective-permute-done.16 = bf16[144,384]{1,0:T(8,128)(2,1)S(1)} collective-permute-done((bf16[144,384]{1,0:T(8,128)(2,1)S(1)}, bf16[144,384]{1,0:T(8,128)(2,1)S(1)}, u32[]{:S(2)}, u32[]{:S(2)}) %collective-permute-start.16) | collective-permute-done | bytes 110624 | tf_op jit(solution)/shard_map/ppermute | solution.py:122
  136.5 6.5 %collective-permute-done.17 = bf16[144,384]{1,0:T(8,128)(2,1)S(1)} collective-permute-done((bf16[144,384]{1,0:T(8,128)(2,1)S(1)}, bf16[144,384]{1,0:T(8,128)(2,1)S(1)}, u32[]{:S(2)}, u32[]{:S(2)}) %collective-permute-start.17) | collective-permute-done | bytes 110624 | tf_op jit(solution)/shard_map/ppermute | solution.py:122
  146.9 2.3 %collective-permute-done.21 = bf16[144,384]{1,0:T(8,128)(2,1)S(1)} collective-permute-done((bf16[144,384]{1,0:T(8,128)(2,1)S(1)}, bf16[144,384]{1,0:T(8,128)(2,1)S(1)}, u32[]{:S(2)}, u32[]{:S(2)}) %collective-permute-start.21) | collective-permute-done | bytes 110624 | tf_op jit(solution)/shard_map/ppermute | solution.py:107
  149.2 2.3 %collective-permute-done.22 = bf16[144,384]{1,0:T(8,128)(2,1)S(1)} collective-permute-done((bf16[144,384]{1,0:T(8,128)(2,1)S(1)}, bf16[144,384]{1,0:T(8,128)(2,1)S(1)}, u32[]{:S(2)}, u32[]{:S(2)}) %collective-permute-start.22) | collective-permute-done | bytes 110624 | tf_op jit(solution)/shard_map/ppermute | solution.py:107
  156.1 3.4 %fusion.11 = f32[2,144,2432]{2,1,0:T(8,128)S(1)} fusion(bf16[768,2432]{1,0:T(8,128)(2,1)} %all-gather.3.cloned.1.call-done, bf16[2,144,384]{2,1,0:T(8,128)(2,1)S(1)} %get-tuple-element.26, bf16[2,144,384]{2,1,0:T(8,128)(2,1)S(1)} %get-tuple-element.25), kind=kOutput, calls=%fused_computation.15 | convolution fusion | flops 1076723712 | bytes 6979584 | tf_op jit(solution)/shard_map/sin,nd->sid/dot_general | solution.py:287
  159.5 3.7 %fusion.9 = f32[2,144,2432]{2,1,0:T(8,128)S(1)} fusion(bf16[768,2432]{1,0:T(8,128)(2,1)} %all-gather.5.cloned.1.call-done, bf16[2,144,384]{2,1,0:T(8,128)(2,1)} %get-tuple-element.24, bf16[2,144,384]{2,1,0:T(8,128)(2,1)} %get-tuple-element.23), kind=kOutput, calls=%fused_computation.13 | convolution fusion | flops 1076723712 | bytes 6979584 | tf_op jit(solution)/shard_map/sin,nd->sid/dot_general | solution.py:289
  (192 shorter events, 57.2 us)
Async XLA Ops:
  6.5 149.5 %all-gather.3.cloned.1.call-start = ((), (), s32[]{:S(2)}) async-start(), calls=%async_computation | async-start | bytes 5603328 | tf_op jit(solution)/shard_map/all_gather | solution.py:242
  11.8 12.9 %collective-permute-start.6 = (bf16[16,3200]{1,0:T(8,128)(2,1)S(1)}, bf16[16,3200]{1,0:T(8,128)(2,1)S(1)}, u32[]{:S(2)}, u32[]{:S(2)}) collective-permute-start(bf16[16,3200]{1,0:T(8,128)(2,1)S(1)} %get-tuple-element.45), channel_id=1, source_target_pairs={{0,4},{4,8},{8,12},{12,0},{1,5},{5,9},{9,13},{13,1},{2,6},{6,10},{... | collective-permute-start | bytes 307208 | tf_op jit(solution)/shard_map/ppermute | solution.py:122
  14.8 9.8 %collective-permute-start.7 = (bf16[16,3200]{1,0:T(8,128)(2,1)S(1)}, bf16[16,3200]{1,0:T(8,128)(2,1)S(1)}, u32[]{:S(2)}, u32[]{:S(2)}) collective-permute-start(bf16[16,3200]{1,0:T(8,128)(2,1)S(1)} %get-tuple-element.45), channel_id=1, source_target_pairs={{0,8},{4,12},{8,0},{12,4},{1,9},{5,13},{9,1},{13,5},{2,10},{6,14},... | collective-permute-start | bytes 307208 | tf_op jit(solution)/shard_map/ppermute | solution.py:122
  17.4 7.2 %collective-permute-start.8 = (bf16[16,3200]{1,0:T(8,128)(2,1)S(1)}, bf16[16,3200]{1,0:T(8,128)(2,1)S(1)}, u32[]{:S(2)}, u32[]{:S(2)}) collective-permute-start(bf16[16,3200]{1,0:T(8,128)(2,1)S(1)} %get-tuple-element.45), channel_id=1, source_target_pairs={{0,12},{4,0},{8,4},{12,8},{1,13},{5,1},{9,5},{13,9},{2,14},{6,2},{... | collective-permute-start | bytes 307208 | tf_op jit(solution)/shard_map/ppermute | solution.py:122
  21.6 15.9 %collective-permute-start = (bf16[2,36,2432]{2,1,0:T(8,128)(2,1)S(1)}, bf16[2,36,2432]{2,1,0:T(8,128)(2,1)S(1)}, u32[]{:S(2)}, u32[]{:S(2)}) collective-permute-start(bf16[2,36,2432]{2,1,0:T(8,128)(2,1)S(1)} %constant_dynamic-slice_fusion.6), channel_id=1, source_target_pairs={{0,1},{1,0},{2,3},{3,2},{4,5},{5,4},{6,7},{7,6},{8,9},{9,8},{10,11... | collective-permute-start | bytes 1050632 | tf_op jit(solution)/shard_map/ppermute | solution.py:107
  22.4 137.1 %all-gather.5.cloned.1.call-start = ((), (), s32[]{:S(2)}) async-start(), calls=%async_computation.1 | async-start | bytes 5603328 | tf_op jit(solution)/shard_map/all_gather | solution.py:243
  39.4 10.5 %collective-permute-start.2 = (bf16[43,2432]{1,0:T(8,128)(2,1)S(1)}, bf16[43,2432]{1,0:T(8,128)(2,1)S(1)}, u32[]{:S(2)}, u32[]{:S(2)}) collective-permute-start(bf16[43,2432]{1,0:T(8,128)(2,1)S(1)} %get-tuple-element.31), channel_id=1, source_target_pairs={{0,4},{4,8},{8,12},{12,0},{1,5},{5,9},{9,13},{13,1},{2,6},{6,10},{... | collective-permute-start | bytes 627464 | tf_op jit(solution)/shard_map/ppermute | solution.py:122
  41.7 17.2 %collective-permute-start.3 = (bf16[43,2432]{1,0:T(8,128)(2,1)}, bf16[43,2432]{1,0:T(8,128)(2,1)S(1)}, u32[]{:S(2)}, u32[]{:S(2)}) collective-permute-start(bf16[43,2432]{1,0:T(8,128)(2,1)} %get-tuple-element.30), channel_id=1, source_target_pairs={{0,8},{4,12},{8,0},{12,4},{1,9},{5,13},{9,1},{13,5},{2,10},{6,14},... | collective-permute-start | bytes 627464 | tf_op jit(solution)/shard_map/ppermute | solution.py:122
  43.0 18.1 %collective-permute-start.4 = (bf16[43,2432]{1,0:T(8,128)(2,1)}, bf16[43,2432]{1,0:T(8,128)(2,1)}, u32[]{:S(2)}, u32[]{:S(2)}) collective-permute-start(bf16[43,2432]{1,0:T(8,128)(2,1)} %get-tuple-element.29), channel_id=1, source_target_pairs={{0,12},{4,0},{8,4},{12,8},{1,13},{5,1},{9,5},{13,9},{2,14},{6,2},{... | collective-permute-start | bytes 627464 | tf_op jit(solution)/shard_map/ppermute | solution.py:122
  44.1 27.4 %collective-permute-start.10 = (bf16[36,2432]{1,0:T(8,128)(2,1)S(1)}, bf16[36,2432]{1,0:T(8,128)(2,1)S(1)}, u32[]{:S(2)}, u32[]{:S(2)}) collective-permute-start(bf16[36,2432]{1,0:T(8,128)(2,1)S(1)} %dynamic-slice_bitcast_fusion.3), channel_id=1, source_target_pairs={{0,2},{2,0},{1,3},{3,1},{4,6},{6,4},{5,7},{7,5},{8,10},{10,8},{9,1... | collective-permute-start | bytes 525320 | tf_op jit(solution)/shard_map/ppermute | solution.py:107
  49.9 23.0 %collective-permute-start.11 = (bf16[36,2432]{1,0:T(8,128)(2,1)S(1)}, bf16[36,2432]{1,0:T(8,128)(2,1)S(1)}, u32[]{:S(2)}, u32[]{:S(2)}) collective-permute-start(bf16[36,2432]{1,0:T(8,128)(2,1)S(1)} %slice.218), channel_id=1, source_target_pairs={{0,2},{2,0},{1,3},{3,1},{4,6},{6,4},{5,7},{7,5},{8,10},{10,8},{9,1... | collective-permute-start | bytes 525320 | tf_op jit(solution)/shard_map/ppermute | solution.py:107
  59.6 13.2 %collective-permute-start.12 = (bf16[36,2432]{1,0:T(8,128)(2,1)S(1)}, bf16[36,2432]{1,0:T(8,128)(2,1)S(1)}, u32[]{:S(2)}, u32[]{:S(2)}) collective-permute-start(bf16[36,2432]{1,0:T(8,128)(2,1)S(1)} %slice.219), channel_id=1, source_target_pairs={{0,2},{2,0},{1,3},{3,1},{4,6},{6,4},{5,7},{7,5},{8,10},{10,8},{9,1... | collective-permute-start | bytes 525320 | tf_op jit(solution)/shard_map/ppermute | solution.py:107
  62.0 10.8 %collective-permute-start.13 = (bf16[36,2432]{1,0:T(8,128)(2,1)S(1)}, bf16[36,2432]{1,0:T(8,128)(2,1)}, u32[]{:S(2)}, u32[]{:S(2)}) collective-permute-start(bf16[36,2432]{1,0:T(8,128)(2,1)S(1)} %slice.220), channel_id=1, source_target_pairs={{0,2},{2,0},{1,3},{3,1},{4,6},{6,4},{5,7},{7,5},{8,10},{10,8},{9,1... | collective-permute-start | bytes 525320 | tf_op jit(solution)/shard_map/ppermute | solution.py:107
  63.7 11.3 %collective-permute-start.5 = (bf16[144,2432]{1,0:T(8,128)(2,1)}, bf16[144,2432]{1,0:T(8,128)(2,1)}, u32[]{:S(2)}, u32[]{:S(2)}) collective-permute-start(bf16[144,2432]{1,0:T(8,128)(2,1)} %pad_maximum_fusion.1), channel_id=1, source_target_pairs={{0,1},{1,0},{2,3},{3,2},{4,5},{5,4},{6,7},{7,6},{8,9},{9,8},{10,11... | collective-permute-start | bytes 2101256 | tf_op jit(solution)/shard_map/ppermute | solution.py:107
  71.4 44.5 %collective-permute-start.15 = (bf16[384,2432]{1,0:T(8,128)(2,1)S(1)}, bf16[384,2432]{1,0:T(8,128)(2,1)}, u32[]{:S(2)}, u32[]{:S(2)}) collective-permute-start(bf16[384,2432]{1,0:T(8,128)(2,1)S(1)} %copy-done.4), channel_id=1, source_target_pairs={{0,2},{2,0},{1,3},{3,1},{4,6},{6,4},{5,7},{7,5},{8,10},{10,8},{9,1... | collective-permute-start | bytes 5603336 | tf_op jit(solution)/shard_map/ppermute | solution.py:107
  74.8 17.2 %collective-permute-start.14 = (bf16[144,2432]{1,0:T(8,128)(2,1)}, bf16[144,2432]{1,0:T(8,128)(2,1)}, u32[]{:S(2)}, u32[]{:S(2)}) collective-permute-start(bf16[144,2432]{1,0:T(8,128)(2,1)} %pad_maximum_fusion.2), channel_id=1, source_target_pairs={{0,1},{1,0},{2,3},{3,2},{4,5},{5,4},{6,7},{7,6},{8,9},{9,8},{10,11... | collective-permute-start | bytes 2101256 | tf_op jit(solution)/shard_map/ppermute | solution.py:107
  126.0 20.9 %collective-permute-start.20 = (bf16[144,384]{1,0:T(8,128)(2,1)S(1)}, bf16[144,384]{1,0:T(8,128)(2,1)S(1)}, u32[]{:S(2)}, u32[]{:S(2)}) collective-permute-start(bf16[144,384]{1,0:T(8,128)(2,1)S(1)} %squeeze.94), channel_id=1, source_target_pairs={{0,2},{2,0},{1,3},{3,1},{4,6},{6,4},{5,7},{7,5},{8,10},{10,8},{9,1... | collective-permute-start | bytes 331784 | tf_op jit(solution)/shard_map/ppermute | solution.py:107
  126.7 9.8 %collective-permute-start.16 = (bf16[144,384]{1,0:T(8,128)(2,1)S(1)}, bf16[144,384]{1,0:T(8,128)(2,1)S(1)}, u32[]{:S(2)}, u32[]{:S(2)}) collective-permute-start(bf16[144,384]{1,0:T(8,128)(2,1)S(1)} %squeeze.91), channel_id=1, source_target_pairs={{0,12},{4,0},{8,4},{12,8},{1,13},{5,1},{9,5},{13,9},{2,14},{6,2},{... | collective-permute-start | bytes 331784 | tf_op jit(solution)/shard_map/ppermute | solution.py:122
  133.0 10.0 %collective-permute-start.17 = (bf16[144,384]{1,0:T(8,128)(2,1)S(1)}, bf16[144,384]{1,0:T(8,128)(2,1)S(1)}, u32[]{:S(2)}, u32[]{:S(2)}) collective-permute-start(bf16[144,384]{1,0:T(8,128)(2,1)S(1)} %squeeze.92), channel_id=1, source_target_pairs={{0,8},{4,12},{8,0},{12,4},{1,9},{5,13},{9,1},{13,5},{2,10},{6,14},... | collective-permute-start | bytes 331784 | tf_op jit(solution)/shard_map/ppermute | solution.py:122
  133.1 9.9 %collective-permute-start.18 = (bf16[144,384]{1,0:T(8,128)(2,1)S(1)}, bf16[144,384]{1,0:T(8,128)(2,1)S(1)}, u32[]{:S(2)}, u32[]{:S(2)}) collective-permute-start(bf16[144,384]{1,0:T(8,128)(2,1)S(1)} %squeeze.93), channel_id=1, source_target_pairs={{0,4},{4,8},{8,12},{12,0},{1,5},{5,9},{9,13},{13,1},{2,6},{6,10},{... | collective-permute-start | bytes 331784 | tf_op jit(solution)/shard_map/ppermute | solution.py:122
  143.2 10.5 %collective-permute-start.19 = (bf16[2,144,384]{2,1,0:T(8,128)(2,1)S(1)}, bf16[2,144,384]{2,1,0:T(8,128)(2,1)S(1)}, u32[]{:S(2)}, u32[]{:S(2)}) collective-permute-start(bf16[2,144,384]{2,1,0:T(8,128)(2,1)S(1)} %constant_dynamic-slice_fusion.1), channel_id=1, source_target_pairs={{0,1},{1,0},{2,3},{3,2},{4,5},{5,4},{6,7},{7,6},{8,9},{9,8},{10,11... | collective-permute-start | bytes 663560 | tf_op jit(solution)/shard_map/ppermute | solution.py:107
  143.3 5.9 %collective-permute-start.21 = (bf16[144,384]{1,0:T(8,128)(2,1)S(1)}, bf16[144,384]{1,0:T(8,128)(2,1)S(1)}, u32[]{:S(2)}, u32[]{:S(2)}) collective-permute-start(bf16[144,384]{1,0:T(8,128)(2,1)S(1)} %collective-permute-done.16), channel_id=1, source_target_pairs={{0,2},{2,0},{1,3},{3,1},{4,6},{6,4},{5,7},{7,5},{8,10},{10,8},{9,1... | collective-permute-start | bytes 331784 | tf_op jit(solution)/shard_map/ppermute | solution.py:107
  144.8 6.8 %collective-permute-start.22 = (bf16[144,384]{1,0:T(8,128)(2,1)S(1)}, bf16[144,384]{1,0:T(8,128)(2,1)S(1)}, u32[]{:S(2)}, u32[]{:S(2)}) collective-permute-start(bf16[144,384]{1,0:T(8,128)(2,1)S(1)} %collective-permute-done.17), channel_id=1, source_target_pairs={{0,2},{2,0},{1,3},{3,1},{4,6},{6,4},{5,7},{7,5},{8,10},{10,8},{9,1... | collective-permute-start | bytes 331784 | tf_op jit(solution)/shard_map/ppermute | solution.py:107
  145.4 8.1 %collective-permute-start.23 = (bf16[144,384]{1,0:T(8,128)(2,1)S(1)}, bf16[144,384]{1,0:T(8,128)(2,1)S(1)}, u32[]{:S(2)}, u32[]{:S(2)}) collective-permute-start(bf16[144,384]{1,0:T(8,128)(2,1)S(1)} %collective-permute-done.18), channel_id=1, source_target_pairs={{0,2},{2,0},{1,3},{3,1},{4,6},{6,4},{5,7},{7,5},{8,10},{10,8},{9,1... | collective-permute-start | bytes 331784 | tf_op jit(solution)/shard_map/ppermute | solution.py:107
  (21 other events, 117.6 us)
Sparse Core Ops, SparseCore 0:
  22.5 11.3 all-gather.2
  134.1 13.8 all-gather.4

commit v6 on v5

--- a/solution.py
+++ b/solution.py
@@ -122,6 +122,20 @@
     return lax.ppermute(block, "seq", [(i, (i + step) % count) for i in range(count)])
 
 
+def blocks_of(array, at_seq):
+    count = array.shape[0]
+    blocks = []
+    for k in range(count):
+        block = lax.dynamic_index_in_dim(array, (at_seq + k) % count, 0, keepdims=False)
+        blocks.append(shifted(block, k, count) if k else block)
+    return blocks
+
+
+def joined(blocks):
+    stacked = lax.optimization_barrier(jnp.stack(blocks))
+    return stacked.reshape(-1, blocks[0].shape[-1])
+
+
 def body_by_sample(
     image_token_states,
     timestep,
@@ -158,9 +172,6 @@
         (samples, 2, 1, text_key_value.shape[3]),
     )
     text = swap_pair(jnp.concatenate([text_key_value, length_row], axis=2), 3, 0)
-    text_shape = text.shape
-    text = text.reshape(n_seq, -1)
-    text_size = text.shape[1]
 
     away_weight = flip(frozen_output_weight, "mp")
 
@@ -184,20 +195,10 @@
 
     piece = swap_pair(normed, 1, 0)
     piece_rows = piece.shape[1]
-    extra = -(-text_size // width)
-    text = jnp.pad(text, ((0, 0), (0, extra * width - text_size))).reshape(n_seq, extra, width)
-    piece = jnp.concatenate([piece, text], axis=1)
-    blocks = []
-    for k in range(n_seq):
-        block = lax.dynamic_index_in_dim(piece, (at_seq + k) % n_seq, 0, keepdims=False)
-        blocks.append(shifted(block, k, n_seq) if k else block)
-    text = [
-        block[piece_rows:].reshape(extra * width)[:text_size].reshape(text_shape[1:])
-        for block in blocks
-    ]
-    blocks = [block[:piece_rows] for block in blocks]
-    piece = jnp.concatenate(blocks, axis=0)
-    piece_mp = jnp.concatenate([flip(block, "mp") for block in blocks], axis=0)
+    blocks = blocks_of(piece, at_seq)
+    text = blocks_of(text, at_seq)
+    piece = joined(blocks)
+    piece_mp = joined([flip(block, "mp") for block in blocks])
     piece_core = flip(piece, "batch")
     piece_both = flip(piece_mp, "batch")
     merged = []
@@ -227,8 +228,8 @@
             (frozen_query_key_value[:, which].astype(jnp.float32) + delta).astype(jnp.bfloat16)
         )
     merged = lax.optimization_barrier(merged)
-    early = jnp.concatenate([piece, piece_core], axis=0)
-    late = jnp.concatenate([piece_mp, piece_both], axis=0)
+    early = joined([piece, piece_core])
+    late = joined([piece_mp, piece_both])
     triple = []
     halves = [
         [jnp.dot(rows, m, preferred_element_type=jnp.float32).astype(jnp.bfloat16) for m in merged]

time: 173 us -> 183 us (1.058)
  waiting for transfers between devices: 27.6 us -> 63 us
  local copies, waits for them, and re-layouts: 45.8 us -> 25 us
  matrix products: 37.5 us -> 34 us
  other arithmetic: 11.3 us -> 13.2 us
  starting transfers between devices: 30.7 us -> 28.8 us
    ppermute x16, waiting for transfers between devices: 8.93 us -> 35.6 us  [flip(): return lax.ppermute(block, axis, [(0, 1), (1, 0)])]
    concatenate x3 -> x0, local copies, waits for them, and re-layouts: 21 us -> none  [the longest x1 10.6 us: body_by_sample(): late = jnp.concatenate([piece_mp, piece_both], axis=0)]
    ppermute x9 -> x12, waiting for transfers between devices: 18.6 us -> 27.3 us  [shifted(): lax.ppermute(block, 'seq', [(i, (i + step) % count) for i in range(count)])]
    slice x8 -> x0, local copies, waits for them, and re-layouts: 3.72 us -> none  [the longest x4 2.73 us: body_by_sample(): block[piece_rows:].reshape(extra * width)[:text_size]]
    concatenate x3 -> x0, other arithmetic: 3.06 us -> none  [the longest x1 1.96 us: body_by_sample(): piece_mp = jnp.concatenate([flip(block, 'mp') for block in blocks], axis=0)]
    dot_general x6, matrix products: 14.2 us -> 11.4 us  [body_by_sample(): jnp.dot(rows, m, preferred_element_type=jnp.float32).astype(jnp.bfloat16)]
    another operation x0 -> x4, other arithmetic: none -> 2.8 us  [joined(): stacked = lax.optimization_barrier(jnp.stack(blocks))]
    unnamed x50 -> x44, local copies, waits for them, and re-layouts: 1.6 us -> 3.81 us
  transfers between devices with their start and end apart: 27 -> 30, of which waited for: 9 -> 16; matrix products, arithmetic and copies ran while one was open for 49% -> 33% of each run, Pallas kernels for 0% -> 0%
where the time goes in v6:
time: 183 us
  waiting for transfers between devices  63 us (34%)
  matrix products  34 us (19%)
  starting transfers between devices  28.8 us (16%)
  local copies, waits for them, and re-layouts  25 us (14%)
  between operations  18.8 us (10%)
  other arithmetic  13.2 us (7%)
    ppermute x16, waiting for transfers between devices, flip(): return lax.ppermute(block, axis, [(0, 1), (1, 0)])  35.6 us
    ppermute x12, waiting for transfers between devices, shifted(): lax.ppermute(block, 'seq', [(i, (i + step) % count) for i in range(count)])  27.3 us
    ppermute x12, starting transfers between devices, shifted(): lax.ppermute(block, 'seq', [(i, (i + step) % count) for i in range(count)])  18.1 us
    dot_general x6, matrix products, body_by_sample(): jnp.dot(rows, m, preferred_element_type=jnp.float32).astype(jnp.bfloat16)  11.4 us
    ppermute x16, starting transfers between devices, flip(): return lax.ppermute(block, axis, [(0, 1), (1, 0)])  10.6 us
    dot_general x3, matrix products, body_by_sample(): jnp.einsum('rd,rn->dn', down_all[which], up_all[which], preferred_element...  10.3 us
    unnamed x44, local copies, waits for them, and re-layouts  3.81 us
    dot_general x1, matrix products, body_by_sample(): jnp.einsum('sin,nd->sid', attn_away, weight_away, preferred_element_type=...  3.68 us
  transfers between devices with their start and end apart: 30, of which 16 were waited for; matrix products, arithmetic and copies ran while one was open for 33% of the time, Pallas kernels for 0%

profile of v6, /device:TPU:0, one launch (start us, length us, event | category | flops | bytes accessed | tf_op | source)
XLA Modules:
  0.0 182.7 jit_solution(7099278769731719401)
XLA Ops:
  12.4 3.0 %collective-permute-start.5 = (bf16[16,3200]{1,0:T(8,128)(2,1)}, bf16[16,3200]{1,0:T(8,128)(2,1)S(1)}, u32[]{:S(2)}, u32[]{:S(2)}) collective-permute-start(bf16[16,3200]{1,0:T(8,128)(2,1)} %get-tuple-element.50), channel_id=1, source_target_pairs={{0,4},{4,8},{8,12},{12,0},{1,5},{5,9},{9,13},{13,1},{2,6},{6,10},{... | collective-permute-start | bytes 307208 | tf_op jit(solution)/shard_map/ppermute | solution.py:122
  15.4 2.6 %collective-permute-start.6 = (bf16[16,3200]{1,0:T(8,128)(2,1)}, bf16[16,3200]{1,0:T(8,128)(2,1)}, u32[]{:S(2)}, u32[]{:S(2)}) collective-permute-start(bf16[16,3200]{1,0:T(8,128)(2,1)} %get-tuple-element.50), channel_id=1, source_target_pairs={{0,8},{4,12},{8,0},{12,4},{1,9},{5,13},{9,1},{13,5},{2,10},{6,14},... | collective-permute-start | bytes 307208 | tf_op jit(solution)/shard_map/ppermute | solution.py:122
  28.8 3.2 %collective-permute-done.15 = bf16[2,22,384]{2,0,1:T(2,128)(2,1)S(1)} collective-permute-done((bf16[2,22,384]{2,0,1:T(2,128)(2,1)S(1)}, bf16[2,22,384]{2,0,1:T(2,128)(2,1)S(1)}, u32[]{:S(2)}, u32[]{:S(2)}) %collective-permute-start.15) | collective-permute-done | bytes 33824 | tf_op jit(solution)/shard_map/ppermute | solution.py:122
  32.1 4.8 %collective-permute-done.16 = bf16[2,22,384]{2,0,1:T(2,128)(2,1)S(1)} collective-permute-done((bf16[2,22,384]{2,0,1:T(2,128)(2,1)S(1)}, bf16[2,22,384]{2,0,1:T(2,128)(2,1)S(1)}, u32[]{:S(2)}, u32[]{:S(2)}) %collective-permute-start.16) | collective-permute-done | bytes 33824 | tf_op jit(solution)/shard_map/ppermute | solution.py:122
  48.5 3.4 %fusion.8 = bf16[2432,384]{1,0:T(8,128)(2,1)} fusion(bf16[2432,3,384]{2,0,1:T(8,128)(2,1)} %param.15, bf16[3,16,2432]{2,1,0:T(8,128)(2,1)S(1)} %get-tuple-element.33, bf16[3,16,2432]{2,1,0:T(8,128)(2,1)S(1)} %get-tuple-element.34, bf16[3,32,384]{2,1,0:T(8,128)(2,1)S(1)} %fusion.48), kind=kOutput, calls=%fused_computation.12 | convolution fusion | flops 62881792 | bytes 4227072 | tf_op jit(solution)/shard_map/rd,rn->dn/dot_general | solution.py:224
  51.9 2.5 %collective-permute-done.1 = bf16[36,2432]{1,0:T(8,128)(2,1)S(1)} collective-permute-done((bf16[36,2432]{1,0:T(8,128)(2,1)S(1)}, bf16[36,2432]{1,0:T(8,128)(2,1)S(1)}, u32[]{:S(2)}, u32[]{:S(2)}) %collective-permute-start.1) | collective-permute-done | bytes 175136 | tf_op jit(solution)/shard_map/ppermute | solution.py:122
  54.4 6.8 %collective-permute-done.2 = bf16[36,2432]{1,0:T(8,128)(2,1)} collective-permute-done((bf16[36,2432]{1,0:T(8,128)(2,1)S(1)}, bf16[36,2432]{1,0:T(8,128)(2,1)}, u32[]{:S(2)}, u32[]{:S(2)}) %collective-permute-start.2) | collective-permute-done | bytes 175136 | tf_op jit(solution)/shard_map/ppermute | solution.py:122
  63.3 3.4 %fusion.7 = bf16[2432,384]{1,0:T(8,128)(2,1)} fusion(bf16[2432,3,384]{2,0,1:T(8,128)(2,1)} %param.15, bf16[3,16,2432]{2,1,0:T(8,128)(2,1)S(1)} %get-tuple-element.34, bf16[3,16,2432]{2,1,0:T(8,128)(2,1)S(1)} %get-tuple-element.33, bf16[3,32,384]{2,1,0:T(8,128)(2,1)S(1)} %fusion.48), kind=kOutput, calls=%fused_computation.11 | convolution fusion | flops 62881792 | bytes 4227072 | tf_op jit(solution)/shard_map/rd,rn->dn/dot_general | solution.py:224
  70.8 3.5 %fusion.6 = bf16[2432,384]{1,0:T(8,128)(2,1)} fusion(bf16[2432,3,384]{2,0,1:T(8,128)(2,1)} %param.15, bf16[3,16,2432]{2,1,0:T(8,128)(2,1)S(1)} %get-tuple-element.34, bf16[3,16,2432]{2,1,0:T(8,128)(2,1)S(1)} %get-tuple-element.33, bf16[3,32,384]{2,1,0:T(8,128)(2,1)S(1)} %fusion.48), kind=kOutput, calls=%fused_computation.10 | convolution fusion | flops 62881792 | bytes 4227072 | tf_op jit(solution)/shard_map/rd,rn->dn/dot_general | solution.py:224
  76.0 2.7 %collective-permute-done.10 = bf16[36,2432]{1,0:T(8,128)(2,1)} collective-permute-done((bf16[36,2432]{1,0:T(8,128)(2,1)S(1)}, bf16[36,2432]{1,0:T(8,128)(2,1)}, u32[]{:S(2)}, u32[]{:S(2)}) %collective-permute-start.10) | collective-permute-done | bytes 175136 | tf_op jit(solution)/shard_map/ppermute | solution.py:107
  78.7 4.2 %collective-permute-done.11 = bf16[36,2432]{1,0:T(8,128)(2,1)} collective-permute-done((bf16[36,2432]{1,0:T(8,128)(2,1)}, bf16[36,2432]{1,0:T(8,128)(2,1)}, u32[]{:S(2)}, u32[]{:S(2)}) %collective-permute-start.11) | collective-permute-done | bytes 175136 | tf_op jit(solution)/shard_map/ppermute | solution.py:107
  82.9 4.2 %collective-permute-done.12 = bf16[36,2432]{1,0:T(8,128)(2,1)} collective-permute-done((bf16[36,2432]{1,0:T(8,128)(2,1)}, bf16[36,2432]{1,0:T(8,128)(2,1)}, u32[]{:S(2)}, u32[]{:S(2)}) %collective-permute-start.12) | collective-permute-done | bytes 175136 | tf_op jit(solution)/shard_map/ppermute | solution.py:107
  97.4 2.6 %convolution_convert_fusion = bf16[288,384]{1,0:T(8,128)(2,1)S(1)} fusion(bf16[288,2432]{1,0:T(8,128)(2,1)S(1)} %bitcast.145, bf16[2432,384]{1,0:T(8,128)(2,1)} %fusion.7), kind=kOutput, calls=%fused_computation.29 | convolution fusion | flops 538030080 | bytes 3489792 | tf_op jit(solution)/shard_map/dot_general | solution.py:235
  100.9 3.0 %convolution_convert_fusion.2 = bf16[288,384]{1,0:T(8,128)(2,1)} fusion(bf16[288,2432]{1,0:T(8,128)(2,1)} %bitcast.146, bf16[2432,384]{1,0:T(8,128)(2,1)S(1)} %copy-done.5), kind=kOutput, calls=%fused_computation.31 | convolution fusion | flops 538030080 | bytes 3489792 | tf_op jit(solution)/shard_map/dot_general | solution.py:235
  108.8 2.3 %convolution_convert_fusion.1 = bf16[288,384]{1,0:T(8,128)(2,1)S(1)} fusion(bf16[288,2432]{1,0:T(8,128)(2,1)} %bitcast.147, bf16[2432,384]{1,0:T(8,128)(2,1)S(1)} %copy-done.7), kind=kOutput, calls=%fused_computation.30 | convolution fusion | flops 538030080 | bytes 3489792 | tf_op jit(solution)/shard_map/dot_general | solution.py:235
  111.2 15.5 %collective-permute-done.18 = bf16[384,2432]{1,0:T(8,128)(2,1)} collective-permute-done((bf16[384,2432]{1,0:T(8,128)(2,1)}, bf16[384,2432]{1,0:T(8,128)(2,1)}, u32[]{:S(2)}, u32[]{:S(2)}) %collective-permute-start.18) | collective-permute-done | bytes 1867808 | tf_op jit(solution)/shard_map/ppermute | solution.py:107
  126.9 2.4 %fusion = (f32[6,576]{1,0:T(8,128)S(1)}, f32[6,576,660]{1,2,0:T(8,128)S(1)}) fusion(pred[660]{0:T(1024)(128)(4,1)S(1)} %concatenate.75, bf16[576,6,64]{0,2,1:T(8,128)(2,1)S(1)} %bitcast.144, bf16[660,6,64]{0,2,1:T(8,128)(2,1)S(1)} %concatenate.83), kind=kOutput, calls=%fused_computation.2 | convolution fusion | flops 298802304 | bytes 10087572 | tf_op jit(solution)/shard_map/ihe,nhe->hin/dot_general | solution.py:257
  131.7 2.6 %divide_convert_fusion = bf16[576,6,64]{0,2,1:T(8,128)(2,1)S(1)} fusion(bf16[660,6,64]{0,2,1:T(8,128)(2,1)S(1)} %copy-done.10, f32[6,576,660]{1,2,0:T(8,128)S(1)} %get-tuple-element.68, f32[6,576]{1,0:T(8,128)S(1)} %get-tuple-element.67, pred[660]{0:T(1024)(128)(4,1)S(1)} %concatenate.75, f32[576,6]{0,1:T(8,128)S(1)} %bitcast.169), kind=kOutput, calls=%fused_computation.43 | convolution fusion | flops 301529088 | bytes 10101396 | tf_op jit(solution)/shard_map/hin,nhe->ihe/dot_general | solution.py:269
  138.3 4.9 %collective-permute-start.19 = (bf16[144,384]{1,0:T(8,128)(2,1)S(1)}, bf16[144,384]{1,0:T(8,128)(2,1)S(1)}, u32[]{:S(2)}, u32[]{:S(2)}) collective-permute-start(bf16[144,384]{1,0:T(8,128)(2,1)S(1)} %squeeze.111), channel_id=1, source_target_pairs={{0,12},{4,0},{8,4},{12,8},{1,13},{5,1},{9,5},{13,9},{2,14},{6,2},{... | collective-permute-start | bytes 331784 | tf_op jit(solution)/shard_map/ppermute | solution.py:122
  146.8 7.2 %collective-permute-done.20 = bf16[144,384]{1,0:T(8,128)(2,1)S(1)} collective-permute-done((bf16[144,384]{1,0:T(8,128)(2,1)S(1)}, bf16[144,384]{1,0:T(8,128)(2,1)S(1)}, u32[]{:S(2)}, u32[]{:S(2)}) %collective-permute-start.20) | collective-permute-done | bytes 110624 | tf_op jit(solution)/shard_map/ppermute | solution.py:122
  156.9 3.3 %collective-permute-done.24 = bf16[144,384]{1,0:T(8,128)(2,1)S(1)} collective-permute-done((bf16[144,384]{1,0:T(8,128)(2,1)S(1)}, bf16[144,384]{1,0:T(8,128)(2,1)S(1)}, u32[]{:S(2)}, u32[]{:S(2)}) %collective-permute-start.24) | collective-permute-done | bytes 110624 | tf_op jit(solution)/shard_map/ppermute | solution.py:107
  160.3 2.3 %collective-permute-done.25 = bf16[144,384]{1,0:T(8,128)(2,1)S(1)} collective-permute-done((bf16[144,384]{1,0:T(8,128)(2,1)S(1)}, bf16[144,384]{1,0:T(8,128)(2,1)S(1)}, u32[]{:S(2)}, u32[]{:S(2)}) %collective-permute-start.25) | collective-permute-done | bytes 110624 | tf_op jit(solution)/shard_map/ppermute | solution.py:107
  167.1 3.4 %fusion.11 = f32[2,144,2432]{2,1,0:T(8,128)S(1)} fusion(bf16[768,2432]{1,0:T(8,128)(2,1)} %all-gather.3.cloned.1.call-done, bf16[2,144,384]{2,1,0:T(8,128)(2,1)S(1)} %get-tuple-element.26, bf16[2,144,384]{2,1,0:T(8,128)(2,1)S(1)} %get-tuple-element.25), kind=kOutput, calls=%fused_computation.15 | convolution fusion | flops 1076723712 | bytes 6979584 | tf_op jit(solution)/shard_map/sin,nd->sid/dot_general | solution.py:288
  170.5 3.7 %fusion.9 = f32[2,144,2432]{2,1,0:T(8,128)S(1)} fusion(bf16[768,2432]{1,0:T(8,128)(2,1)} %all-gather.5.cloned.1.call-done, bf16[2,144,384]{2,1,0:T(8,128)(2,1)} %get-tuple-element.24, bf16[2,144,384]{2,1,0:T(8,128)(2,1)} %get-tuple-element.23), kind=kOutput, calls=%fused_computation.13 | convolution fusion | flops 1076723712 | bytes 6979584 | tf_op jit(solution)/shard_map/sin,nd->sid/dot_general | solution.py:290
  (175 shorter events, 66.5 us)
Async XLA Ops:
  6.5 160.5 %all-gather.3.cloned.1.call-start = ((), (), s32[]{:S(2)}) async-start(), calls=%async_computation | async-start | bytes 5603328 | tf_op jit(solution)/shard_map/all_gather | solution.py:243
  12.4 26.1 %collective-permute-start.5 = (bf16[16,3200]{1,0:T(8,128)(2,1)}, bf16[16,3200]{1,0:T(8,128)(2,1)S(1)}, u32[]{:S(2)}, u32[]{:S(2)}) collective-permute-start(bf16[16,3200]{1,0:T(8,128)(2,1)} %get-tuple-element.50), channel_id=1, source_target_pairs={{0,4},{4,8},{8,12},{12,0},{1,5},{5,9},{9,13},{13,1},{2,6},{6,10},{... | collective-permute-start | bytes 307208 | tf_op jit(solution)/shard_map/ppermute | solution.py:122
  15.4 23.0 %collective-permute-start.6 = (bf16[16,3200]{1,0:T(8,128)(2,1)}, bf16[16,3200]{1,0:T(8,128)(2,1)}, u32[]{:S(2)}, u32[]{:S(2)}) collective-permute-start(bf16[16,3200]{1,0:T(8,128)(2,1)} %get-tuple-element.50), channel_id=1, source_target_pairs={{0,8},{4,12},{8,0},{12,4},{1,9},{5,13},{9,1},{13,5},{2,10},{6,14},... | collective-permute-start | bytes 307208 | tf_op jit(solution)/shard_map/ppermute | solution.py:122
  18.0 20.4 %collective-permute-start.7 = (bf16[16,3200]{1,0:T(8,128)(2,1)}, bf16[16,3200]{1,0:T(8,128)(2,1)}, u32[]{:S(2)}, u32[]{:S(2)}) collective-permute-start(bf16[16,3200]{1,0:T(8,128)(2,1)} %get-tuple-element.50), channel_id=1, source_target_pairs={{0,12},{4,0},{8,4},{12,8},{1,13},{5,1},{9,5},{13,9},{2,14},{6,2},{... | collective-permute-start | bytes 307208 | tf_op jit(solution)/shard_map/ppermute | solution.py:122
  22.2 21.9 %collective-permute-start = (bf16[2,36,2432]{2,1,0:T(8,128)(2,1)S(1)}, bf16[2,36,2432]{2,1,0:T(8,128)(2,1)S(1)}, u32[]{:S(2)}, u32[]{:S(2)}) collective-permute-start(bf16[2,36,2432]{2,1,0:T(8,128)(2,1)S(1)} %constant_dynamic-slice_fusion.5), channel_id=1, source_target_pairs={{0,1},{1,0},{2,3},{3,2},{4,5},{5,4},{6,7},{7,6},{8,9},{9,8},{10,11... | collective-permute-start | bytes 1050632 | tf_op jit(solution)/shard_map/ppermute | solution.py:107
  23.0 147.5 %all-gather.5.cloned.1.call-start = ((), (), s32[]{:S(2)}) async-start(), calls=%async_computation.1 | async-start | bytes 5603328 | tf_op jit(solution)/shard_map/all_gather | solution.py:244
  44.6 9.8 %collective-permute-start.1 = (bf16[36,2432]{1,0:T(8,128)(2,1)S(1)}, bf16[36,2432]{1,0:T(8,128)(2,1)S(1)}, u32[]{:S(2)}, u32[]{:S(2)}) collective-permute-start(bf16[36,2432]{1,0:T(8,128)(2,1)S(1)} %get-tuple-element.30), channel_id=1, source_target_pairs={{0,4},{4,8},{8,12},{12,0},{1,5},{5,9},{9,13},{13,1},{2,6},{6,10},{... | collective-permute-start | bytes 525320 | tf_op jit(solution)/shard_map/ppermute | solution.py:122
  45.6 15.6 %collective-permute-start.2 = (bf16[36,2432]{1,0:T(8,128)(2,1)S(1)}, bf16[36,2432]{1,0:T(8,128)(2,1)}, u32[]{:S(2)}, u32[]{:S(2)}) collective-permute-start(bf16[36,2432]{1,0:T(8,128)(2,1)S(1)} %get-tuple-element.31), channel_id=1, source_target_pairs={{0,8},{4,12},{8,0},{12,4},{1,9},{5,13},{9,1},{13,5},{2,10},{6,14},... | collective-permute-start | bytes 525320 | tf_op jit(solution)/shard_map/ppermute | solution.py:122
  47.0 14.2 %collective-permute-start.3 = (bf16[36,2432]{1,0:T(8,128)(2,1)S(1)}, bf16[36,2432]{1,0:T(8,128)(2,1)}, u32[]{:S(2)}, u32[]{:S(2)}) collective-permute-start(bf16[36,2432]{1,0:T(8,128)(2,1)S(1)} %get-tuple-element.32), channel_id=1, source_target_pairs={{0,12},{4,0},{8,4},{12,8},{1,13},{5,1},{9,5},{13,9},{2,14},{6,2},{... | collective-permute-start | bytes 525320 | tf_op jit(solution)/shard_map/ppermute | solution.py:122
  63.3 26.3 %collective-permute-start.4 = (bf16[144,2432]{1,0:T(8,128)(2,1)}, bf16[144,2432]{1,0:T(8,128)(2,1)S(1)}, u32[]{:S(2)}, u32[]{:S(2)}) collective-permute-start(bf16[144,2432]{1,0:T(8,128)(2,1)} %reshape.121), channel_id=1, source_target_pairs={{0,1},{1,0},{2,3},{3,2},{4,5},{5,4},{6,7},{7,6},{8,9},{9,8},{10,11... | collective-permute-start | bytes 2101256 | tf_op jit(solution)/shard_map/ppermute | solution.py:107
  66.8 7.8 %collective-permute-start.9 = (bf16[36,2432]{1,0:T(8,128)(2,1)S(1)}, bf16[36,2432]{1,0:T(8,128)(2,1)}, u32[]{:S(2)}, u32[]{:S(2)}) collective-permute-start(bf16[36,2432]{1,0:T(8,128)(2,1)S(1)} %bitcast.155), channel_id=1, source_target_pairs={{0,2},{2,0},{1,3},{3,1},{4,6},{6,4},{5,7},{7,5},{8,10},{10,8},{9,1... | collective-permute-start | bytes 525320 | tf_op jit(solution)/shard_map/ppermute | solution.py:107
  68.3 10.4 %collective-permute-start.10 = (bf16[36,2432]{1,0:T(8,128)(2,1)S(1)}, bf16[36,2432]{1,0:T(8,128)(2,1)}, u32[]{:S(2)}, u32[]{:S(2)}) collective-permute-start(bf16[36,2432]{1,0:T(8,128)(2,1)S(1)} %collective-permute-done.1), channel_id=1, source_target_pairs={{0,2},{2,0},{1,3},{3,1},{4,6},{6,4},{5,7},{7,5},{8,10},{10,8},{9,1... | collective-permute-start | bytes 525320 | tf_op jit(solution)/shard_map/ppermute | solution.py:107
  68.8 14.1 %collective-permute-start.11 = (bf16[36,2432]{1,0:T(8,128)(2,1)}, bf16[36,2432]{1,0:T(8,128)(2,1)}, u32[]{:S(2)}, u32[]{:S(2)}) collective-permute-start(bf16[36,2432]{1,0:T(8,128)(2,1)} %collective-permute-done.2), channel_id=1, source_target_pairs={{0,2},{2,0},{1,3},{3,1},{4,6},{6,4},{5,7},{7,5},{8,10},{10,8},{9,1... | collective-permute-start | bytes 525320 | tf_op jit(solution)/shard_map/ppermute | solution.py:107
  70.3 16.7 %collective-permute-start.12 = (bf16[36,2432]{1,0:T(8,128)(2,1)}, bf16[36,2432]{1,0:T(8,128)(2,1)}, u32[]{:S(2)}, u32[]{:S(2)}) collective-permute-start(bf16[36,2432]{1,0:T(8,128)(2,1)} %collective-permute-done.3), channel_id=1, source_target_pairs={{0,2},{2,0},{1,3},{3,1},{4,6},{6,4},{5,7},{7,5},{8,10},{10,8},{9,1... | collective-permute-start | bytes 525320 | tf_op jit(solution)/shard_map/ppermute | solution.py:107
  74.5 52.1 %collective-permute-start.18 = (bf16[384,2432]{1,0:T(8,128)(2,1)}, bf16[384,2432]{1,0:T(8,128)(2,1)}, u32[]{:S(2)}, u32[]{:S(2)}) collective-permute-start(bf16[384,2432]{1,0:T(8,128)(2,1)} %param.16), channel_id=1, source_target_pairs={{0,2},{2,0},{1,3},{3,1},{4,6},{6,4},{5,7},{7,5},{8,10},{10,8},{9,1... | collective-permute-start | bytes 5603336 | tf_op jit(solution)/shard_map/ppermute | solution.py:107
  89.5 6.6 %collective-permute-start.13 = (bf16[144,2432]{1,0:T(8,128)(2,1)}, bf16[144,2432]{1,0:T(8,128)(2,1)S(1)}, u32[]{:S(2)}, u32[]{:S(2)}) collective-permute-start(bf16[144,2432]{1,0:T(8,128)(2,1)} %reshape.123), channel_id=1, source_target_pairs={{0,1},{1,0},{2,3},{3,2},{4,5},{5,4},{6,7},{7,6},{8,9},{9,8},{10,11... | collective-permute-start | bytes 2101256 | tf_op jit(solution)/shard_map/ppermute | solution.py:107
  136.7 20.2 %collective-permute-start.23 = (bf16[144,384]{1,0:T(8,128)(2,1)S(1)}, bf16[144,384]{1,0:T(8,128)(2,1)S(1)}, u32[]{:S(2)}, u32[]{:S(2)}) collective-permute-start(bf16[144,384]{1,0:T(8,128)(2,1)S(1)} %squeeze.114), channel_id=1, source_target_pairs={{0,2},{2,0},{1,3},{3,1},{4,6},{6,4},{5,7},{7,5},{8,10},{10,8},{9,1... | collective-permute-start | bytes 331784 | tf_op jit(solution)/shard_map/ppermute | solution.py:107
  138.3 8.5 %collective-permute-start.19 = (bf16[144,384]{1,0:T(8,128)(2,1)S(1)}, bf16[144,384]{1,0:T(8,128)(2,1)S(1)}, u32[]{:S(2)}, u32[]{:S(2)}) collective-permute-start(bf16[144,384]{1,0:T(8,128)(2,1)S(1)} %squeeze.111), channel_id=1, source_target_pairs={{0,12},{4,0},{8,4},{12,8},{1,13},{5,1},{9,5},{13,9},{2,14},{6,2},{... | collective-permute-start | bytes 331784 | tf_op jit(solution)/shard_map/ppermute | solution.py:122
  143.3 10.7 %collective-permute-start.20 = (bf16[144,384]{1,0:T(8,128)(2,1)S(1)}, bf16[144,384]{1,0:T(8,128)(2,1)S(1)}, u32[]{:S(2)}, u32[]{:S(2)}) collective-permute-start(bf16[144,384]{1,0:T(8,128)(2,1)S(1)} %squeeze.112), channel_id=1, source_target_pairs={{0,8},{4,12},{8,0},{12,4},{1,9},{5,13},{9,1},{13,5},{2,10},{6,14},... | collective-permute-start | bytes 331784 | tf_op jit(solution)/shard_map/ppermute | solution.py:122
  144.6 9.4 %collective-permute-start.21 = (bf16[144,384]{1,0:T(8,128)(2,1)S(1)}, bf16[144,384]{1,0:T(8,128)(2,1)S(1)}, u32[]{:S(2)}, u32[]{:S(2)}) collective-permute-start(bf16[144,384]{1,0:T(8,128)(2,1)S(1)} %squeeze.113), channel_id=1, source_target_pairs={{0,4},{4,8},{8,12},{12,0},{1,5},{5,9},{9,13},{13,1},{2,6},{6,10},{... | collective-permute-start | bytes 331784 | tf_op jit(solution)/shard_map/ppermute | solution.py:122
  154.2 10.5 %collective-permute-start.22 = (bf16[2,144,384]{2,1,0:T(8,128)(2,1)S(1)}, bf16[2,144,384]{2,1,0:T(8,128)(2,1)S(1)}, u32[]{:S(2)}, u32[]{:S(2)}) collective-permute-start(bf16[2,144,384]{2,1,0:T(8,128)(2,1)S(1)} %constant_dynamic-slice_fusion.1), channel_id=1, source_target_pairs={{0,1},{1,0},{2,3},{3,2},{4,5},{5,4},{6,7},{7,6},{8,9},{9,8},{10,11... | collective-permute-start | bytes 663560 | tf_op jit(solution)/shard_map/ppermute | solution.py:107
  154.3 5.9 %collective-permute-start.24 = (bf16[144,384]{1,0:T(8,128)(2,1)S(1)}, bf16[144,384]{1,0:T(8,128)(2,1)S(1)}, u32[]{:S(2)}, u32[]{:S(2)}) collective-permute-start(bf16[144,384]{1,0:T(8,128)(2,1)S(1)} %collective-permute-done.19), channel_id=1, source_target_pairs={{0,2},{2,0},{1,3},{3,1},{4,6},{6,4},{5,7},{7,5},{8,10},{10,8},{9,1... | collective-permute-start | bytes 331784 | tf_op jit(solution)/shard_map/ppermute | solution.py:107
  154.9 7.7 %collective-permute-start.25 = (bf16[144,384]{1,0:T(8,128)(2,1)S(1)}, bf16[144,384]{1,0:T(8,128)(2,1)S(1)}, u32[]{:S(2)}, u32[]{:S(2)}) collective-permute-start(bf16[144,384]{1,0:T(8,128)(2,1)S(1)} %collective-permute-done.20), channel_id=1, source_target_pairs={{0,2},{2,0},{1,3},{3,1},{4,6},{6,4},{5,7},{7,5},{8,10},{10,8},{9,1... | collective-permute-start | bytes 331784 | tf_op jit(solution)/shard_map/ppermute | solution.py:107
  156.4 8.1 %collective-permute-start.26 = (bf16[144,384]{1,0:T(8,128)(2,1)S(1)}, bf16[144,384]{1,0:T(8,128)(2,1)S(1)}, u32[]{:S(2)}, u32[]{:S(2)}) collective-permute-start(bf16[144,384]{1,0:T(8,128)(2,1)S(1)} %collective-permute-done.21), channel_id=1, source_target_pairs={{0,2},{2,0},{1,3},{3,1},{4,6},{6,4},{5,7},{7,5},{8,10},{10,8},{9,1... | collective-permute-start | bytes 331784 | tf_op jit(solution)/shard_map/ppermute | solution.py:107
  (21 other events, 93.5 us)
Sparse Core Ops, SparseCore 0:
  23.1 11.3 all-gather.2
  145.1 13.5 all-gather.4

commit v7 on v4

--- a/solution.py
+++ b/solution.py
@@ -118,6 +118,10 @@
     return jnp.concatenate([first, second], axis=concat_axis)
 
 
+def shifted(block, step, count):
+    return lax.ppermute(block, "seq", [(i, (i + step) % count) for i in range(count)])
+
+
 def body_by_sample(
     image_token_states,
     timestep,
@@ -147,7 +151,7 @@
     half_rank = up_mine.shape[0] // 2
     down_mine = lax.dynamic_slice_in_dim(adapter_down_factors[0], at_core * half_rank, half_rank, 0)
     packed = jnp.concatenate([down_mine, up_mine[:half_rank], up_mine[half_rank:]], axis=1)
-    packed = lax.all_gather(packed, "seq", axis=0)
+    packed = jnp.stack([packed] + [shifted(packed, k, n_seq) for k in range(1, n_seq)])
 
     length_row = jnp.broadcast_to(
         prompt_token_length.astype(jnp.bfloat16)[:, None, None, None],
@@ -192,7 +196,10 @@
     piece_both = flip(piece_mp, "batch")
     merged = []
     chosen = jnp.stack(
-        [lax.dynamic_index_in_dim(packed, owner[which], 0, keepdims=False) for which in range(3)]
+        [
+            lax.dynamic_index_in_dim(packed, (at_seq - owner[which]) % n_seq, 0, keepdims=False)
+            for which in range(3)
+        ]
     )
     down_mine = chosen[:, :, :width]
     down_came = flip(down_mine, "batch")

time: 163 us -> 152 us (0.933)
  blocking collectives: 14.9 us -> 0 us
  starting transfers between devices: 14 us -> 18.8 us
  between operations: 22.4 us -> 18.7 us
    all_gather x1 -> x0, blocking collectives: 14.9 us -> none  [body_by_sample(): packed = lax.all_gather(packed, 'seq', axis=0)]
    ppermute x0 -> x3, starting transfers between devices: none -> 7.01 us  [shifted(): lax.ppermute(block, 'seq', [(i, (i + step) % count) for i in range(count)])]
    all_to_all x1, starting transfers between devices: 5.37 us -> 3.51 us  [body_by_sample(): piece = lax.all_to_all(piece, 'seq', 0, 0, tiled=True)]
    unnamed x44 -> x36, local copies, waits for them, and re-layouts: 4.42 us -> 3.72 us
  transfers between devices with their start and end apart: 13 -> 16, of which waited for: 6 -> 6; matrix products, arithmetic and copies ran while one was open for 32% -> 33% of each run, Pallas kernels for 0% -> 0%
where the time goes in v7:
time: 152 us; the launch traced here: 151 us
  waiting for transfers between devices  52.9 us (35%)
  matrix products  33.2 us (22%)
  starting transfers between devices  18.8 us (12%)
  between operations  18.7 us (12%)
  local copies, waits for them, and re-layouts  18.5 us (12%)
  other arithmetic  8.86 us (6%)
    ppermute x9, waiting for transfers between devices, flip(): return lax.ppermute(block, axis, [(0, 1), (1, 0)])  25.7 us
    all_to_all x1, waiting for transfers between devices, body_by_sample(): lax.all_to_all(attn.reshape(n_seq, img_rows, columns), 'seq', 0, 0, tiled...  13.6 us
    all_to_all x1, waiting for transfers between devices, body_by_sample(): piece = lax.all_to_all(piece, 'seq', 0, 0, tiled=True)  13.4 us
    dot_general x3, matrix products, body_by_sample(): jnp.einsum('rd,rn->dn', down_all[which], up_all[which], preferred_element...  10.3 us
    dot_general x6, matrix products, body_by_sample(): jnp.dot(rows, m, preferred_element_type=jnp.float32).astype(jnp.bfloat16)  9.54 us
    ppermute x3, starting transfers between devices, shifted(): lax.ppermute(block, 'seq', [(i, (i + step) % count) for i in range(count)])  7.01 us
    ppermute x9, starting transfers between devices, flip(): return lax.ppermute(block, axis, [(0, 1), (1, 0)])  4.56 us
    unnamed x36, local copies, waits for them, and re-layouts  3.72 us
  transfers between devices with their start and end apart: 16, of which 6 were waited for; matrix products, arithmetic and copies ran while one was open for 33% of the time, Pallas kernels for 0%

profile of v7, /device:TPU:0, one launch (start us, length us, event | category | flops | bytes accessed | tf_op | source)
XLA Modules:
  0.0 150.9 jit_solution(3689466150432660584)
XLA Ops:
  6.6 1.5 fusion.65
  11.8 3.1 %collective-permute-start.3 = (bf16[16,3200]{1,0:T(8,128)(2,1)S(1)}, bf16[16,3200]{1,0:T(8,128)(2,1)S(1)}, u32[]{:S(2)}, u32[]{:S(2)}) collective-permute-start(bf16[16,3200]{1,0:T(8,128)(2,1)S(1)} %get-tuple-element.38), channel_id=1, source_target_pairs={{0,4},{4,8},{8,12},{12,0},{1,5},{5,9},{9,13},{13,1},{2,6},{6,10},{... | collective-permute-start | bytes 307208 | tf_op jit(solution)/shard_map/ppermute | solution.py:122
  14.9 2.6 %collective-permute-start.4 = (bf16[16,3200]{1,0:T(8,128)(2,1)S(1)}, bf16[16,3200]{1,0:T(8,128)(2,1)S(1)}, u32[]{:S(2)}, u32[]{:S(2)}) collective-permute-start(bf16[16,3200]{1,0:T(8,128)(2,1)S(1)} %get-tuple-element.38), channel_id=1, source_target_pairs={{0,8},{4,12},{8,0},{12,4},{1,9},{5,13},{9,1},{13,5},{2,10},{6,14},... | collective-permute-start | bytes 307208 | tf_op jit(solution)/shard_map/ppermute | solution.py:122
  17.5 1.3 collective-permute-start.5
  18.8 1.5 collective-permute-start.9
  27.9 3.5 %all-to-all-start = ((bf16[4,43,2432]{2,1,0:T(8,128)(2,1)}), bf16[4,43,2432]{2,1,0:T(8,128)(2,1)S(1)}, u32[]{:S(2)}, u32[]{:S(2)}) async-start(bf16[4,43,2432]{2,1,0:T(8,128)(2,1)} %pad_maximum_fusion), calls=%async_computation | async-start | bytes 1867776 | tf_op jit(solution)/shard_map/all_to_all | solution.py:190
  31.8 3.4 %fusion.8 = bf16[2432,384]{1,0:T(8,128)(2,1)} fusion(bf16[2432,3,384]{2,0,1:T(8,128)(2,1)} %param.15, bf16[3,16,2432]{2,1,0:T(8,128)(2,1)S(1)} %get-tuple-element.27, bf16[3,16,2432]{2,1,0:T(8,128)(2,1)S(1)} %get-tuple-element.28, bf16[3,32,384]{2,1,0:T(8,128)(2,1)S(1)} %fusion.46), kind=kOutput, calls=%fused_computation.12 | convolution fusion | flops 62881792 | bytes 4227072 | tf_op jit(solution)/shard_map/rd,rn->dn/dot_general | solution.py:217
  35.2 3.4 %fusion.7 = bf16[2432,384]{1,0:T(8,128)(2,1)} fusion(bf16[2432,3,384]{2,0,1:T(8,128)(2,1)} %param.15, bf16[3,16,2432]{2,1,0:T(8,128)(2,1)S(1)} %get-tuple-element.28, bf16[3,16,2432]{2,1,0:T(8,128)(2,1)S(1)} %get-tuple-element.27, bf16[3,32,384]{2,1,0:T(8,128)(2,1)S(1)} %fusion.46), kind=kOutput, calls=%fused_computation.11 | convolution fusion | flops 62881792 | bytes 4227072 | tf_op jit(solution)/shard_map/rd,rn->dn/dot_general | solution.py:217
  38.6 3.4 %fusion.6 = bf16[2432,384]{1,0:T(8,128)(2,1)} fusion(bf16[2432,3,384]{2,0,1:T(8,128)(2,1)} %param.15, bf16[3,16,2432]{2,1,0:T(8,128)(2,1)S(1)} %get-tuple-element.28, bf16[3,16,2432]{2,1,0:T(8,128)(2,1)S(1)} %get-tuple-element.27, bf16[3,32,384]{2,1,0:T(8,128)(2,1)S(1)} %fusion.46), kind=kOutput, calls=%fused_computation.10 | convolution fusion | flops 62881792 | bytes 4227072 | tf_op jit(solution)/shard_map/rd,rn->dn/dot_general | solution.py:217
  42.1 13.4 %all-to-all-done = bf16[4,43,2432]{2,1,0:T(8,128)(2,1)S(1)} async-done(((bf16[4,43,2432]{2,1,0:T(8,128)(2,1)}), bf16[4,43,2432]{2,1,0:T(8,128)(2,1)S(1)}, u32[]{:S(2)}, u32[]{:S(2)}) %all-to-all-start) | async-done | bytes 836640 | tf_op jit(solution)/shard_map/all_to_all | solution.py:190
  59.5 16.3 %collective-permute-done.7 = bf16[144,2432]{1,0:T(8,128)(2,1)} collective-permute-done((bf16[144,2432]{1,0:T(8,128)(2,1)S(1)}, bf16[144,2432]{1,0:T(8,128)(2,1)}, u32[]{:S(2)}, u32[]{:S(2)}) %collective-permute-start.7) | collective-permute-done | bytes 700448 | tf_op jit(solution)/shard_map/ppermute | solution.py:107
  87.4 2.9 %convolution_convert_fusion.1 = bf16[288,384]{1,0:T(8,128)(2,1)S(1)} fusion(bf16[288,2432]{1,0:T(8,128)(2,1)} %copy-done.9, bf16[2432,384]{1,0:T(8,128)(2,1)} %fusion.6), kind=kOutput, calls=%fused_computation.28 | convolution fusion | flops 538030080 | bytes 3489792 | tf_op jit(solution)/shard_map/dot_general | solution.py:228
  90.6 3.0 %convolution_convert_fusion.2 = bf16[288,384]{1,0:T(8,128)(2,1)} fusion(bf16[288,2432]{1,0:T(8,128)(2,1)} %copy-done.9, bf16[2432,384]{1,0:T(8,128)(2,1)S(1)} %copy-done.4), kind=kOutput, calls=%fused_computation.29 | convolution fusion | flops 538030080 | bytes 3489792 | tf_op jit(solution)/shard_map/dot_general | solution.py:228
  94.9 3.4 %fusion = (f32[6,576]{1,0:T(8,128)S(1)}, f32[6,576,660]{1,2,0:T(8,128)S(1)}) fusion(pred[660]{0:T(1024)(128)(4,1)S(1)} %iota_compare_fusion, bf16[576,6,64]{0,2,1:T(8,128)(2,1)S(1)} %bitcast.92, bf16[84,6,64]{0,2,1:T(8,128)(2,1)S(1)} %copy.38, bf16[288,6,64]{0,2,1:T(8,128)(2,1)S(1)} %bitcast.95, bf16[288,6,64]{0,2,1:T(8,128)(2,1)S(1)} %bitcast.94), kind=kOutput, calls=%fused_computation.2 | convolution fusion | flops 300322944 | bytes 10087572 | tf_op jit(solution)/shard_map/ihe,nhe->hin/dot_general | solution.py:247
  98.3 2.5 %fusion.1 = f32[6,576]{1,0:T(8,128)S(1)} fusion(f32[6,576,660]{1,2,0:T(8,128)S(1)} %get-tuple-element.48, f32[6,576]{1,0:T(8,128)S(1)} %get-tuple-element.47, pred[660]{0:T(1024)(128)(4,1)S(1)} %iota_compare_fusion), kind=kLoop, calls=%fused_computation.3 | loop fusion | flops 9120384 | bytes 9152148 | tf_op jit(solution)/shard_map/reduce_sum | solution.py:258
  100.8 2.7 %divide_convert_fusion = bf16[576,6,64]{0,2,1:T(8,128)(2,1)S(1)} fusion(f32[6,576,660]{1,2,0:T(8,128)S(1)} %get-tuple-element.48, f32[6,576]{1,0:T(8,128)S(1)} %get-tuple-element.47, pred[660]{0:T(1024)(128)(4,1)S(1)} %iota_compare_fusion, bf16[84,6,64]{0,2,1:T(8,128)(2,1)S(1)} %copy-done.12, bf16[288,6,64]{0,2,1:T(8,128)(2,1)S(1)} %bitcast.96, ...), kind=kOutput, calls=%fused_computation.33 | convolution fusion | flops 303049728 | bytes 10101396 | tf_op jit(solution)/shard_map/hin,nhe->ihe/dot_general | solution.py:259
  106.8 3.5 %all-to-all-start.1 = ((bf16[4,144,384]{2,1,0:T(8,128)(2,1)}), bf16[4,144,384]{2,1,0:T(8,128)(2,1)S(1)}, u32[]{:S(2)}, u32[]{:S(2)}) async-start(bf16[4,144,384]{2,1,0:T(8,128)(2,1)} %copy.41), calls=%async_computation.1 | async-start | bytes 884736 | tf_op jit(solution)/shard_map/all_to_all | solution.py:271
  110.2 13.6 %all-to-all-done.1 = bf16[4,144,384]{2,1,0:T(8,128)(2,1)S(1)} async-done(((bf16[4,144,384]{2,1,0:T(8,128)(2,1)}), bf16[4,144,384]{2,1,0:T(8,128)(2,1)S(1)}, u32[]{:S(2)}, u32[]{:S(2)}) %all-to-all-start.1) | async-done | bytes 442400 | tf_op jit(solution)/shard_map/all_to_all | solution.py:271
  124.0 1.5 collective-permute-done.10
  126.3 1.5 collective-permute-start.11
  127.8 3.4 %fusion.11 = f32[2,144,2432]{2,1,0:T(8,128)S(1)} fusion(bf16[768,2432]{1,0:T(8,128)(2,1)} %all-gather.3.cloned.1.call-done, bf16[2,144,384]{2,1,0:T(8,128)(2,1)S(1)} %get-tuple-element.26, bf16[2,144,384]{2,1,0:T(8,128)(2,1)S(1)} %get-tuple-element.25), kind=kOutput, calls=%fused_computation.15 | convolution fusion | flops 1076723712 | bytes 6979584 | tf_op jit(solution)/shard_map/sin,nd->sid/dot_general | solution.py:274
  131.2 7.7 %collective-permute-done.11 = bf16[2,144,768]{2,1,0:T(8,128)(2,1)} collective-permute-done((bf16[2,144,768]{2,1,0:T(8,128)(2,1)}, bf16[2,144,768]{2,1,0:T(8,128)(2,1)}, u32[]{:S(2)}, u32[]{:S(2)}) %collective-permute-start.11) | collective-permute-done | bytes 442400 | tf_op jit(solution)/shard_map/ppermute | solution.py:107
  138.8 3.6 %fusion.9 = f32[2,144,2432]{2,1,0:T(8,128)S(1)} fusion(bf16[2,144,768]{2,1,0:T(8,128)(2,1)} %collective-permute-done.11, bf16[768,2432]{1,0:T(8,128)(2,1)} %all-gather.5.cloned.1.call-done), kind=kOutput, calls=%fused_computation.13 | convolution fusion | flops 1075838976 | bytes 6979584 | tf_op jit(solution)/shard_map/sin,nd->sid/dot_general | solution.py:276
  142.5 1.6 %add_convert_fusion = bf16[2,144,2432]{2,1,0:T(8,128)(2,1)} fusion(f32[2,144,2432]{2,1,0:T(8,128)S(1)} %fusion.11, f32[2,144,2432]{2,1,0:T(8,128)S(1)} %fusion.9, bf16[2,144,2432]{2,1,0:T(8,128)(2,1)S(1)} %copy-done.3, f32[2,2432]{1,0:T(2,128)S(1)} %copy-done.13), kind=kLoop, calls=%fused_computation.17 | loop fusion | flops 3502080 | bytes 8424448 | tf_op jit(solution)/shard_map/convert_element_type | solution.py:279
  (121 shorter events, 28.0 us)
Async XLA Ops:
  6.5 14.6 %copy-start = (f32[10,3,2432]{2,1,0:T(4,128)S(1)}, f32[10,3,2432]{2,1,0:T(4,128)}, u32[]{:S(2)}) copy-start(f32[10,3,2432]{2,1,0:T(4,128)} %param.13) | copy-start | bytes 875524
  6.5 13.8 %copy-start.15 = (s32[2]{0:T(128)S(1)}, s32[2]{0:T(128)}, u32[]{:S(2)}) copy-start(s32[2]{0:T(128)} %param.12) | copy-start | bytes 28
  6.5 13.9 %copy-start.8 = (bf16[2,2,21,768]{3,1,2,0:T(2,128)(2,1)S(1)}, bf16[2,2,21,768]{3,1,2,0:T(2,128)(2,1)}, u32[]{:S(2)}) copy-start(bf16[2,2,21,768]{3,1,2,0:T(2,128)(2,1)} %param.14) | copy-start | bytes 387076
  6.5 14.0 %copy-start.2 = (bf16[2,144,2432]{2,1,0:T(8,128)(2,1)S(1)}, bf16[2,144,2432]{2,1,0:T(8,128)(2,1)}, u32[]{:S(2)}) copy-start(bf16[2,144,2432]{2,1,0:T(8,128)(2,1)} %param.10) | copy-start | bytes 4202500
  6.5 121.3 %all-gather.3.cloned.1.call-start = ((), (), s32[]{:S(2)}) async-start(), calls=%async_computation.2 | async-start | bytes 5603328 | tf_op jit(solution)/shard_map/all_gather | solution.py:236
  11.8 9.4 %copy-start.14 = (s32[2]{0:T(128)S(1)}, s32[2]{0:T(128)}, u32[]{:S(2)}) copy-start(s32[2]{0:T(128)} %param.11) | copy-start | bytes 28
  11.8 14.2 %collective-permute-start.3 = (bf16[16,3200]{1,0:T(8,128)(2,1)S(1)}, bf16[16,3200]{1,0:T(8,128)(2,1)S(1)}, u32[]{:S(2)}, u32[]{:S(2)}) collective-permute-start(bf16[16,3200]{1,0:T(8,128)(2,1)S(1)} %get-tuple-element.38), channel_id=1, source_target_pairs={{0,4},{4,8},{8,12},{12,0},{1,5},{5,9},{9,13},{13,1},{2,6},{6,10},{... | collective-permute-start | bytes 307208 | tf_op jit(solution)/shard_map/ppermute | solution.py:122
  14.9 11.2 %collective-permute-start.4 = (bf16[16,3200]{1,0:T(8,128)(2,1)S(1)}, bf16[16,3200]{1,0:T(8,128)(2,1)S(1)}, u32[]{:S(2)}, u32[]{:S(2)}) collective-permute-start(bf16[16,3200]{1,0:T(8,128)(2,1)S(1)} %get-tuple-element.38), channel_id=1, source_target_pairs={{0,8},{4,12},{8,0},{12,4},{1,9},{5,13},{9,1},{13,5},{2,10},{6,14},... | collective-permute-start | bytes 307208 | tf_op jit(solution)/shard_map/ppermute | solution.py:122
  17.5 8.6 %collective-permute-start.5 = (bf16[16,3200]{1,0:T(8,128)(2,1)S(1)}, bf16[16,3200]{1,0:T(8,128)(2,1)S(1)}, u32[]{:S(2)}, u32[]{:S(2)}) collective-permute-start(bf16[16,3200]{1,0:T(8,128)(2,1)S(1)} %get-tuple-element.38), channel_id=1, source_target_pairs={{0,12},{4,0},{8,4},{12,8},{1,13},{5,1},{9,5},{13,9},{2,14},{6,2},{... | collective-permute-start | bytes 307208 | tf_op jit(solution)/shard_map/ppermute | solution.py:122
  18.8 71.6 %collective-permute-start.9 = (bf16[384,2432]{1,0:T(8,128)(2,1)}, bf16[384,2432]{1,0:T(8,128)(2,1)}, u32[]{:S(2)}, u32[]{:S(2)}) collective-permute-start(bf16[384,2432]{1,0:T(8,128)(2,1)} %param.16), channel_id=1, source_target_pairs={{0,2},{2,0},{1,3},{3,1},{4,6},{6,4},{5,7},{7,5},{8,10},{10,8},{9,1... | collective-permute-start | bytes 5603336 | tf_op jit(solution)/shard_map/ppermute | solution.py:107
  20.5 4.3 %collective-permute-start.1 = (bf16[2,2,22,384]{3,1,2,0:T(2,128)(2,1)S(1)}, bf16[2,2,22,384]{3,1,2,0:T(2,128)(2,1)S(1)}, u32[]{:S(2)}, u32[]{:S(2)}) collective-permute-start(bf16[2,2,22,384]{3,1,2,0:T(2,128)(2,1)S(1)} %fusion.47), channel_id=1, source_target_pairs={{0,1},{1,0},{2,3},{3,2},{4,5},{5,4},{6,7},{7,6},{8,9},{9,8},{10,11... | collective-permute-start | bytes 202760 | tf_op jit(solution)/shard_map/ppermute | solution.py:107
  24.8 1.9 %collective-permute-start = (bf16[2,36,2432]{2,1,0:T(8,128)(2,1)S(1)}, bf16[2,36,2432]{2,1,0:T(8,128)(2,1)S(1)}, u32[]{:S(2)}, u32[]{:S(2)}) collective-permute-start(bf16[2,36,2432]{2,1,0:T(8,128)(2,1)S(1)} %constant_dynamic-slice_fusion.4), channel_id=1, source_target_pairs={{0,1},{1,0},{2,3},{3,2},{4,5},{5,4},{6,7},{7,6},{8,9},{9,8},{10,11... | collective-permute-start | bytes 1050632 | tf_op jit(solution)/shard_map/ppermute | solution.py:107
  26.2 5.5 %collective-permute-start.6 = (bf16[3,16,2432]{2,1,0:T(8,128)(2,1)S(1)}, bf16[3,16,2432]{2,1,0:T(8,128)(2,1)S(1)}, u32[]{:S(2)}, u32[]{:S(2)}) collective-permute-start(bf16[3,16,2432]{2,1,0:T(8,128)(2,1)S(1)} %slice.136), channel_id=1, source_target_pairs={{0,1},{1,0},{2,3},{3,2},{4,5},{5,4},{6,7},{7,6},{8,9},{9,8},{10,11... | collective-permute-start | bytes 700424 | tf_op jit(solution)/shard_map/ppermute | solution.py:107
  27.9 27.6 %all-to-all-start = ((bf16[4,43,2432]{2,1,0:T(8,128)(2,1)}), bf16[4,43,2432]{2,1,0:T(8,128)(2,1)S(1)}, u32[]{:S(2)}, u32[]{:S(2)}) async-start(bf16[4,43,2432]{2,1,0:T(8,128)(2,1)} %pad_maximum_fusion), calls=%async_computation | async-start | bytes 1867776 | tf_op jit(solution)/shard_map/all_to_all | solution.py:190
  31.5 107.4 %all-gather.5.cloned.1.call-start = ((), (), s32[]{:S(2)}) async-start(), calls=%async_computation.3 | async-start | bytes 5603328 | tf_op jit(solution)/shard_map/all_gather | solution.py:237
  55.7 20.0 %collective-permute-start.7 = (bf16[144,2432]{1,0:T(8,128)(2,1)S(1)}, bf16[144,2432]{1,0:T(8,128)(2,1)}, u32[]{:S(2)}, u32[]{:S(2)}) collective-permute-start(bf16[144,2432]{1,0:T(8,128)(2,1)S(1)} %reshape.82), channel_id=1, source_target_pairs={{0,2},{2,0},{1,3},{3,1},{4,6},{6,4},{5,7},{7,5},{8,10},{10,8},{9,1... | collective-permute-start | bytes 2101256 | tf_op jit(solution)/shard_map/ppermute | solution.py:107
  56.5 19.3 %collective-permute-start.2 = (bf16[144,2432]{1,0:T(8,128)(2,1)S(1)}, bf16[144,2432]{1,0:T(8,128)(2,1)}, u32[]{:S(2)}, u32[]{:S(2)}) collective-permute-start(bf16[144,2432]{1,0:T(8,128)(2,1)S(1)} %reshape.82), channel_id=1, source_target_pairs={{0,1},{1,0},{2,3},{3,2},{4,5},{5,4},{6,7},{7,6},{8,9},{9,8},{10,11... | collective-permute-start | bytes 2101256 | tf_op jit(solution)/shard_map/ppermute | solution.py:107
  57.3 19.6 %copy-start.4 = (bf16[2432,384]{1,0:T(8,128)(2,1)S(1)}, bf16[2432,384]{1,0:T(8,128)(2,1)}, u32[]{:S(2)}) copy-start(bf16[2432,384]{1,0:T(8,128)(2,1)} %fusion.8) | copy-start | bytes 5603332
  75.7 7.6 %collective-permute-start.8 = (bf16[144,2432]{1,0:T(8,128)(2,1)}, bf16[144,2432]{1,0:T(8,128)(2,1)}, u32[]{:S(2)}, u32[]{:S(2)}) collective-permute-start(bf16[144,2432]{1,0:T(8,128)(2,1)} %collective-permute-done.7), channel_id=1, source_target_pairs={{0,1},{1,0},{2,3},{3,2},{4,5},{5,4},{6,7},{7,6},{8,9},{9,8},{10,11... | collective-permute-start | bytes 2101256 | tf_op jit(solution)/shard_map/ppermute | solution.py:107
  106.8 17.1 %all-to-all-start.1 = ((bf16[4,144,384]{2,1,0:T(8,128)(2,1)}), bf16[4,144,384]{2,1,0:T(8,128)(2,1)S(1)}, u32[]{:S(2)}, u32[]{:S(2)}) async-start(bf16[4,144,384]{2,1,0:T(8,128)(2,1)} %copy.41), calls=%async_computation.1 | async-start | bytes 884736 | tf_op jit(solution)/shard_map/all_to_all | solution.py:271
  123.9 1.5 %collective-permute-start.10 = (bf16[2,144,384]{2,1,0:T(8,128)(2,1)S(1)}, bf16[2,144,384]{2,1,0:T(8,128)(2,1)S(1)}, u32[]{:S(2)}, u32[]{:S(2)}) collective-permute-start(bf16[2,144,384]{2,1,0:T(8,128)(2,1)S(1)} %constant_dynamic-slice_fusion), channel_id=1, source_target_pairs={{0,1},{1,0},{2,3},{3,2},{4,5},{5,4},{6,7},{7,6},{8,9},{9,8},{10,11... | collective-permute-start | bytes 663560 | tf_op jit(solution)/shard_map/ppermute | solution.py:107
  126.3 12.5 %collective-permute-start.11 = (bf16[2,144,768]{2,1,0:T(8,128)(2,1)}, bf16[2,144,768]{2,1,0:T(8,128)(2,1)}, u32[]{:S(2)}, u32[]{:S(2)}) collective-permute-start(bf16[2,144,768]{2,1,0:T(8,128)(2,1)} %pad_maximum_fusion.2), channel_id=1, source_target_pairs={{0,2},{2,0},{1,3},{3,1},{4,6},{6,4},{5,7},{7,5},{8,10},{10,8},{9,1... | collective-permute-start | bytes 1327112 | tf_op jit(solution)/shard_map/ppermute | solution.py:107
  131.2 11.3 %copy-start.13 = (f32[2,2432]{1,0:T(2,128)S(1)}, f32[2,2432]{1,0:T(2,128)}, u32[]{:S(2)}) copy-start(f32[2,2432]{1,0:T(2,128)} %get-tuple-element.39) | copy-start | bytes 58372
  138.8 3.6 %copy-start.3 = (bf16[2,144,2432]{2,1,0:T(8,128)(2,1)S(1)}, bf16[2,144,2432]{2,1,0:T(8,128)(2,1)}, u32[]{:S(2)}) copy-start(bf16[2,144,2432]{2,1,0:T(8,128)(2,1)} %param.10) | copy-start | bytes 4202500
  (8 other events, 14.3 us)
Sparse Core Ops, SparseCore 0:
  20.4 10.3 all-gather.2
  95.0 11.4 all-gather.4
